TPU v7x, 32 devices: a whole 2x2x4 slice. The times are simulated.
32 devices in a mesh: dp: 4 (over z), seq: 8 (over y, x, core).
Axes of the slice: x: 2, y: 2, z: 4, core: 2. Of those that a mesh axis runs over, the one named last changes fastest.
Arguments:
- inputs: bfloat16 [8, 1536, 1600], P('dp', 'seq'), may hold values from -6 to 6
- segments: int32 [8, 1536], P('dp'), may hold values from 0 to 7, as said below
- cotangent: bfloat16 [8, 1536, 1600], P('dp', 'seq'), may hold values from -6 to 6
- mix_weight: bfloat16 [1600, 4800], P('seq', 'dp'), may hold values from -0.15625 to 0.15625
- merge_weight: bfloat16 [1600, 1600], P('seq', 'dp'), may hold values from -1.25 to 1.25
- expand_weight: bfloat16 [1600, 6400], P('seq', 'dp'), may hold values from -0.15625 to 0.15625
- shrink_weight: bfloat16 [6400, 1600], P('seq', 'dp'), may hold values from -0.078125 to 0.078125
- first_gain: bfloat16 [1600], P('seq'), may hold values from 0.5 to 1.5
- first_bias: bfloat16 [1600], P('seq'), may hold values from -3 to 3
- query_bias: bfloat16 [1600], P('seq'), may hold values from -3 to 3
- value_bias: bfloat16 [1600], P('seq'), may hold values from -3 to 3
- merge_bias: bfloat16 [1600], P('seq'), may hold values from -3 to 3
- second_gain: bfloat16 [1600], P('seq'), may hold values from 0.5 to 1.5
- second_bias: bfloat16 [1600], P('seq'), may hold values from -3 to 3
- expand_bias: bfloat16 [6400], P('seq'), may hold values from -3 to 3
- shrink_bias: bfloat16 [1600], P('seq'), may hold values from -3 to 3
Outputs:
- block_out: bfloat16 [8, 1536, 1600], P('dp', 'seq')
- input_grad: float32 [8, 1536, 1600], P('dp', 'seq')
- grad_mix: float32 [1600, 4800], P('seq', 'dp')
- grad_merge: float32 [1600, 1600], P('seq', 'dp')
- grad_expand: float32 [1600, 6400], P('seq', 'dp')
- grad_shrink: float32 [6400, 1600], P('seq', 'dp')
- grad_first_gain: float32 [1600], P('seq')
- grad_first_bias: float32 [1600], P('seq')
- grad_query_bias: float32 [1600], P('seq')
- grad_value_bias: float32 [1600], P('seq')
- grad_merge_bias: float32 [1600], P('seq')
- grad_second_gain: float32 [1600], P('seq')
- grad_second_bias: float32 [1600], P('seq')
- grad_expand_bias: float32 [6400], P('seq')
- grad_shrink_bias: float32 [1600], P('seq')
Inputs may be any that keep to these rules, and one draw needn't show every extreme that they name: `segments`: document numbers of a packed sequence start at 0 and never fall; a packed sequence holds at most eight documents; among the 2 packed sequences of each dp index, one has a document that starts before position 192 and ends within the last 192 positions.
All inputs are finite; a program needn't handle non-finite values.
Results may differ from a plain program's by a relative error of at most 0.011.
Values may be sent and summed in bfloat16 or wider, within the bound.
No kernel may reach another device: no remote copies, remote signals or barrier semaphores. Data moves between devices by JAX's collectives and lax.ppermute only.
A program may use at most 384 MiB of HBM per device.

v0:
```python
import jax
import jax.numpy as jnp
from jax import lax
from jax.sharding import PartitionSpec as P

HEADS = 25


def layer_norm(v, gain, bias):
    center = v - jnp.mean(v, axis=-1, keepdims=True)
    spread = jnp.mean(center * center, axis=-1, keepdims=True)
    return center * lax.rsqrt(spread + 1e-05) * gain + bias


def gelu_tanh(v):
    return 0.5 * v * (1.0 + jnp.tanh(0.7978845608028654 * (v + 0.044715 * v * v * v)))


def contract_rows(left, right):
    return lax.dot_general(
        left, right, (((0,), (0,)), ((), ())), preferred_element_type=jnp.float32
    )


def contract_last(left, right):
    return lax.dot_general(
        left, right, (((1,), (1,)), ((), ())), preferred_element_type=jnp.float32
    )


def body(
    inputs,
    segments,
    cotangent,
    mix_weight,
    merge_weight,
    expand_weight,
    shrink_weight,
    first_gain,
    first_bias,
    query_bias,
    value_bias,
    merge_bias,
    second_gain,
    second_bias,
    expand_bias,
    shrink_bias,
):
    micro, rows, width = inputs.shape
    length = segments.shape[1]
    head_dim = width // HEADS
    scale = head_dim ** (-0.5)
    hidden_units = expand_weight.shape[1] * lax.axis_size("dp")

    def fetch():
        pieces = (
            lax.all_gather(mix_weight, "seq", axis=0, tiled=True),
            lax.all_gather(merge_weight, "seq", axis=0, tiled=True),
            lax.all_gather(expand_weight, "seq", axis=0, tiled=True),
            lax.all_gather(shrink_weight, "seq", axis=0, tiled=True),
            lax.all_gather(first_gain, "seq", axis=0, tiled=True),
            lax.all_gather(first_bias, "seq", axis=0, tiled=True),
            lax.all_gather(query_bias, "seq", axis=0, tiled=True),
            lax.all_gather(value_bias, "seq", axis=0, tiled=True),
            lax.all_gather(merge_bias, "seq", axis=0, tiled=True),
            lax.all_gather(second_gain, "seq", axis=0, tiled=True),
            lax.all_gather(second_bias, "seq", axis=0, tiled=True),
            lax.all_gather(expand_bias, "seq", axis=0, tiled=True),
            lax.all_gather(shrink_bias, "seq", axis=0, tiled=True),
        )
        matrices = (
            lax.all_gather(pieces[0], "dp", axis=1, tiled=True),
            lax.all_gather(pieces[1], "dp", axis=1, tiled=True),
            lax.all_gather(pieces[2], "dp", axis=1, tiled=True),
            lax.all_gather(pieces[3], "dp", axis=1, tiled=True),
        )
        vectors = tuple((piece.astype(jnp.float32) for piece in pieces[4:]))
        return (matrices, vectors)

    acc_mix = jnp.zeros((width, 3 * width), jnp.float32)
    acc_merge = jnp.zeros((width, width), jnp.float32)
    acc_expand = jnp.zeros((width, hidden_units), jnp.float32)
    acc_shrink = jnp.zeros((hidden_units, width), jnp.float32)
    acc_vectors = [jnp.zeros((width,), jnp.float32) for index_v in range(7)] + [
        jnp.zeros((hidden_units,), jnp.float32),
        jnp.zeros((width,), jnp.float32),
    ]
    base = lax.axis_index("seq") * rows
    query_pos = base + jnp.arange(rows, dtype=jnp.int32)
    key_pos = jnp.arange(length, dtype=jnp.int32)
    head_ids = jnp.arange(HEADS, dtype=jnp.int32)
    results = []
    input_grads = []
    for step in range(micro):
        matrices, vectors = fetch()
        mix, merge, expand, shrink = matrices
        gain_one, bias_one, q_bias, v_bias, m_bias, gain_two, bias_two, e_bias, s_bias = vectors
        x_row = inputs[step].astype(jnp.float32)
        first, first_pull = jax.vjp(layer_norm, x_row, gain_one, bias_one)
        first_low = first.astype(jnp.bfloat16)
        mixed = jnp.dot(first_low, mix, preferred_element_type=jnp.float32)
        query = (mixed[:, :width] + q_bias).astype(jnp.bfloat16)
        key = mixed[:, width : 2 * width].astype(jnp.bfloat16)
        value = (mixed[:, 2 * width :] + v_bias).astype(jnp.bfloat16)
        keys_all, values_all = (
            lax.all_gather(key, "seq", axis=0, tiled=True),
            lax.all_gather(value, "seq", axis=0, tiled=True),
        )
        seg_row = segments[step]
        seg_query = lax.dynamic_slice_in_dim(seg_row, base, rows, 0)
        visible = (seg_query[:, None] == seg_row[None, :]) & (
            key_pos[None, :] <= query_pos[:, None]
        )

        def head_forward(head):
            q_head = lax.dynamic_slice_in_dim(query, head * head_dim, head_dim, 1)
            k_head = lax.dynamic_slice_in_dim(keys_all, head * head_dim, head_dim, 1)
            v_head = lax.dynamic_slice_in_dim(values_all, head * head_dim, head_dim, 1)
            scores = contract_last(q_head, k_head) * scale
            scores = jnp.where(visible, scores, -1e30)
            top = jnp.max(scores, axis=-1, keepdims=True)
            expo = jnp.exp(scores - top)
            total = jnp.sum(expo, axis=-1, keepdims=True)
            probs = expo / total
            mixed_head = jnp.dot(
                probs.astype(jnp.bfloat16), v_head, preferred_element_type=jnp.float32
            )
            return (mixed_head, top[:, 0] + jnp.log(total[:, 0]))

        head_outs, log_totals = lax.map(head_forward, head_ids)
        attended = head_outs.transpose(1, 0, 2).reshape(rows, width).astype(jnp.bfloat16)
        hidden = x_row + jnp.dot(attended, merge, preferred_element_type=jnp.float32) + m_bias
        second, second_pull = jax.vjp(layer_norm, hidden, gain_two, bias_two)
        second_low = second.astype(jnp.bfloat16)
        pre = jnp.dot(second_low, expand, preferred_element_type=jnp.float32) + e_bias
        act, gelu_pull = jax.vjp(gelu_tanh, pre)
        act_low = act.astype(jnp.bfloat16)
        result = hidden + jnp.dot(act_low, shrink, preferred_element_type=jnp.float32) + s_bias
        results.append(result.astype(jnp.bfloat16))
        matrices, vectors = fetch()
        mix, merge, expand, shrink = matrices
        grad_out = cotangent[step]
        grad_out_f = grad_out.astype(jnp.float32)
        acc_shrink = acc_shrink + contract_rows(act_low, grad_out)
        acc_vectors[8] = acc_vectors[8] + jnp.sum(grad_out_f, axis=0)
        d_act = contract_last(grad_out, shrink)
        d_pre = gelu_pull(d_act)[0].astype(jnp.bfloat16)
        acc_expand = acc_expand + contract_rows(second_low, d_pre)
        acc_vectors[7] = acc_vectors[7] + jnp.sum(d_pre.astype(jnp.float32), axis=0)
        d_second = contract_last(d_pre, expand)
        d_norm_two, d_gain_two, d_bias_two = second_pull(d_second)
        acc_vectors[5] = acc_vectors[5] + d_gain_two
        acc_vectors[6] = acc_vectors[6] + d_bias_two
        d_hidden = grad_out_f + d_norm_two
        d_branch = d_hidden.astype(jnp.bfloat16)
        acc_merge = acc_merge + contract_rows(attended, d_branch)
        acc_vectors[4] = acc_vectors[4] + jnp.sum(d_branch.astype(jnp.float32), axis=0)
        d_attended = contract_last(d_branch, merge).astype(jnp.bfloat16)

        def head_backward(packed):
            head, log_total = packed
            q_head = lax.dynamic_slice_in_dim(query, head * head_dim, head_dim, 1)
            k_head = lax.dynamic_slice_in_dim(keys_all, head * head_dim, head_dim, 1)
            v_head = lax.dynamic_slice_in_dim(values_all, head * head_dim, head_dim, 1)
            g_head = lax.dynamic_slice_in_dim(d_attended, head * head_dim, head_dim, 1)
            scores = jnp.where(visible, contract_last(q_head, k_head) * scale, -1e30)
            probs = jnp.exp(scores - log_total[:, None])
            d_weights = contract_last(g_head, v_head)
            delta = jnp.sum(probs * d_weights, axis=-1, keepdims=True)
            d_scores = (probs * (d_weights - delta)).astype(jnp.bfloat16)
            d_q = jnp.dot(d_scores, k_head, preferred_element_type=jnp.float32) * scale
            d_k = contract_rows(d_scores, q_head) * scale
            d_v = contract_rows(probs.astype(jnp.bfloat16), g_head)
            return (d_q, d_k, d_v)

        dq_heads, dk_heads, dv_heads = lax.map(head_backward, (head_ids, log_totals))
        d_query = dq_heads.transpose(1, 0, 2).reshape(rows, width).astype(jnp.bfloat16)
        dk_whole = dk_heads.transpose(1, 0, 2).reshape(length, width)
        dv_whole = dv_heads.transpose(1, 0, 2).reshape(length, width)
        d_key, d_value = (
            lax.psum_scatter(dk_whole, "seq", scatter_dimension=0, tiled=True),
            lax.psum_scatter(dv_whole, "seq", scatter_dimension=0, tiled=True),
        )
        d_key = d_key.astype(jnp.bfloat16)
        d_value = d_value.astype(jnp.bfloat16)
        d_mixed = jnp.concatenate([d_query, d_key, d_value], axis=1)
        acc_mix = acc_mix + contract_rows(first_low, d_mixed)
        acc_vectors[2] = acc_vectors[2] + jnp.sum(d_query.astype(jnp.float32), axis=0)
        acc_vectors[3] = acc_vectors[3] + jnp.sum(d_value.astype(jnp.float32), axis=0)
        d_first = contract_last(d_mixed, mix)
        d_norm_one, d_gain_one, d_bias_one = first_pull(d_first)
        acc_vectors[0] = acc_vectors[0] + d_gain_one
        acc_vectors[1] = acc_vectors[1] + d_bias_one
        input_grads.append(d_hidden + d_norm_one)
    summed = lax.psum(
        (
            acc_vectors[0],
            acc_vectors[1],
            acc_vectors[2],
            acc_vectors[3],
            acc_vectors[4],
            acc_vectors[5],
            acc_vectors[6],
            acc_vectors[7],
            acc_vectors[8],
        ),
        "dp",
    )
    owned = (
        lax.psum_scatter(acc_mix, "dp", scatter_dimension=1, tiled=True),
        lax.psum_scatter(acc_merge, "dp", scatter_dimension=1, tiled=True),
        lax.psum_scatter(acc_expand, "dp", scatter_dimension=1, tiled=True),
        lax.psum_scatter(acc_shrink, "dp", scatter_dimension=1, tiled=True),
    )
    final = (
        lax.psum_scatter(owned[0], "seq", scatter_dimension=0, tiled=True),
        lax.psum_scatter(owned[1], "seq", scatter_dimension=0, tiled=True),
        lax.psum_scatter(owned[2], "seq", scatter_dimension=0, tiled=True),
        lax.psum_scatter(owned[3], "seq", scatter_dimension=0, tiled=True),
        lax.psum_scatter(summed[0], "seq", scatter_dimension=0, tiled=True),
        lax.psum_scatter(summed[1], "seq", scatter_dimension=0, tiled=True),
        lax.psum_scatter(summed[2], "seq", scatter_dimension=0, tiled=True),
        lax.psum_scatter(summed[3], "seq", scatter_dimension=0, tiled=True),
        lax.psum_scatter(summed[4], "seq", scatter_dimension=0, tiled=True),
        lax.psum_scatter(summed[5], "seq", scatter_dimension=0, tiled=True),
        lax.psum_scatter(summed[6], "seq", scatter_dimension=0, tiled=True),
        lax.psum_scatter(summed[7], "seq", scatter_dimension=0, tiled=True),
        lax.psum_scatter(summed[8], "seq", scatter_dimension=0, tiled=True),
    )
    return (
        jnp.stack(results),
        jnp.stack(input_grads),
        final[0],
        final[1],
        final[2],
        final[3],
        final[4],
        final[5],
        final[6],
        final[7],
        final[8],
        final[9],
        final[10],
        final[11],
        final[12],
    )


def solution(mesh):
    placed = (
        P("dp", "seq", None),
        P("dp", None),
        P("dp", "seq", None),
        P("seq", "dp"),
        P("seq", "dp"),
        P("seq", "dp"),
        P("seq", "dp"),
        P("seq"),
        P("seq"),
        P("seq"),
        P("seq"),
        P("seq"),
        P("seq"),
        P("seq"),
        P("seq"),
        P("seq"),
    )
    return jax.shard_map(
        body,
        mesh=mesh,
        in_specs=placed,
        out_specs=(
            P("dp", "seq", None),
            P("dp", "seq", None),
            P("seq", "dp"),
            P("seq", "dp"),
            P("seq", "dp"),
            P("seq", "dp"),
            P("seq"),
            P("seq"),
            P("seq"),
            P("seq"),
            P("seq"),
            P("seq"),
            P("seq"),
            P("seq"),
            P("seq"),
        ),
        check_vma=False,
    )
```

profile of v0, /device:TPU:0, one launch (start us, length us, event | category | flops | bytes accessed | tf_op | source)
XLA Modules:
  0.0 4640.0 jit_solution(6996000481569919356)
XLA Ops:
  8.0 41.0 all-gather.14.cloned.1.call-done
  62.0 25.3 all-reduce.22
  88.1 241.6 %all-gather.16.cloned.1.call-done = bf16[1600,4800]{0,1:T(8,128)(2,1)} async-done(((bf16[1600,1200]{0,1:T(8,128)(2,1)}), bf16[1600,4800]{0,1:T(8,128)(2,1)}) %all-gather.16.cloned.1.call-update) | async-done | bytes 15360016 | tf_op jit(solution)/shard_map/all_gather | solution.py:72
  367.9 31.0 all-gather.26.cloned.1.call-done
  409.2 34.6 all-gather.36.cloned.1.call-done
  460.8 26.0 all-gather.32.cloned.1.call-done
  486.8 43.1 all-gather.34.cloned.1.call-done
  529.9 121.4 %while.57 = (s32[]{:T(128)}, bf16[25,192,64]{1,2,0:T(8,128)(2,1)S(1)}, f32[25,192]{1,0:T(8,128)S(1)}, s32[25]{0:T(128)S(1)}, bf16[192,1600]{1,0:T(8,128)(2,1)S(1...) while((s32[]{:T(128)}, ...), condition=%wide.region_13.14_spmd.clone, body=%wide.region_10.13_spmd.clone.sunk | while | flops 78741312 | bytes 4459731 | solution.py:130
  657.7 15.1 all-gather.18.cloned.1.call-done
  672.8 42.9 all-gather.20.cloned.1.call-done
  715.9 122.5 %while.56 = (s32[]{:T(128)}, bf16[25,192,64]{1,2,0:T(8,128)(2,1)S(1)}, f32[25,192]{1,0:T(8,128)S(1)}, s32[25]{0:T(128)S(1)}, bf16[192,1600]{1,0:T(8,128)(2,1)}, ...) while((s32[]{:T(128)}, ...), condition=%wide.region_5.6_spmd.clone, body=%wide.region_2.5_spmd.clone.sunk | while | flops 78741312 | bytes 4457171 | solution.py:130
  843.7 235.9 %all-gather.28.cloned.1.call-done = bf16[1600,6400]{0,1:T(8,128)(2,1)} async-done(((bf16[1600,1600]{0,1:T(8,128)(2,1)}), bf16[1600,6400]{0,1:T(8,128)(2,1)}) %all-gather.28.cloned.1.call-update) | async-done | bytes 20480016 | tf_op jit(solution)/shard_map/all_gather | solution.py:74
  1105.9 322.5 %all-gather.30.cloned.1.call-done = bf16[6400,1600]{0,1:T(8,128)(2,1)} async-done(((bf16[6400,400]{0,1:T(8,128)(2,1)}), bf16[6400,1600]{0,1:T(8,128)(2,1)}) %all-gather.30.cloned.1.call-update) | async-done | bytes 20480016 | tf_op jit(solution)/shard_map/all_gather | solution.py:75
  1492.4 231.2 %while.59 = (s32[]{:T(128)}, bf16[25,192,64]{1,2,0:T(8,128)(2,1)S(1)}, f32[25,1536,64]{1,2,0:T(8,128)}, f32[25,1536,64]{1,2,0:T(8,128)}, s32[25]{0:T(128)S(1)}, ...) while((s32[]{:T(128)}, ...), condition=%wide.region_29.30_spmd.clone, body=%wide.region_27.29_spmd.clone.sunk | while | flops 192393024 | bytes 11089403 | solution.py:176
  1761.5 233.4 %while.58 = (s32[]{:T(128)}, bf16[25,192,64]{1,2,0:T(8,128)(2,1)S(1)}, f32[25,1536,64]{1,2,0:T(8,128)}, f32[25,1536,64]{1,2,0:T(8,128)}, s32[25]{0:T(128)S(1)}, ...) while((s32[]{:T(128)}, ...), condition=%wide.region_20.21_spmd.clone, body=%wide.region_18.20_spmd.clone.sunk | while | flops 192393024 | bytes 11089403 | solution.py:176
  2018.5 19.2 fusion.134
  2037.7 32.4 convolution_add_fusion
  2086.6 81.2 %reduce-scatter.37.cloned.1.call-done = f32[192,1600]{1,0:T(8,128)} async-done(((f32[1536,1600]{1,0:T(8,128)}), f32[192,1600]{1,0:T(8,128)}) %reduce-scatter.37.cloned.1.call-update) | async-done | bytes 1228816
  2170.4 15.4 fusion.125
  2185.8 26.9 convolution_add_fusion.2
  2214.1 17.5 fusion.160
  2231.6 31.5 convolution_add_fusion.1
  2263.1 46.3 copy.60
  2338.5 500.7 %reduce-scatter.35.cloned.1.call-done = f32[6400,400]{0,1:T(8,128)} async-done(((f32[6400,1600]{0,1:T(8,128)}), f32[6400,400]{0,1:T(8,128)}) %reduce-scatter.35.cloned.1.call-update) | async-done | bytes 10240016 | tf_op jit(solution)/shard_map/reduce_scatter | solution.py:213
  2851.8 172.9 %reduce-scatter.33.cloned.1.call-done = f32[1600,400]{0,1:T(8,128)} async-done(((f32[1600,1600]{0,1:T(8,128)}), f32[1600,400]{0,1:T(8,128)}) %reduce-scatter.33.cloned.1.call-update) | async-done | bytes 2560016 | tf_op jit(solution)/shard_map/reduce_scatter | solution.py:211
  3029.1 524.7 %reduce-scatter.53.cloned.1.call-done = f32[1600,1200]{0,1:T(8,128)} async-done(((f32[1600,4800]{0,1:T(8,128)}), f32[1600,1200]{0,1:T(8,128)}) %reduce-scatter.53.cloned.1.call-update) | async-done | bytes 7680016
  3563.8 692.0 %reduce-scatter.49.cloned.1.call-done = f32[1600,1600]{1,0:T(8,128)} async-done(((f32[6400,1600]{1,0:T(8,128)}), f32[1600,1600]{1,0:T(8,128)}) %reduce-scatter.49.cloned.1.call-update) | async-done | bytes 10240016
  4322.9 19.3 all-reduce.21
  4342.2 73.5 %reduce-scatter.51.cloned.1.call-done = f32[800,400]{1,0:T(8,128)} async-done(((f32[6400,400]{1,0:T(8,128)}), f32[800,400]{1,0:T(8,128)}) %reduce-scatter.51.cloned.1.call-update) | async-done | bytes 1280016
  4418.7 48.3 %reduce-scatter.47.cloned.1.call-done = f32[200,400]{1,0:T(8,128)} async-done(((f32[1600,400]{1,0:T(8,128)}), f32[200,400]{1,0:T(8,128)}) %reduce-scatter.47.cloned.1.call-update) | async-done | bytes 320016
  4467.0 74.9 %reduce-scatter.45.cloned.1.call-done = f32[200,1200]{1,0:T(8,128)} async-done(((f32[1600,1200]{1,0:T(8,128)}), f32[200,1200]{1,0:T(8,128)}) %reduce-scatter.45.cloned.1.call-update) | async-done | bytes 960016
  4541.8 91.2 %reduce-scatter.55.cloned.1.call-done = f32[200,1600]{1,0:T(8,128)} async-done(((f32[1600,1600]{1,0:T(8,128)}), f32[200,1600]{1,0:T(8,128)}) %reduce-scatter.55.cloned.1.call-update) | async-done | bytes 1280016
  (1063 shorter events, 1025.8 us)
Async XLA Ops:
  7.2 41.8 all-gather.14.cloned.1.call-start
  7.9 321.8 %all-gather.16.cloned.1.call-start = ((), (), s32[]{:S(2)}) async-start(), calls=%async_computation.13 | async-start | bytes 19968000 | tf_op jit(solution)/shard_map/all_gather | solution.py:72
  55.9 305.4 %all-gather.22.cloned.1.call-start = ((), (), s32[]{:S(2)}) async-start(), calls=%async_computation.16 | async-start | bytes 1843200 | tf_op jit(solution)/shard_map/all_gather | solution.py:58
  56.6 342.3 %all-gather.26.cloned.1.call-start = ((), (), s32[]{:S(2)}) async-start(), calls=%async_computation.18 | async-start | bytes 5990400 | tf_op jit(solution)/shard_map/all_gather | solution.py:59
  57.2 386.7 %all-gather.36.cloned.1.call-start = ((), (), s32[]{:S(2)}) async-start(), calls=%async_computation.25 | async-start | bytes 6451200 | tf_op jit(solution)/shard_map/all_gather | solution.py:60
  57.8 429.0 %all-gather.32.cloned.1.call-start = ((), (), s32[]{:S(2)}) async-start(), calls=%async_computation.21 | async-start | bytes 5750784 | tf_op jit(solution)/shard_map/all_gather | solution.py:106
  344.4 185.4 %all-gather.34.cloned.1.call-start = ((), (), s32[]{:S(2)}) async-start(), calls=%async_computation.22 | async-start | bytes 5750784 | tf_op jit(solution)/shard_map/all_gather | solution.py:107
  361.2 290.2 %all-gather.24.cloned.1.call-start = ((), (), s32[]{:S(2)}) async-start(), calls=%async_computation.17 | async-start | bytes 6656000 | tf_op jit(solution)/shard_map/all_gather | solution.py:73
  364.8 308.1 %all-gather.18.cloned.1.call-start = ((), (), s32[]{:S(2)}) async-start(), calls=%async_computation.14 | async-start | bytes 5750784 | tf_op jit(solution)/shard_map/all_gather | solution.py:106
  367.3 348.4 %all-gather.20.cloned.1.call-start = ((), (), s32[]{:S(2)}) async-start(), calls=%async_computation.15 | async-start | bytes 5750784 | tf_op jit(solution)/shard_map/all_gather | solution.py:107
  367.9 711.7 %all-gather.28.cloned.1.call-start = ((), (), s32[]{:S(2)}) async-start(), calls=%async_computation.19 | async-start | bytes 26624000 | tf_op jit(solution)/shard_map/all_gather | solution.py:74
  408.4 1020.0 %all-gather.30.cloned.1.call-start = ((), (), s32[]{:S(2)}) async-start(), calls=%async_computation.20 | async-start | bytes 25600000 | tf_op jit(solution)/shard_map/all_gather | solution.py:75
  408.4 683.5 %copy-start.35 = (f32[1600]{0:T(1024)}, f32[1600]{0:T(1024)S(1)}, u32[]{:S(2)}) copy-start(f32[1600]{0:T(1024)S(1)} %convert_element_type.222) | copy-start | bytes 19204
  408.5 1067.4 %copy-start.33 = (f32[1600]{0:T(1024)}, f32[1600]{0:T(1024)S(1)}, u32[]{:S(2)}) copy-start(f32[1600]{0:T(1024)S(1)} %convert_element_type.221) | copy-start | bytes 19204
  460.4 1619.5 %reduce-scatter.43.cloned.1.call-start = ((), (), s32[]{:S(2)}) async-start(), calls=%async_computation.29 | async-start | bytes 11501568
  656.4 819.5 %copy-start.43 = (f32[192]{0:T(256)}, f32[192]{0:T(256)S(1)}, u32[]{:S(2)}) copy-start(f32[192]{0:T(256)S(1)} %broadcast_multiply_fusion) | copy-start | bytes 2308
  843.3 632.6 %copy-start.2 = (f32[192,1600]{1,0:T(8,128)}, f32[192,1600]{1,0:T(8,128)S(1)}, u32[]{:S(2)}) copy-start(f32[192,1600]{1,0:T(8,128)S(1)} %get-tuple-element.584) | copy-start | bytes 3686404
  843.3 632.6 %copy-start.41 = (f32[192]{0:T(256)}, f32[192]{0:T(256)S(1)}, u32[]{:S(2)}) copy-start(f32[192]{0:T(256)S(1)} %broadcast_multiply_fusion.2) | copy-start | bytes 2308
  843.6 632.3 %copy-start.57 = (f32[192]{0:T(256)}, f32[192]{0:T(256)S(1)}, u32[]{:S(2)}) copy-start(f32[192]{0:T(256)S(1)} %fusion.147) | copy-start | bytes 2308
  843.7 632.3 %copy-start.45 = (f32[192]{0:T(256)}, f32[192]{0:T(256)S(1)}, u32[]{:S(2)}) copy-start(f32[192]{0:T(256)S(1)} %fusion.145) | copy-start | bytes 2308
  1734.6 347.9 %reduce-scatter.41.cloned.1.call-start = ((), (), s32[]{:S(2)}) async-start(), calls=%async_computation.28 | async-start | bytes 11501568
  1745.6 339.4 %reduce-scatter.39.cloned.1.call-start = ((), (), s32[]{:S(2)}) async-start(), calls=%async_computation.27 | async-start | bytes 11501568
  2005.6 162.2 %reduce-scatter.37.cloned.1.call-start = ((), (), s32[]{:S(2)}) async-start(), calls=%async_computation.26 | async-start | bytes 11501568
  2017.0 822.2 %reduce-scatter.35.cloned.1.call-start = ((), (), s32[]{:S(2)}) async-start(), calls=%async_computation.24 | async-start | bytes 51200000 | tf_op jit(solution)/shard_map/reduce_scatter | solution.py:213
  2070.2 954.5 %reduce-scatter.33.cloned.1.call-start = ((), (), s32[]{:S(2)}) async-start(), calls=%async_computation.23 | async-start | bytes 13312000 | tf_op jit(solution)/shard_map/reduce_scatter | solution.py:211
  2079.8 1474.1 %reduce-scatter.53.cloned.1.call-start = ((), (), s32[]{:S(2)}) async-start(), calls=%async_computation.34 | async-start | bytes 39936000
  2212.8 2043.0 %reduce-scatter.49.cloned.1.call-start = ((), (), s32[]{:S(2)}) async-start(), calls=%async_computation.32 | async-start | bytes 53248000
  2309.4 2006.6 %all-reduce.25.cloned.1.call-start = ((), (), s32[]{:S(2)}) async-start(), calls=%async_computation.36 | async-start | bytes 188416
  2338.5 2077.2 %reduce-scatter.51.cloned.1.call-start = ((), (), s32[]{:S(2)}) async-start(), calls=%async_computation.33 | async-start | bytes 14745600
  2851.8 1615.2 %reduce-scatter.47.cloned.1.call-start = ((), (), s32[]{:S(2)}) async-start(), calls=%async_computation.31 | async-start | bytes 3686400
  3029.1 1512.8 %reduce-scatter.45.cloned.1.call-start = ((), (), s32[]{:S(2)}) async-start(), calls=%async_computation.30 | async-start | bytes 9216000
  3563.5 1069.5 %reduce-scatter.55.cloned.1.call-start = ((), (), s32[]{:S(2)}) async-start(), calls=%async_computation.35 | async-start | bytes 11980800
  (80 other events, 3218.6 us)
Sparse Core Ops, SparseCore 0:
  9.9 38.9 all-gather.13
  55.9 273.7 all-gather.15
  331.6 24.0 all-gather.21
  357.4 41.4 all-gather.25
  400.6 43.1 all-gather.35
  446.2 40.5 all-gather.31
  489.2 40.5 all-gather.33
  532.0 99.4 all-gather.23
  633.9 38.9 all-gather.17
  675.1 40.5 all-gather.19
  717.3 362.1 all-gather.27
  1081.0 347.3 all-gather.29
  1734.7 78.7 reduce-scatter.42
  1817.4 80.1 reduce-scatter.40
  2005.7 77.9 reduce-scatter.38
  2087.7 80.0 reduce-scatter.36
  2170.0 669.1 reduce-scatter.34
  2841.5 183.1 reduce-scatter.32
  3027.2 526.6 reduce-scatter.52
  3556.1 699.6 reduce-scatter.48
  4260.1 55.8 all-reduce.24
  4320.0 95.6 reduce-scatter.50
  4420.0 46.8 reduce-scatter.46
  4471.5 70.2 reduce-scatter.44
  4546.0 87.0 reduce-scatter.54
where the time goes:
time: 4660 us; the launch traced here: 4640 us
  waiting for transfers between devices  3310 us (71%)
  matrix products  864 us (19%)
  local copies, waits for them, and re-layouts  286 us (6%)
  loops' own time  69.4 us (1%)
    unnamed x36, waiting for transfers between devices  1600 us
    reduce_scatter x1, waiting for transfers between devices, body(): lax.psum_scatter(acc_shrink, 'dp', scatter_dimension=1, tiled=True)  501 us
    all_gather x1, waiting for transfers between devices, fetch(): lax.all_gather(pieces[3], 'dp', axis=1, tiled=True)  322 us
    dot_general x158, matrix products, contract_last(): lax.dot_general(left, right, (((1,), (1,)), ((), ())), preferred_element_...  320 us
    dot_general x108, matrix products, contract_rows(): lax.dot_general(left, right, (((0,), (0,)), ((), ())), preferred_element_...  302 us
    all_gather x1, waiting for transfers between devices, fetch(): lax.all_gather(pieces[0], 'dp', axis=1, tiled=True)  242 us
    all_gather x1, waiting for transfers between devices, fetch(): lax.all_gather(pieces[2], 'dp', axis=1, tiled=True)  236 us
    reduce_scatter x1, waiting for transfers between devices, body(): lax.psum_scatter(acc_merge, 'dp', scatter_dimension=1, tiled=True)  173 us
  transfers between devices with their start and end apart: 25, of which 20 were waited for; matrix products, arithmetic and copies ran while one was open for 19% of the time, Pallas kernels for 0%

commit v1 on v0

v1 whole, which is shorter than its diff:
```python
import functools

import jax
import jax.numpy as jnp
from jax import lax
from jax.experimental import pallas as pl
from jax.experimental.pallas import tpu as pltpu
from jax.sharding import PartitionSpec as P

HEADS = 25
LANES = 128
LOW = jnp.bfloat16
FULL = jnp.float32
VMEM_BYTES = 50 * 1024 * 1024


def layer_norm(v, gain, bias):
    center = v - jnp.mean(v, axis=-1, keepdims=True)
    spread = jnp.mean(center * center, axis=-1, keepdims=True)
    return center * lax.rsqrt(spread + 1e-05) * gain + bias


def gelu_tanh(v):
    return 0.5 * v * (1.0 + jnp.tanh(0.7978845608028654 * (v + 0.044715 * v * v * v)))


def dot_nn(left, right):
    return lax.dot_general(left, right, (((1,), (0,)), ((), ())), preferred_element_type=FULL)


def dot_tn(left, right):
    return lax.dot_general(left, right, (((0,), (0,)), ((), ())), preferred_element_type=FULL)


def dot_nt(left, right):
    return lax.dot_general(left, right, (((1,), (1,)), ((), ())), preferred_element_type=FULL)


def softmax_pieces(query, keys, seg_col, seg_row, index, block):
    scores = []
    for j in range(index + 1):
        piece = dot_nt(query, keys[j])
        seen = seg_col == seg_row[:, j * block : (j + 1) * block]
        if j == index:
            row_id = lax.broadcasted_iota(jnp.int32, (block, block), 0)
            col_id = lax.broadcasted_iota(jnp.int32, (block, block), 1)
            seen = seen & (col_id <= row_id)
        scores.append(jnp.where(seen, piece, -1e30))
    top = functools.reduce(jnp.maximum, [jnp.max(p, axis=1, keepdims=True) for p in scores])
    expo = [jnp.exp(p - top) for p in scores]
    total = functools.reduce(jnp.add, [jnp.sum(p, axis=1, keepdims=True) for p in expo])
    return expo, total


def attend_forward_kernel(count, block, dim, heads, *refs):
    q_refs, k_refs, v_refs = refs[:count], refs[count : 2 * count], refs[2 * count : 3 * count]
    col_ref, row_ref, out_ref = refs[3 * count :]
    pair = pl.program_id(0)
    out_ref[...] = jnp.zeros_like(out_ref)
    for sub in range(LANES // dim):

        @pl.when(pair * (LANES // dim) + sub < heads)
        def _():
            lanes = slice(sub * dim, (sub + 1) * dim)
            keys = [r[:, lanes] for r in k_refs]
            values = [r[:, lanes] for r in v_refs]
            for i in range(count):
                rows = slice(i * block, (i + 1) * block)
                query = q_refs[i][:, lanes]
                expo, total = softmax_pieces(
                    query, keys, col_ref[rows, :], row_ref[...], i, block
                )
                mixed = functools.reduce(
                    jnp.add, [dot_nn(e.astype(LOW), v) for e, v in zip(expo, values)]
                )
                out_ref[rows, lanes] = (mixed / total).astype(LOW)


def attend_backward_kernel(count, block, dim, heads, *refs):
    q_refs, k_refs, v_refs = refs[:count], refs[count : 2 * count], refs[2 * count : 3 * count]
    g_ref, col_ref, row_ref, dq_ref, dk_ref, dv_ref, acc_k, acc_v = refs[3 * count :]
    pair = pl.program_id(0)
    scale = dim**-0.5
    dq_ref[...] = jnp.zeros_like(dq_ref)
    dk_ref[...] = jnp.zeros_like(dk_ref)
    dv_ref[...] = jnp.zeros_like(dv_ref)
    for sub in range(LANES // dim):

        @pl.when(pair * (LANES // dim) + sub < heads)
        def _():
            lanes = slice(sub * dim, (sub + 1) * dim)
            keys = [r[:, lanes] for r in k_refs]
            values = [r[:, lanes] for r in v_refs]
            acc_k[...] = jnp.zeros_like(acc_k)
            acc_v[...] = jnp.zeros_like(acc_v)
            for i in range(count):
                rows = slice(i * block, (i + 1) * block)
                query = q_refs[i][:, lanes]
                grad = g_ref[rows, lanes]
                expo, total = softmax_pieces(
                    query, keys, col_ref[rows, :], row_ref[...], i, block
                )
                inverse = 1.0 / total
                probs = [e * inverse for e in expo]
                d_weights = [dot_nt(grad, v) for v in values[: i + 1]]
                delta = functools.reduce(
                    jnp.add,
                    [jnp.sum(p * d, axis=1, keepdims=True) for p, d in zip(probs, d_weights)],
                )
                d_query = jnp.zeros((block, dim), FULL)
                for j in range(i + 1):
                    cols = slice(j * block, (j + 1) * block)
                    d_scores = (probs[j] * (d_weights[j] - delta)).astype(LOW)
                    d_query = d_query + dot_nn(d_scores, keys[j])
                    acc_k[cols, :] += dot_tn(d_scores, query)
                    acc_v[cols, :] += dot_tn(probs[j].astype(LOW), grad)
                dq_ref[rows, lanes] = (d_query * scale).astype(LOW)
            dk_ref[:, lanes] = acc_k[...].astype(LOW)
            dv_ref[:, lanes] = acc_v[...].astype(LOW)


def attend_specs(count, block, span):
    per = span // LANES
    specs = []
    for part in range(3):
        for j in range(count):
            specs.append(
                pl.BlockSpec(
                    (block, LANES), lambda p, j=j, part=part: (j, part * per + p)
                )
            )
    return specs


def attend_forward(mixed, seg, count, dim, heads):
    length, wide = mixed.shape
    span = wide // 3
    block = length // count
    whole = lambda shape: pl.BlockSpec(shape, lambda p: (0, 0))
    return pl.pallas_call(
        functools.partial(attend_forward_kernel, count, block, dim, heads),
        grid=(span // LANES,),
        in_specs=attend_specs(count, block, span) + [whole((length, 1)), whole((1, length))],
        out_specs=pl.BlockSpec((length, LANES), lambda p: (0, p)),
        out_shape=jax.ShapeDtypeStruct((length, span), LOW),
        compiler_params=pltpu.CompilerParams(vmem_limit_bytes=VMEM_BYTES),
        cost_estimate=pl.CostEstimate(
            flops=2 * length * length * dim * heads * 2,
            bytes_accessed=4 * length * span * 2,
            transcendentals=length * length * heads // 2,
        ),
        name="attend_forward",
    )(*([mixed] * (3 * count)), seg.reshape(length, 1), seg.reshape(1, length))


def attend_backward(mixed, grad, seg, count, dim, heads):
    length, wide = mixed.shape
    span = wide // 3
    block = length // count
    whole = lambda shape: pl.BlockSpec(shape, lambda p: (0, 0))
    column = pl.BlockSpec((length, LANES), lambda p: (0, p))
    shape = jax.ShapeDtypeStruct((length, span), LOW)
    return pl.pallas_call(
        functools.partial(attend_backward_kernel, count, block, dim, heads),
        grid=(span // LANES,),
        in_specs=attend_specs(count, block, span)
        + [column, whole((length, 1)), whole((1, length))],
        out_specs=[column, column, column],
        out_shape=[shape, shape, shape],
        scratch_shapes=[pltpu.VMEM((length, dim), FULL), pltpu.VMEM((length, dim), FULL)],
        compiler_params=pltpu.CompilerParams(vmem_limit_bytes=VMEM_BYTES),
        cost_estimate=pl.CostEstimate(
            flops=5 * length * length * dim * heads * 2,
            bytes_accessed=8 * length * span * 2,
            transcendentals=length * length * heads // 2,
        ),
        name="attend_backward",
    )(*([mixed] * (3 * count)), grad, seg.reshape(length, 1), seg.reshape(1, length))


def body(
    seq_n,
    dp_n,
    inputs,
    segments,
    cotangent,
    mix_weight,
    merge_weight,
    expand_weight,
    shrink_weight,
    first_gain,
    first_bias,
    query_bias,
    value_bias,
    merge_bias,
    second_gain,
    second_bias,
    expand_bias,
    shrink_bias,
):
    micro, rows, width = inputs.shape
    length = segments.shape[1]
    dim = width // HEADS
    teams = seq_n // 2
    bits = teams.bit_length() - 1
    own_rows = 2 * rows
    feats = width // seq_n
    share = width // teams
    starts_exact = [share * t // dim for t in range(teams)]
    heads = max(-(-share * (t + 1) // dim) - starts_exact[t] for t in range(teams))
    starts = [dim * min(h, HEADS - heads) for h in starts_exact]
    window = heads * dim
    span = -(-window // LANES) * LANES
    hidden_units = expand_weight.shape[1] * dp_n
    per_team = hidden_units // dp_n // teams
    half_team = per_team // 2

    place = lax.axis_index("seq")
    core = place % 2
    team = place // 2

    def hop(v, mask):
        return lax.ppermute(v, "seq", [(i, i ^ mask) for i in range(seq_n)])

    def pick(v, index):
        return lax.dynamic_index_in_dim(v, index, 0, keepdims=False)

    def reorder(v):
        return jnp.stack([pick(v, team ^ j) for j in range(teams)])

    def by_core(mine, other):
        return jnp.where(core == 0, jnp.stack([mine, other]), jnp.stack([other, mine]))

    def part_rows(total):
        edges = [total * p // bits for p in range(bits + 1)]
        return list(zip(edges[:-1], edges[1:]))

    def gather_team(v):
        done = []
        for p, (low, high) in enumerate(part_rows(v.shape[0])):
            cur = v[low:high][None]
            order = [(p + i) % bits for i in range(bits)]
            for b in order:
                cur = jnp.concatenate([cur, hop(cur, 2 << b)], axis=0)
            cur = cur.reshape((2,) * bits + cur.shape[1:])
            axes = [bits - 1 - order.index(bits - 1 - a) for a in range(bits)]
            cur = cur.transpose(axes + list(range(bits, cur.ndim)))
            done.append(cur.reshape((teams,) + cur.shape[bits:]))
        return jnp.concatenate(done, axis=1)

    def reduce_team(v):
        done = []
        for p, (low, high) in enumerate(part_rows(v.shape[1])):
            cur = v[:, low:high]
            cur = cur.reshape((2,) * bits + cur.shape[1:])
            left = list(range(bits - 1, -1, -1))
            order = [(p + i) % bits for i in range(bits)]
            for b in reversed(order):
                axis = left.index(b)
                keep = lax.index_in_dim(cur, 0, axis, keepdims=False)
                give = lax.index_in_dim(cur, 1, axis, keepdims=False)
                left.remove(b)
                cur = keep.astype(FULL) + hop(give, 2 << b).astype(FULL)
                if left:
                    cur = cur.astype(LOW)
            done.append(cur)
        return jnp.concatenate(done, axis=0)

    def exchange_team(v):
        return jnp.stack([v[0]] + [hop(v[k], 2 * k) for k in range(1, teams)])

    def swap_in(v):
        got = hop(pick(v, 1 - core), 1)
        return by_core(pick(v, core), got).reshape(own_rows, width)

    def swap_out(v):
        v = v.reshape(2, rows, width)
        got = hop(pick(v, 1 - core), 1)
        return by_core(pick(v, core), got)

    def gather_small(v):
        cur = v[None]
        for b in range(bits + 1):
            got = hop(cur, 1 << b)
            bit = (place >> b) & 1
            cur = jnp.where(
                bit == 0, jnp.concatenate([cur, got]), jnp.concatenate([got, cur])
            )
        return cur

    def reduce_small(v):
        for b in reversed(range(bits + 1)):
            half = v.shape[0] // 2
            bit = (place >> b) & 1
            mine = jnp.where(bit == 0, v[:half], v[half:])
            give = jnp.where(bit == 0, v[half:], v[:half])
            v = mine + hop(give, 1 << b)
        v = v[0]
        for b in range(dp_n.bit_length() - 1):
            v = v + lax.ppermute(v, "dp", [(i, i ^ (1 << b)) for i in range(dp_n)])
        return v

    small = (
        first_gain,
        first_bias,
        query_bias,
        value_bias,
        merge_bias,
        second_gain,
        second_bias,
        expand_bias,
        shrink_bias,
    )
    sizes = [v.shape[0] for v in small]
    offsets = [sum(sizes[:i]) for i in range(len(sizes) + 1)]

    x_own_low = swap_in(inputs)
    x_own = x_own_low.astype(FULL)
    packed = gather_small(jnp.concatenate(small))
    gain_one, bias_one, q_bias, v_bias, m_bias, gain_two, bias_two, e_bias, s_bias = [
        packed[:, offsets[i] : offsets[i + 1]].reshape(-1).astype(FULL) for i in range(9)
    ]
    start = jnp.asarray(starts, jnp.int32)[team]

    mix_rows = lax.all_gather(mix_weight, "dp", axis=0)
    mix_rows = mix_rows.transpose(1, 0, 2).reshape(feats, 3, width)
    mix_cuts = jnp.stack(
        [mix_rows[:, :, s : s + window].reshape(feats, 3 * window) for s in starts]
    )
    mix_got = exchange_team(reorder(mix_cuts))
    mix_other = hop(mix_got, 1)
    mix_mine = reorder(mix_got)
    mix_other = reorder(mix_other)
    mix = by_core(mix_mine, mix_other).transpose(1, 0, 2, 3)
    mix = mix.reshape(width, 3, window)
    mix = jnp.pad(mix, ((0, 0), (0, 0), (0, span - window))).reshape(width, 3 * span)

    merge_rows = lax.all_gather(merge_weight, "dp", axis=0)
    merge_rows = merge_rows.transpose(1, 0, 2).reshape(feats, width)
    merge_got = gather_team(merge_rows)
    merge_other = reorder(hop(merge_got, 1))
    merge = by_core(reorder(merge_got), merge_other).transpose(1, 0, 2, 3)
    merge = merge.reshape(width, width)

    cut = expand_weight.reshape(feats, teams, 2, half_team).transpose(2, 1, 3, 0)
    cut = by_core(pick(cut, core), hop(pick(cut, 1 - core), 1))
    cut = cut.transpose(1, 2, 0, 3).reshape(teams, half_team, 2 * feats)
    cut = reorder(exchange_team(reorder(cut))).transpose(1, 0, 2).reshape(half_team, width)
    expand_mine = lax.all_gather(cut, "dp", axis=0, tiled=True)
    expand_other = hop(expand_mine, 1)

    cut = shrink_weight.reshape(teams // 2, 2, half_team, -1).transpose(1, 0, 2, 3)
    cut = by_core(pick(cut, core), hop(pick(cut, 1 - core), 1))
    cut = cut.reshape((teams, half_team) + cut.shape[3:])
    cut = reorder(exchange_team(reorder(cut))).transpose(2, 0, 1).reshape(-1, teams * half_team)
    shrink_mine = lax.all_gather(cut, "dp", axis=0, tiled=True)
    shrink_other = hop(shrink_mine, 1)

    x_all = reorder(gather_team(x_own_low)).reshape(length, width)
    first = layer_norm(x_all.astype(FULL), gain_one, bias_one).astype(LOW)

    def windowed(v):
        return jnp.pad(lax.dynamic_slice_in_dim(v, start, window, 0), (0, span - window))

    mix_bias = jnp.concatenate([windowed(q_bias), jnp.zeros((span,), FULL), windowed(v_bias)])
    mixed = (dot_nn(first, mix) + mix_bias).astype(LOW)
    shrinking = jnp.where(jnp.arange(3 * span) < span, dim**-0.5, 1.0).astype(LOW)
    mixed = mixed * shrinking
    seg = pick(segments, core)
    attended_win = attend_forward(mixed, seg, teams, dim, heads)
    pieces = reorder(exchange_team(reorder(attended_win.reshape(teams, own_rows, span))))
    attended = jnp.concatenate(
        [
            pieces[t][:, share * t - starts[t] : share * (t + 1) - starts[t]]
            for t in range(teams)
        ],
        axis=1,
    )
    hidden = x_own + dot_nn(attended, merge) + m_bias
    second_own, second_pull = jax.vjp(layer_norm, hidden, gain_two, bias_two)
    second = gather_team(second_own.astype(LOW)).reshape(length, width)

    g_own_low = swap_in(cotangent)
    g_own = g_own_low.astype(FULL)
    g_all = gather_team(g_own_low).reshape(length, width)

    e_cut = e_bias.reshape(dp_n, teams, 2, half_team).transpose(1, 2, 0, 3)
    e_cut = pick(e_cut, team).reshape(2, dp_n * half_team)
    e_mine, e_other = pick(e_cut, core), pick(e_cut, 1 - core)

    def feed(expand_t, shrink_t, bias):
        pre = dot_nt(second, expand_t) + bias
        act, pull = jax.vjp(gelu_tanh, pre)
        act = act.astype(LOW)
        d_act = dot_nn(g_all, shrink_t)
        d_pre = pull(d_act)[0].astype(LOW)
        return act, d_pre

    act_mine, d_pre_mine = feed(expand_mine, shrink_mine, e_mine)
    act_other, d_pre_other = feed(expand_other, shrink_other, e_other)
    d_second = dot_nn(d_pre_mine, expand_mine) + dot_nn(d_pre_other, expand_other)
    d_second = reduce_team(d_second.astype(LOW).reshape(teams, own_rows, width))
    out = dot_nt(act_mine, shrink_mine) + dot_nt(act_other, shrink_other)
    out = reduce_team(out.astype(LOW).reshape(teams, own_rows, width))
    block_out = swap_out((hidden + out + s_bias).astype(LOW))

    def core_sum(mine, other):
        return (mine + hop(other.astype(LOW), 1).astype(FULL)).astype(LOW)

    g_shrink = core_sum(dot_tn(g_all, act_mine), dot_tn(g_all, act_other))
    g_shrink = lax.psum_scatter(g_shrink, "dp", scatter_dimension=0, tiled=True)
    g_expand = core_sum(dot_tn(d_pre_mine, second), dot_tn(d_pre_other, second))
    g_expand = lax.psum_scatter(g_expand, "dp", scatter_dimension=0, tiled=True)

    cut = g_shrink.reshape(-1, teams, half_team).transpose(1, 2, 0)
    cut = reorder(exchange_team(reorder(cut)))
    cut = cut.reshape((2, teams // 2) + cut.shape[1:])
    cut = by_core(pick(cut, core), hop(pick(cut, 1 - core), 1))
    grad_shrink = cut.transpose(1, 0, 2, 3).reshape(shrink_weight.shape).astype(FULL)

    cut = g_expand.reshape(half_team, teams, 2 * feats).transpose(1, 0, 2)
    cut = reorder(exchange_team(reorder(cut)))
    cut = cut.reshape(teams, half_team, 2, feats).transpose(2, 3, 0, 1)
    cut = by_core(pick(cut, core), hop(pick(cut, 1 - core), 1))
    grad_expand = cut.transpose(1, 2, 0, 3).reshape(expand_weight.shape).astype(FULL)

    d_norm_two, d_gain_two, d_bias_two = second_pull(d_second)
    d_hidden = g_own + d_norm_two
    d_branch = d_hidden.astype(LOW)
    d_attended = dot_nt(d_branch, merge).astype(LOW)
    pieces = jnp.stack(
        [
            jnp.pad(d_attended[:, s : s + window], ((0, 0), (0, span - window)))
            for s in starts
        ]
    )
    d_attended_win = reorder(exchange_team(reorder(pieces))).reshape(length, span)
    d_parts = attend_backward(mixed, d_attended_win, seg, teams, dim, heads)

    column = jnp.arange(span, dtype=jnp.int32) + start
    owned = (column >= share * team) & (column < share * (team + 1))
    d_parts = [jnp.where(owned, d, jnp.zeros((), LOW)) for d in d_parts]
    d_first = functools.reduce(
        jnp.add,
        [dot_nt(d_parts[m], mix[:, m * span : (m + 1) * span]) for m in range(3)],
    )
    d_first = reduce_team(reorder(d_first.astype(LOW).reshape(teams, own_rows, width)))

    def core_halves(v):
        v = v.reshape((teams, 2, feats) + v.shape[1:]).transpose((1, 0, 2, 3))
        return core_sum(pick(v, core), pick(v, 1 - core))

    g_merge = core_halves(dot_tn(attended, d_branch))
    g_merge = g_merge.reshape(teams, feats, dp_n, -1).transpose(2, 0, 1, 3)
    g_merge = lax.psum_scatter(g_merge, "dp", scatter_dimension=0, tiled=True)[0]
    grad_merge = reduce_team(reorder(g_merge))

    g_mix = jnp.concatenate([dot_tn(first, d)[:, :window] for d in d_parts], axis=1)
    g_mix = reorder(exchange_team(reorder(core_halves(g_mix))))
    g_mix = g_mix.reshape(teams, feats, 3, window)
    g_mix = jnp.concatenate(
        [
            g_mix[t, :, :, share * t - starts[t] : share * (t + 1) - starts[t]]
            for t in range(teams)
        ],
        axis=-1,
    )
    g_mix = g_mix.reshape(feats, dp_n, -1).transpose(1, 0, 2)
    grad_mix = lax.psum_scatter(g_mix, "dp", scatter_dimension=0, tiled=True)[0].astype(FULL)

    x_again, first_pull = jax.vjp(layer_norm, x_own, gain_one, bias_one)
    d_norm_one, d_gain_one, d_bias_one = first_pull(d_first)
    input_grad = swap_out(d_hidden + d_norm_one)

    def spread(v):
        return lax.dynamic_update_slice_in_dim(
            jnp.zeros((width + span,), FULL), v, start, 0
        )[:width]

    d_e = jnp.stack([jnp.sum(d.astype(FULL), axis=0) for d in (d_pre_mine, d_pre_other)])
    d_e = jnp.where(core == 0, d_e, d_e[::-1]).reshape(2, dp_n, half_team).transpose(1, 0, 2)
    d_e = lax.dynamic_update_slice_in_dim(
        jnp.zeros((dp_n, teams, 2, half_team), FULL), d_e[:, None], team, 1
    )
    partial = (
        d_gain_one,
        d_bias_one,
        spread(jnp.sum(d_parts[0].astype(FULL), axis=0)),
        spread(jnp.sum(d_parts[2].astype(FULL), axis=0)),
        jnp.sum(d_branch.astype(FULL), axis=0),
        d_gain_two,
        d_bias_two,
        d_e.reshape(-1),
        jnp.sum(g_own, axis=0),
    )
    total = reduce_small(
        jnp.concatenate([v.reshape(seq_n, -1) for v in partial], axis=1)
    )
    vectors = [total[offsets[i] : offsets[i + 1]] for i in range(9)]
    return (block_out, input_grad, grad_mix, grad_merge, grad_expand, grad_shrink, *vectors)


def solution(mesh):
    rows = P("dp", "seq", None)
    matrix = P("seq", "dp")
    vector = P("seq")
    return jax.shard_map(
        functools.partial(body, mesh.shape["seq"], mesh.shape["dp"]),
        mesh=mesh,
        in_specs=(rows, P("dp", None), rows) + (matrix,) * 4 + (vector,) * 9,
        out_specs=(rows, rows) + (matrix,) * 4 + (vector,) * 9,
        check_vma=False,
    )
```

time: 4660 us -> 1110 us (0.24)
  waiting for transfers between devices: 3310 us -> 189 us
  matrix products: 864 us -> 177 us
  other arithmetic: 45 us -> 163 us
  Pallas kernels: 0 us -> 82.5 us
  local copies, waits for them, and re-layouts: 286 us -> 364 us
  starting transfers between devices: 2.68 us -> 75.1 us
  loops' own time: 69.4 us -> 0 us
    unnamed x36 -> x8, waiting for transfers between devices: 1600 us -> 0.78 us
    all_gather x12 -> x3, waiting for transfers between devices: 1030 us -> 0.02 us  [the longest x1 0.02 us: body(): expand_mine = lax.all_gather(cut, 'dp', axis=0, tiled=True)]
    dot_general x374 -> x22, matrix products: 864 us -> 177 us  [the longest x8 61.5 us: dot_tn(): lax.dot_general(left, right, (((0,), (0,)), ((), ())), preferred_element_...]
    reduce_scatter x2 -> x3, waiting for transfers between devices: 674 us -> 5.74 us  [the longest x1 5.73 us: body(): lax.psum_scatter(g_mix, 'dp', scatter_dimension=0, tiled=True)[0]]
    ppermute x0 -> x80, waiting for transfers between devices: none -> 183 us  [the longest x78 182 us: hop(): return lax.ppermute(v, 'seq', [(i, i ^ mask) for i in range(seq_n)])]
    unnamed x217 -> x286, local copies, waits for them, and re-layouts: 170 us -> 49.6 us
    pallas_call x0 -> x2, Pallas kernels: none -> 82.5 us  [the longest x1 51.9 us: attend_backward(): pl.pallas_call(functools.partial(attend_backward_kernel, count, block, di...]
    ppermute x0 -> x80, starting transfers between devices: none -> 74.2 us  [the longest x78 69.2 us: hop(): return lax.ppermute(v, 'seq', [(i, i ^ mask) for i in range(seq_n)])]
  transfers between devices with their start and end apart: 25 -> 87, of which waited for: 20 -> 34; matrix products, arithmetic and copies ran while one was open for 19% -> 58% of each run, Pallas kernels for 0% -> 7%
where the time goes in v1:
time: 1110 us; the launch traced here: 1100 us
  local copies, waits for them, and re-layouts  364 us (33%)
  waiting for transfers between devices  189 us (17%)
  matrix products  177 us (16%)
  other arithmetic  163 us (15%)
  Pallas kernels  82.5 us (7%)
  starting transfers between devices  75.1 us (7%)
  blocking collectives  33 us (3%)
  between operations  16.8 us (2%)
    ppermute x78, waiting for transfers between devices, hop(): return lax.ppermute(v, 'seq', [(i, i ^ mask) for i in range(seq_n)])  182 us
    ppermute x78, starting transfers between devices, hop(): return lax.ppermute(v, 'seq', [(i, i ^ mask) for i in range(seq_n)])  69.2 us
    dot_general x8, matrix products, dot_tn(): lax.dot_general(left, right, (((0,), (0,)), ((), ())), preferred_element_...  61.5 us
    dot_general x8, matrix products, dot_nt(): lax.dot_general(left, right, (((1,), (1,)), ((), ())), preferred_element_...  60.3 us
    dot_general x6, matrix products, dot_nn(): lax.dot_general(left, right, (((1,), (0,)), ((), ())), preferred_element_...  55.4 us
    pallas_call x1, Pallas kernels, attend_backward(): pl.pallas_call(functools.partial(attend_backward_kernel, count, block, di...  51.9 us
    unnamed x286, local copies, waits for them, and re-layouts  49.6 us
    ppermute x20, local copies, waits for them, and re-layouts, hop(): return lax.ppermute(v, 'seq', [(i, i ^ mask) for i in range(seq_n)])  44.8 us
  transfers between devices with their start and end apart: 87, of which 34 were waited for; matrix products, arithmetic and copies ran while one was open for 58% of the time, Pallas kernels for 7%

profile of v1, /device:TPU:0, one launch (start us, length us, event | category | flops | bytes accessed | tf_op | source)
XLA Modules:
  0.0 1100.8 jit_solution(3416661191373693442)
XLA Ops:
  15.6 33.0 %all-gather.1 = bf16[800,400]{1,0:T(8,128)(2,1)S(1)} all-gather(bf16[200,400]{1,0:T(8,128)(2,1)S(1)} %copy-done.83), channel_id=3, replica_groups=mesh['dp'=4,'seq'=8] {'dp'}, dimensions={0}, use_global_device_ids=true | all-gather | bytes 800000 | tf_op jit(solution)/shard_map/all_gather | solution.py:338
  117.2 17.9 %collective-permute-done.3 = bf16[1,192,1600]{2,1,0:T(8,128)(2,1)S(1)} collective-permute-done((bf16[1,192,1600]{2,1,0:T(8,128)(2,1)S(1)}, bf16[1,192,1600]{2,1,0:T(8,128)(2,1)S(1)}, u32[]{:S(2)}, u32[]{:S(2)}) %collective-permute-start.3) | collective-permute-done | bytes 614432 | tf_op jit(solution)/shard_map/ppermute | solution.py:223
  153.7 13.9 %collective-permute-done.4 = bf16[2,192,1600]{2,1,0:T(8,128)(2,1)} collective-permute-done((bf16[2,192,1600]{2,1,0:T(8,128)(2,1)}, bf16[2,192,1600]{2,1,0:T(8,128)(2,1)}, u32[]{:S(2)}, u32[]{:S(2)}) %collective-permute-start.4) | collective-permute-done | bytes 1228832 | tf_op jit(solution)/shard_map/ppermute | solution.py:223
  198.1 8.5 collective-permute-done.8
  209.9 8.9 collective-permute-done.9
  259.4 30.2 %copy.469 = bf16[4,2,200,1344]{2,1,0,3:T(2,128)(2,1)} copy(bf16[4,2,200,1344]{2,3,0,1:T(8,128)(2,1)S(1)} %fusion.5) | data formatting | bytes 8601600 | tf_op jit(solution)/shard_map/transpose | solution.py:334
  289.6 14.7 %reshape.687 = bf16[1600,3,448]{0,2,1:T(8,128)(2,1)} reshape(bf16[4,2,200,1344]{2,1,0,3:T(2,128)(2,1)} %copy.469) | data formatting | bytes 8601600 | tf_op jit(solution)/shard_map/reshape | solution.py:335
  309.3 12.1 %fusion.4.refs_0_.refs_1_.refs_2_.refs_3_.refs_4_.refs_5_.refs_6_.refs_7_.refs_8_.refs_9_.refs_10_.refs_11_ = bf16[1536,1536]{1,0:T(8,128)(2,1)} fusion(bf16[1536,1600]{1,0:T(8,128)(2,1)} %bitcast.450, bf16[1600,1536]{0,1:T(8,128)(2,1)S(1)} %bitcast.421, f32[1536]{0:T(1024)S(1)} %copy-done.99, bf16[1536]{0:T(1024)(128)(2,1)S(1)} %copy-done.103), kind=kOutput, calls=%fused_computation.21 | convolution fusion | flops 7556825088 | bytes 14558208 | tf_op jit(solution)/shard_map/dot_general | solution.py:28
  321.5 30.6 %attend_forward.1 = bf16[1536,512]{1,0:T(8,128)(2,1)S(1)} custom-call(bf16[1536,1536]{1,0:T(8,128)(2,1)} %fusion.4.refs_0_.refs_1_.refs_2_.refs_3_.refs_4_.refs_5_.refs_6_.refs_7_.refs_8_.refs_9_.refs_10_.refs_11_, bf16[1536,1536]{1,0:T(8,128)(2,1)} %fusion.4.refs_0_.refs_1_.refs_2_.refs_3_.refs_4_.refs_5_.refs_6_.refs_7_.refs_8_.refs_9_.refs_10_.refs_11_, ...), custom_call_target="tpu_custom_call" | custom-call | flops 4227858432 | bytes 6291456 | tf_op jit(solution)/shard_map/attend_forward/pallas_call | solution.py:140
  365.2 7.6 collective-permute-done.13
  425.8 8.7 fusion.3
  451.4 12.0 %collective-permute-done.23 = bf16[2,192,1600]{2,1,0:T(8,128)(2,1)} collective-permute-done((bf16[2,192,1600]{2,1,0:T(8,128)(2,1)}, bf16[2,192,1600]{2,1,0:T(8,128)(2,1)}, u32[]{:S(2)}, u32[]{:S(2)}) %collective-permute-start.23) | collective-permute-done | bytes 1228832 | tf_op jit(solution)/shard_map/ppermute | solution.py:223
  476.4 9.9 fusion.79
  492.1 11.2 %add_convert_fusion.3 = bf16[1536,1600]{0,1:T(8,128)(2,1)} fusion(f32[1536,1600]{0,1:T(8,128)S(1)} %fusion.61, bf16[1600,800]{0,1:T(8,128)(2,1)} %collective-permute-done.33, f32[1536,800]{0,1:T(8,128)} %fusion.79, f32[800]{0:T(1024)S(1)} %copy-done.102), kind=kOutput, calls=%fused_computation.9 | convolution fusion | flops 3949363200 | bytes 22224000 | tf_op jit(solution)/shard_map/dot_general | solution.py:36
  516.1 10.1 convolution_convert_fusion
  526.2 9.7 convert_reduce_fusion.1
  542.3 10.3 convert_reduce_fusion.2
  556.9 7.5 fusion.80
  564.4 9.5 add_convert_fusion.2
  612.6 12.8 %collective-permute-done.46 = bf16[2,192,1600]{2,1,0:T(8,128)(2,1)} collective-permute-done((bf16[2,192,1600]{2,1,0:T(8,128)(2,1)}, bf16[2,192,1600]{2,1,0:T(8,128)(2,1)}, u32[]{:S(2)}, u32[]{:S(2)}) %collective-permute-start.46) | collective-permute-done | bytes 1228832 | tf_op jit(solution)/shard_map/ppermute | solution.py:223
  644.8 9.1 collective-permute-done.47
  708.4 51.9 %attend_backward.1 = (bf16[1536,512]{1,0:T(8,128)(2,1)S(1)}, bf16[1536,512]{1,0:T(8,128)(2,1)S(1)}, bf16[1536,512]{1,0:T(8,128)(2,1)}) custom-call(bf16[1536,1536]{1,0:T(8,128)(2,1)} %fusion.4.refs_0_.refs_1_.refs_2_.refs_3_.refs_4_.refs_5_.refs_6_.refs_7_.refs_8_.refs_9_.refs_10_.refs_11_, ...), custom_call_target="tpu_custom_call" | custom-call | flops 10569646080 | bytes 12582912 | tf_op jit(solution)/shard_map/attend_backward/pallas_call | solution.py:163
  762.9 8.0 fusion.33
  782.9 12.3 %add_convert_fusion.5 = bf16[1600,800]{1,0:T(8,128)(2,1)} fusion(bf16[1600,800]{1,0:T(8,128)(2,1)} %copy.552, bf16[1536,1600]{1,0:T(8,128)(2,1)} %bitcast.444, f32[1536,800]{0,1:T(8,128)} %copy-done.116, f32[800]{0:T(1024)S(1)} %copy-done.101), kind=kOutput, calls=%fused_computation.22 | convolution fusion | flops 3948288000 | bytes 14953600 | tf_op jit(solution)/shard_map/dot_general | solution.py:32
  795.3 10.9 add_convert_fusion.1
  806.2 7.5 copy.527
  878.5 11.9 %collective-permute-done.53 = bf16[2,192,1600]{2,1,0:T(8,128)(2,1)} collective-permute-done((bf16[2,192,1600]{2,1,0:T(8,128)(2,1)}, bf16[2,192,1600]{2,1,0:T(8,128)(2,1)}, u32[]{:S(2)}, u32[]{:S(2)}) %collective-permute-start.53) | collective-permute-done | bytes 1228832 | tf_op jit(solution)/shard_map/ppermute | solution.py:223
  897.9 7.7 pad_maximum_fusion
  905.6 10.2 copy.543
  944.0 10.3 reshape.719
  972.8 13.0 %collective-permute-done.59 = bf16[200,1344]{1,0:T(8,128)(2,1)S(1)} collective-permute-done((bf16[200,1344]{1,0:T(8,128)(2,1)S(1)}, bf16[200,1344]{1,0:T(8,128)(2,1)S(1)}, u32[]{:S(2)}, u32[]{:S(2)}) %collective-permute-start.59) | collective-permute-done | bytes 537632 | tf_op jit(solution)/shard_map/ppermute | solution.py:223
  985.8 10.1 collective-permute-done.58
  (780 shorter events, 641.7 us)
Async XLA Ops:
  7.2 168.4 %all-gather.10.cloned.1.call-start = ((), (), s32[]{:S(2)}) async-start(), calls=%async_computation.9 | async-start | bytes 2560000 | tf_op jit(solution)/shard_map/all_gather | solution.py:325
  7.9 426.6 %all-gather.6.cloned.1.call-start = ((), (), s32[]{:S(2)}) async-start(), calls=%async_computation.4 | async-start | bytes 3328000 | tf_op jit(solution)/shard_map/all_gather | solution.py:349
  14.7 34.3 %collective-permute-start.24 = (bf16[4,200,200]{2,1,0:T(8,128)(2,1)S(1)}, bf16[4,200,200]{2,1,0:T(8,128)(2,1)S(1)}, u32[]{:S(2)}, u32[]{:S(2)}) collective-permute-start(bf16[4,200,200]{2,1,0:T(8,128)(2,1)S(1)} %bitcast.479), channel_id=1, source_target_pairs={{0,1},{1,0},{2,3},{3,2},{4,5},{5,4},{6,7},{7,6},{8,9},{9,8},{10,11... | collective-permute-start | bytes 960008 | tf_op jit(solution)/shard_map/ppermute | solution.py:223
  15.4 64.3 %collective-permute-start.5 = (bf16[1,2400]{1,0:T(2,128)(2,1)S(1)}, bf16[1,2400]{1,0:T(2,128)(2,1)S(1)}, u32[]{:S(2)}, u32[]{:S(2)}) collective-permute-start(bf16[1,2400]{1,0:T(2,128)(2,1)S(1)} %broadcast_in_dim.81), channel_id=1, source_target_pairs={{0,1},{1,0},{2,3},{3,2},{4,5},{5,4},{6,7},{7,6},{8,9},{9,8},{10,11... | collective-permute-start | bytes 14408 | tf_op jit(solution)/shard_map/ppermute | solution.py:223
  61.4 35.3 %collective-permute-start.17 = (bf16[1,100,1600]{2,1,0:T(8,128)(2,1)S(1)}, bf16[1,100,1600]{2,1,0:T(8,128)(2,1)S(1)}, u32[]{:S(2)}, u32[]{:S(2)}) collective-permute-start(bf16[1,100,1600]{2,1,0:T(8,128)(2,1)S(1)} %broadcast_in_dim.86), channel_id=1, source_target_pairs={{0,4},{1,5},{2,6},{3,7},{4,0},{5,1},{6,2},{7,3},{8,12},{9,13},{10,... | collective-permute-start | bytes 960008 | tf_op jit(solution)/shard_map/ppermute | solution.py:223
  75.1 372.0 %all-gather.8.cloned.1.call-start = ((), (), s32[]{:S(2)}) async-start(), calls=%async_computation.5 | async-start | bytes 3584000 | tf_op jit(solution)/shard_map/all_gather | solution.py:356
  103.5 42.7 %collective-permute-start.16 = (bf16[2,100,1600]{2,0,1:T(2,128)(2,1)}, bf16[2,100,1600]{2,0,1:T(2,128)(2,1)}, u32[]{:S(2)}, u32[]{:S(2)}) collective-permute-start(bf16[2,100,1600]{2,0,1:T(2,128)(2,1)} %copy.472), channel_id=1, source_target_pairs={{0,4},{1,5},{2,6},{3,7},{4,0},{5,1},{6,2},{7,3},{8,12},{9,13},{10,... | collective-permute-start | bytes 1920008 | tf_op jit(solution)/shard_map/ppermute | solution.py:223
  107.5 35.6 %collective-permute-start.18 = (bf16[2,100,1600]{2,0,1:T(2,128)(2,1)}, bf16[2,100,1600]{2,0,1:T(2,128)(2,1)}, u32[]{:S(2)}, u32[]{:S(2)}) collective-permute-start(bf16[2,100,1600]{2,0,1:T(2,128)(2,1)} %copy.474), channel_id=1, source_target_pairs={{0,2},{1,3},{2,0},{3,1},{4,6},{5,7},{6,4},{7,5},{8,10},{9,11},{10,... | collective-permute-start | bytes 1920008 | tf_op jit(solution)/shard_map/ppermute | solution.py:223
  109.7 912.0 %reduce-scatter.11.cloned.1.call-start = ((), (), s32[]{:S(2)}) async-start(), calls=%async_computation.8 | async-start | bytes 3584000 | tf_op jit(solution)/shard_map/reduce_scatter | solution.py:411
  140.4 258.8 %collective-permute-start.40 = (bf16[1,192,1600]{2,1,0:T(8,128)(2,1)}, bf16[1,192,1600]{2,1,0:T(8,128)(2,1)}, u32[]{:S(2)}, u32[]{:S(2)}) collective-permute-start(bf16[1,192,1600]{2,1,0:T(8,128)(2,1)} %get-tuple-element.212), channel_id=1, source_target_pairs={{0,2},{1,3},{2,0},{3,1},{4,6},{5,7},{6,4},{7,5},{8,10},{9,11},{10,... | collective-permute-start | bytes 1843208 | tf_op jit(solution)/shard_map/ppermute | solution.py:223
  150.4 88.7 %collective-permute-start.19 = (bf16[4,200,1600]{2,1,0:T(8,128)(2,1)}, bf16[4,200,1600]{2,1,0:T(8,128)(2,1)}, u32[]{:S(2)}, u32[]{:S(2)}) collective-permute-start(bf16[4,200,1600]{2,1,0:T(8,128)(2,1)} %pad_maximum_fusion.10), channel_id=1, source_target_pairs={{0,1},{1,0},{2,3},{3,2},{4,5},{5,4},{6,7},{7,6},{8,9},{9,8},{10,11... | collective-permute-start | bytes 7680008 | tf_op jit(solution)/shard_map/ppermute | solution.py:223
  206.6 195.7 %collective-permute-start.42 = (bf16[1,192,1600]{2,1,0:T(8,128)(2,1)}, bf16[1,192,1600]{2,1,0:T(8,128)(2,1)}, u32[]{:S(2)}, u32[]{:S(2)}) collective-permute-start(bf16[1,192,1600]{2,1,0:T(8,128)(2,1)} %get-tuple-element.213), channel_id=1, source_target_pairs={{0,4},{1,5},{2,6},{3,7},{4,0},{5,1},{6,2},{7,3},{8,12},{9,13},{10,... | collective-permute-start | bytes 1843208 | tf_op jit(solution)/shard_map/ppermute | solution.py:223
  401.7 41.1 %collective-permute-start.41 = (bf16[2,192,1600]{2,1,0:T(8,128)(2,1)}, bf16[2,192,1600]{2,1,0:T(8,128)(2,1)}, u32[]{:S(2)}, u32[]{:S(2)}) collective-permute-start(bf16[2,192,1600]{2,1,0:T(8,128)(2,1)} %pad_maximum_fusion.30), channel_id=1, source_target_pairs={{0,4},{1,5},{2,6},{3,7},{4,0},{5,1},{6,2},{7,3},{8,12},{9,13},{10,... | collective-permute-start | bytes 3686408 | tf_op jit(solution)/shard_map/ppermute | solution.py:223
  423.3 40.0 %collective-permute-start.23 = (bf16[2,192,1600]{2,1,0:T(8,128)(2,1)}, bf16[2,192,1600]{2,1,0:T(8,128)(2,1)}, u32[]{:S(2)}, u32[]{:S(2)}) collective-permute-start(bf16[2,192,1600]{2,1,0:T(8,128)(2,1)} %copy.485), channel_id=1, source_target_pairs={{0,2},{1,3},{2,0},{3,1},{4,6},{5,7},{6,4},{7,5},{8,10},{9,11},{10,... | collective-permute-start | bytes 3686408 | tf_op jit(solution)/shard_map/ppermute | solution.py:223
  425.0 43.7 %collective-permute-start.21 = (bf16[2,192,1600]{2,1,0:T(8,128)(2,1)}, bf16[2,192,1600]{2,1,0:T(8,128)(2,1)}, u32[]{:S(2)}, u32[]{:S(2)}) collective-permute-start(bf16[2,192,1600]{2,1,0:T(8,128)(2,1)} %copy.481), channel_id=1, source_target_pairs={{0,4},{1,5},{2,6},{3,7},{4,0},{5,1},{6,2},{7,3},{8,12},{9,13},{10,... | collective-permute-start | bytes 3686408 | tf_op jit(solution)/shard_map/ppermute | solution.py:223
  434.6 41.8 %collective-permute-start.32 = (bf16[800,1600]{1,0:T(8,128)(2,1)}, bf16[800,1600]{1,0:T(8,128)(2,1)}, u32[]{:S(2)}, u32[]{:S(2)}) collective-permute-start(bf16[800,1600]{1,0:T(8,128)(2,1)} %all-gather.6.cloned.1.call-done), channel_id=1, source_target_pairs={{0,1},{1,0},{2,3},{3,2},{4,5},{5,4},{6,7},{7,6},{8,9},{9,8},{10,11... | collective-permute-start | bytes 7680008 | tf_op jit(solution)/shard_map/ppermute | solution.py:223
  451.3 40.8 %collective-permute-start.33 = (bf16[1600,800]{0,1:T(8,128)(2,1)S(1)}, bf16[1600,800]{0,1:T(8,128)(2,1)}, u32[]{:S(2)}, u32[]{:S(2)}) collective-permute-start(bf16[1600,800]{0,1:T(8,128)(2,1)S(1)} %copy.503), channel_id=1, source_target_pairs={{0,1},{1,0},{2,3},{3,2},{4,5},{5,4},{6,7},{7,6},{8,9},{9,8},{10,11... | collective-permute-start | bytes 7680008 | tf_op jit(solution)/shard_map/ppermute | solution.py:223
  541.8 235.8 %collective-permute-start.70 = (bf16[1600,800]{0,1:T(8,128)(2,1)}, bf16[1600,800]{0,1:T(8,128)(2,1)}, u32[]{:S(2)}, u32[]{:S(2)}) collective-permute-start(bf16[1600,800]{0,1:T(8,128)(2,1)} %convolution_convert_fusion), channel_id=1, source_target_pairs={{0,1},{1,0},{2,3},{3,2},{4,5},{5,4},{6,7},{7,6},{8,9},{9,8},{10,11... | collective-permute-start | bytes 7680008 | tf_op jit(solution)/shard_map/ppermute | solution.py:223
  541.8 318.9 %collective-permute-start.65 = (bf16[800,1600]{1,0:T(8,128)(2,1)}, bf16[800,1600]{1,0:T(8,128)(2,1)}, u32[]{:S(2)}, u32[]{:S(2)}) collective-permute-start(bf16[800,1600]{1,0:T(8,128)(2,1)} %convolution_convert_fusion.1), channel_id=1, source_target_pairs={{0,1},{1,0},{2,3},{3,2},{4,5},{5,4},{6,7},{7,6},{8,9},{9,8},{10,11... | collective-permute-start | bytes 7680008 | tf_op jit(solution)/shard_map/ppermute | solution.py:223
  554.7 42.4 %collective-permute-start.36 = (bf16[2,192,1600]{2,1,0:T(8,128)(2,1)}, bf16[2,192,1600]{2,1,0:T(8,128)(2,1)}, u32[]{:S(2)}, u32[]{:S(2)}) collective-permute-start(bf16[2,192,1600]{2,1,0:T(8,128)(2,1)} %get-tuple-element.170), channel_id=1, source_target_pairs={{0,2},{1,3},{2,0},{3,1},{4,6},{5,7},{6,4},{7,5},{8,10},{9,11},{10,... | collective-permute-start | bytes 3686408 | tf_op jit(solution)/shard_map/ppermute | solution.py:223
  556.4 47.1 %collective-permute-start.34 = (bf16[2,192,1600]{2,1,0:T(8,128)(2,1)}, bf16[2,192,1600]{2,1,0:T(8,128)(2,1)}, u32[]{:S(2)}, u32[]{:S(2)}) collective-permute-start(bf16[2,192,1600]{2,1,0:T(8,128)(2,1)} %get-tuple-element.140), channel_id=1, source_target_pairs={{0,4},{1,5},{2,6},{3,7},{4,0},{5,1},{6,2},{7,3},{8,12},{9,13},{10,... | collective-permute-start | bytes 3686408 | tf_op jit(solution)/shard_map/ppermute | solution.py:223
  597.0 37.0 %collective-permute-start.44 = (bf16[2,192,1600]{2,1,0:T(8,128)(2,1)}, bf16[2,192,1600]{2,1,0:T(8,128)(2,1)}, u32[]{:S(2)}, u32[]{:S(2)}) collective-permute-start(bf16[2,192,1600]{2,1,0:T(8,128)(2,1)} %get-tuple-element.138), channel_id=1, source_target_pairs={{0,4},{1,5},{2,6},{3,7},{4,0},{5,1},{6,2},{7,3},{8,12},{9,13},{10,... | collective-permute-start | bytes 3686408 | tf_op jit(solution)/shard_map/ppermute | solution.py:223
  603.5 38.6 %collective-permute-start.37 = (bf16[192,1600]{1,0:T(8,128)(2,1)}, bf16[192,1600]{1,0:T(8,128)(2,1)}, u32[]{:S(2)}, u32[]{:S(2)}) collective-permute-start(bf16[192,1600]{1,0:T(8,128)(2,1)} %copy.511), channel_id=1, source_target_pairs={{0,4},{1,5},{2,6},{3,7},{4,0},{5,1},{6,2},{7,3},{8,12},{9,13},{10,... | collective-permute-start | bytes 1843208 | tf_op jit(solution)/shard_map/ppermute | solution.py:223
  625.3 34.4 %collective-permute-start.35 = (bf16[192,1600]{1,0:T(8,128)(2,1)}, bf16[192,1600]{1,0:T(8,128)(2,1)}, u32[]{:S(2)}, u32[]{:S(2)}) collective-permute-start(bf16[192,1600]{1,0:T(8,128)(2,1)} %copy.507), channel_id=1, source_target_pairs={{0,2},{1,3},{2,0},{3,1},{4,6},{5,7},{6,4},{7,5},{8,10},{9,11},{10,... | collective-permute-start | bytes 1843208 | tf_op jit(solution)/shard_map/ppermute | solution.py:223
  699.2 221.3 %collective-permute-start.38 = (bf16[192,1600]{1,0:T(8,128)(2,1)}, bf16[192,1600]{1,0:T(8,128)(2,1)}, u32[]{:S(2)}, u32[]{:S(2)}) collective-permute-start(bf16[192,1600]{1,0:T(8,128)(2,1)} %get-tuple-element.217), channel_id=1, source_target_pairs={{0,1},{1,0},{2,3},{3,2},{4,5},{5,4},{6,7},{7,6},{8,9},{9,8},{10,11... | collective-permute-start | bytes 1843208 | tf_op jit(solution)/shard_map/ppermute | solution.py:223
  704.8 233.8 %collective-permute-start.60 = (bf16[4,200,1600]{2,1,0:T(8,128)(2,1)}, bf16[4,200,1600]{2,1,0:T(8,128)(2,1)}, u32[]{:S(2)}, u32[]{:S(2)}) collective-permute-start(bf16[4,200,1600]{2,1,0:T(8,128)(2,1)} %fusion.25), channel_id=1, source_target_pairs={{0,1},{1,0},{2,3},{3,2},{4,5},{5,4},{6,7},{7,6},{8,9},{9,8},{10,11... | collective-permute-start | bytes 7680008 | tf_op jit(solution)/shard_map/ppermute | solution.py:223
  795.2 232.9 %reduce-scatter.13.cloned.1.call-start = ((), (), s32[]{:S(2)}) async-start(), calls=%async_computation.10 | async-start | bytes 3328000
  831.2 36.7 %collective-permute-start.51 = (bf16[2,192,1600]{2,1,0:T(8,128)(2,1)}, bf16[2,192,1600]{2,1,0:T(8,128)(2,1)}, u32[]{:S(2)}, u32[]{:S(2)}) collective-permute-start(bf16[2,192,1600]{2,1,0:T(8,128)(2,1)} %copy.532), channel_id=1, source_target_pairs={{0,4},{1,5},{2,6},{3,7},{4,0},{5,1},{6,2},{7,3},{8,12},{9,13},{10,... | collective-permute-start | bytes 3686408 | tf_op jit(solution)/shard_map/ppermute | solution.py:223
  867.9 201.2 %reduce-scatter.9.cloned.1.call-start = ((), (), s32[]{:S(2)}) async-start(), calls=%async_computation.7 | async-start | bytes 4096000 | tf_op jit(solution)/shard_map/reduce_scatter | solution.py:455
  877.5 45.7 %collective-permute-start.52 = (bf16[192,1600]{1,0:T(8,128)(2,1)}, bf16[192,1600]{1,0:T(8,128)(2,1)}, u32[]{:S(2)}, u32[]{:S(2)}) collective-permute-start(bf16[192,1600]{1,0:T(8,128)(2,1)} %copy.534), channel_id=1, source_target_pairs={{0,2},{1,3},{2,0},{3,1},{4,6},{5,7},{6,4},{7,5},{8,10},{9,11},{10,... | collective-permute-start | bytes 1843208 | tf_op jit(solution)/shard_map/ppermute | solution.py:223
  920.4 45.1 %collective-permute-start.56 = (bf16[4,200,1344]{2,1,0:T(8,128)(2,1)}, bf16[4,200,1344]{2,1,0:T(8,128)(2,1)}, u32[]{:S(2)}, u32[]{:S(2)}) collective-permute-start(bf16[4,200,1344]{2,1,0:T(8,128)(2,1)} %fusion.31), channel_id=1, source_target_pairs={{0,1},{1,0},{2,3},{3,2},{4,5},{5,4},{6,7},{7,6},{8,9},{9,8},{10,11... | collective-permute-start | bytes 6451208 | tf_op jit(solution)/shard_map/ppermute | solution.py:223
  961.5 116.0 %reduce-scatter.7.cloned.1.call-start = ((), (), s32[]{:S(2)}) async-start(), calls=%async_computation.6 | async-start | bytes 3072000 | tf_op jit(solution)/shard_map/reduce_scatter | solution.py:469
  (188 other events, 2796.7 us)
Sparse Core Ops, SparseCore 0:
  9.6 59.7 all-gather.9
  75.3 56.0 all-gather.5
  133.0 57.6 all-gather.7
  795.3 57.0 reduce-scatter.10
  868.0 53.4 reduce-scatter.12
  961.6 63.7 reduce-scatter.8
  1027.7 49.7 reduce-scatter.6

commit v2 on v1

v2 whole, which is shorter than its diff:
```python
import functools

import jax
import jax.numpy as jnp
from jax import lax
from jax.experimental import pallas as pl
from jax.experimental.pallas import tpu as pltpu
from jax.sharding import PartitionSpec as P

HEADS = 25
COST = 0.25
LANES = 128
CHUNK = 256
LOW = jnp.bfloat16
FULL = jnp.float32
VMEM_BYTES = 60 * 1024 * 1024


def dot_nn(left, right):
    return lax.dot_general(left, right, (((1,), (0,)), ((), ())), preferred_element_type=FULL)


def dot_tn(left, right):
    return lax.dot_general(left, right, (((0,), (0,)), ((), ())), preferred_element_type=FULL)


def dot_nt(left, right):
    return lax.dot_general(left, right, (((1,), (1,)), ((), ())), preferred_element_type=FULL)


def norm_parts(v):
    center = v - jnp.mean(v, axis=-1, keepdims=True)
    spread = jnp.mean(center * center, axis=-1, keepdims=True)
    inverse = lax.rsqrt(spread + 1e-05)
    return center * inverse, inverse


def norm_back(grad, gain, normal, inverse):
    e = grad * gain
    mean_e = jnp.mean(e, axis=-1, keepdims=True)
    mean_en = jnp.mean(e * normal, axis=-1, keepdims=True)
    return inverse * (e - mean_e - normal * mean_en)


def total_rows(v):
    return jnp.sum(v, axis=0, keepdims=True)


def fixed(shape):
    return pl.BlockSpec(shape, lambda *_: (0,) * len(shape), pipeline_mode=pl.Buffered(1))


def call(
    kernel, name, grid, at, operands, in_specs, outs, out_specs, scratch, flops, nbytes, exps=0, after=()
):
    if after:
        count, inner = len(operands), kernel
        kernel = lambda at_ref, *refs: inner(at_ref, *refs[:count], *refs[count + len(after) :])
        operands = (*operands, *after)
        in_specs = list(in_specs) + [pl.BlockSpec(memory_space=pl.ANY)] * len(after)
    spec = pltpu.PrefetchScalarGridSpec(
        num_scalar_prefetch=1,
        grid=grid,
        in_specs=in_specs,
        out_specs=out_specs,
        scratch_shapes=scratch,
    )
    return pl.pallas_call(
        kernel,
        grid_spec=spec,
        out_shape=[jax.ShapeDtypeStruct(s, d) for s, d in outs],
        compiler_params=pltpu.CompilerParams(vmem_limit_bytes=VMEM_BYTES),
        cost_estimate=pl.CostEstimate(
            flops=int(COST * flops),
            bytes_accessed=int(COST * nbytes),
            transcendentals=int(COST * exps),
        ),
        name=name,
    )(at, *operands)


def row_slot(half, core, rows):
    slot = core if half == 0 else 1 - core
    return pl.ds(pl.multiple_of(slot * rows, rows), rows)


def load_pair(step, sizes, refs, buf, core, rows):
    low = 0
    for size, ref in zip(sizes, refs):
        for i in range(size // rows):
            r = low // rows + i

            @pl.when(step == r // 2)
            def _():
                buf[row_slot(r % 2, core, rows), :] = ref[i * rows : (i + 1) * rows, :]

        low += size


def pair_rows(refs, core, rows, buf):
    for half in range(2):
        here = slice(half * rows, (half + 1) * rows)
        value = functools.reduce(jnp.add, [ref[here, :].astype(FULL) for ref in refs])
        buf[row_slot(half, core, rows), :] = value.astype(buf.dtype)


def fold_kernel(at_ref, x_ref, y_ref, far0_ref, far1_ref, xo_ref, yo_ref):
    rows = far0_ref.shape[0]
    xo_ref[:rows, :] = x_ref[:rows, :]
    xo_ref[rows:, :] = (x_ref[rows:, :].astype(FULL) + far1_ref[...].astype(FULL)).astype(LOW)
    yo_ref[:rows, :] = (y_ref[:rows, :].astype(FULL) + far0_ref[...].astype(FULL)).astype(LOW)
    yo_ref[rows:, :] = y_ref[rows:, :]


def place_rows(place, refs, wide, out):
    each = refs[0].shape[0]
    if len(refs) == 1:
        out[...] = refs[0][...]
        return
    for r, ref in enumerate(refs):
        begin = pl.multiple_of((place ^ r) * each, each)
        wide[pl.ds(begin, each), :] = ref[...].astype(FULL)
    filled = each * len(refs)
    if filled < wide.shape[0]:
        wide[filled:, :] = jnp.zeros((wide.shape[0] - filled, wide.shape[1]), FULL)
    block = 16
    for size in range(16, 129, 16):
        block = size if out.shape[0] % size == 0 else block

    def narrow(i, carry):
        span = pl.ds(pl.multiple_of(i * block, block), block)
        out[span, :] = wide[span, :].astype(LOW)
        return carry

    lax.fori_loop(0, out.shape[0] // block, narrow, 0)


def flip(v):
    rows, cols = v.shape
    v = jnp.pad(v.astype(FULL), ((0, -rows % LANES), (0, -cols % LANES)))
    return v.T[:cols, :rows]


def cut_feed_kernel(at_ref, e_ref, s_ref, ek_ref, eg_ref, sk_ref, sg_ref, *, teams, hr):
    first = at_ref[0] % 2 == 0
    cols = s_ref.shape[1]
    e, s = e_ref[...].astype(FULL), s_ref[...].astype(FULL)
    for t in range(teams):
        a, b = e[:, 2 * t * hr : (2 * t + 1) * hr], e[:, (2 * t + 1) * hr : (2 * t + 2) * hr]
        ek_ref[:, t * hr : (t + 1) * hr] = jnp.where(first, a, b).astype(LOW)
        eg_ref[:, t * hr : (t + 1) * hr] = jnp.where(first, b, a).astype(LOW)
    for t in range(teams // 2):
        a, b = s[2 * t * hr : (2 * t + 1) * hr], s[(2 * t + 1) * hr : (2 * t + 2) * hr]
        sk_ref[:, t * cols : (t + 1) * cols] = jnp.where(first, a, b).astype(LOW)
        sg_ref[:, t * cols : (t + 1) * cols] = jnp.where(first, b, a).astype(LOW)


def join_feed_kernel(at_ref, ek_ref, eo_ref, sk_ref, so_ref, *out_refs, teams, hr):
    first, team = at_ref[0] % 2 == 0, at_ref[0] // 2
    feats = ek_ref.shape[0]
    cols = 2 * feats
    mine, other = flip(ek_ref[...]), flip(eo_ref[...])
    low = jnp.where(first, mine, other).astype(LOW)
    high = jnp.where(first, other, mine).astype(LOW)
    for t in range(teams):
        part = slice((t % (teams // 2)) * cols, (t % (teams // 2) + 1) * cols)
        here = first if t < teams // 2 else jnp.logical_not(first)
        piece = jnp.where(here, sk_ref[:, part], so_ref[:, part])
        for k, ref in enumerate(out_refs):

            @pl.when((team ^ t) == k)
            def _():
                ref[0, :, :feats] = low[t * hr : (t + 1) * hr, :]
                ref[0, :, feats:] = high[t * hr : (t + 1) * hr, :]
                ref[1] = piece


def lay_feed_kernel(at_ref, *refs, teams, hp):
    part_refs, e_ref, s_ref, whole = refs[:teams], *refs[teams:]
    team = at_ref[0] // 2
    for k, ref in enumerate(part_refs):
        whole[team ^ k] = ref[...]
    hr, cols = whole.shape[2:]
    e_ref[hr:, :] = jnp.zeros((hp - hr, e_ref.shape[1]), LOW)
    s_ref[...] = jnp.zeros_like(s_ref)
    for t in range(teams):
        e_ref[:hr, t * cols : (t + 1) * cols] = whole[t, 0]
        s_ref[:, t * hp : t * hp + hr] = flip(whole[t, 1]).astype(LOW)


def split_feed_kernel(at_ref, e_ref, s_ref, *out_refs, teams, hp):
    team = at_ref[0] // 2
    hr, cols = out_refs[0].shape[1:]
    for t in range(teams):
        piece = flip(s_ref[:, t * hp : t * hp + hr]).astype(LOW)
        for k, ref in enumerate(out_refs):

            @pl.when((team ^ t) == k)
            def _():
                ref[0] = e_ref[:hr, t * cols : (t + 1) * cols]
                ref[1] = piece


def part_feed_kernel(at_ref, *refs, teams):
    part_refs, ek_ref, eg_ref, sk_ref, sg_ref, whole = refs[:teams], *refs[teams:]
    first, team = at_ref[0] % 2 == 0, at_ref[0] // 2
    for k, ref in enumerate(part_refs):
        whole[team ^ k] = ref[...]
    hr, cols = whole.shape[2:]
    feats = cols // 2
    for t in range(teams):
        e = flip(whole[t, 0])
        a, b = e[:feats, :], e[feats:, :]
        ek_ref[:, t * hr : (t + 1) * hr] = jnp.where(first, a, b).astype(LOW)
        eg_ref[:, t * hr : (t + 1) * hr] = jnp.where(first, b, a).astype(LOW)
    for t in range(teams // 2):
        a, b = whole[t, 1], whole[teams // 2 + t, 1]
        sk_ref[:, t * cols : (t + 1) * cols] = jnp.where(first, a, b)
        sg_ref[:, t * cols : (t + 1) * cols] = jnp.where(first, b, a)


def end_feed_kernel(at_ref, ek_ref, eo_ref, sk_ref, so_ref, e_ref, s_ref, *, teams, hr):
    first = at_ref[0] % 2 == 0
    cols = s_ref.shape[1]
    mine, other = ek_ref[...].astype(FULL), eo_ref[...].astype(FULL)
    low, high = jnp.where(first, mine, other), jnp.where(first, other, mine)
    for t in range(teams):
        e_ref[:, 2 * t * hr : (2 * t + 1) * hr] = low[:, t * hr : (t + 1) * hr]
        e_ref[:, (2 * t + 1) * hr : (2 * t + 2) * hr] = high[:, t * hr : (t + 1) * hr]
    mine, other = sk_ref[...].astype(FULL), so_ref[...].astype(FULL)
    low, high = jnp.where(first, mine, other), jnp.where(first, other, mine)
    for t in range(teams // 2):
        s_ref[2 * t * hr : (2 * t + 1) * hr, :] = low[:, t * cols : (t + 1) * cols]
        s_ref[(2 * t + 1) * hr : (2 * t + 2) * hr, :] = high[:, t * cols : (t + 1) * cols]


def cut_mix_kernel(at_ref, rows_ref, *refs, teams, dp_n, each, span, starts, width):
    out_refs, merge_ref, full = refs[:teams], refs[teams], refs[teams + 1]
    team = at_ref[0] // 2
    part = width // dp_n
    for d in range(dp_n):
        full[:, d * each : (d + 1) * each] = rows_ref[d, :, :each]
        merge_ref[:, d * part : (d + 1) * part] = rows_ref[d, :, each:]
    full[:, dp_n * each :] = jnp.zeros((full.shape[0], full.shape[1] - dp_n * each), LOW)
    for t in range(teams):
        for k, ref in enumerate(out_refs):

            @pl.when((team ^ t) == k)
            def _():
                for m in range(3):
                    begin = m * width + starts[t]
                    ref[:, m * span : (m + 1) * span] = full[:, begin : begin + span]


def join_mix_kernel(at_ref, *refs, teams, dp_n, each, span, starts, width):
    part_refs, out_ref, whole, flat = refs[: 2 * teams], *refs[2 * teams :]
    team = at_ref[0] // 2
    share, half = width // teams, span // 2
    for i, ref in enumerate(part_refs):
        for m in range(3):
            low = m * span + (i // teams) * half
            whole[team ^ (i % teams), :, low : low + half] = ref[:, m * half : (m + 1) * half]
    for m in range(3):
        for t in range(teams):
            low = m * span + share * t - starts[t]
            begin = m * width + share * t
            flat[:, begin : begin + share] = whole[t, :, low : low + share]
    for d in range(dp_n):
        out_ref[d] = flat[:, d * each : (d + 1) * each]


def norm_kernel(sizes, rows, at_ref, *refs):
    count = len(sizes)
    vec_ref, first_ref, buf = refs[count:]
    load_pair(pl.program_id(0), sizes, refs[:count], buf, at_ref[0] % 2, rows)
    normal, _ = norm_parts(buf[...].astype(FULL))
    first_ref[...] = (normal * vec_ref[0:1, :] + vec_ref[1:2, :]).astype(LOW)


def mix_kernel(parts, at_ref, *refs):
    first_ref, bias_ref, mixed_ref, mix_ref, wide = refs[parts:]

    @pl.when(pl.program_id(0) == 0)
    def _():
        place_rows(at_ref[0], refs[:parts], wide, mix_ref)

    mixed = dot_nn(first_ref[...], mix_ref[...]) + bias_ref[0:1, :]
    mixed_ref[...] = (mixed * bias_ref[1:2, :]).astype(LOW)


def softmax_pieces(query, keys, seg_col, seg_row, index, block):
    scores = []
    for j in range(index + 1):
        piece = dot_nt(query, keys[j])
        seen = seg_col == seg_row[:, j * block : (j + 1) * block]
        if j == index:
            row_id = lax.broadcasted_iota(jnp.int32, (block, block), 0)
            col_id = lax.broadcasted_iota(jnp.int32, (block, block), 1)
            seen = seen & (col_id <= row_id)
        scores.append(jnp.where(seen, piece, -1e30))
    top = functools.reduce(jnp.maximum, [jnp.max(p, axis=1, keepdims=True) for p in scores])
    expo = [jnp.exp(p - top) for p in scores]
    total = functools.reduce(jnp.add, [jnp.sum(p, axis=1, keepdims=True) for p in expo])
    return expo, total


def attend_forward_kernel(count, block, dim, heads, base, at_ref, *refs):
    q_refs, k_refs, v_refs = refs[:count], refs[count : 2 * count], refs[2 * count : 3 * count]
    col_ref, row_ref = refs[3 * count : 3 * count + 2]
    out_refs = refs[3 * count + 2 :]
    pair = pl.program_id(0) + base
    team = at_ref[0] // 2
    for ref in out_refs:
        ref[...] = jnp.zeros_like(ref)
    for sub in range(LANES // dim):

        @pl.when(pair * (LANES // dim) + sub < heads)
        def _():
            lanes = slice(sub * dim, (sub + 1) * dim)
            keys = [r[:, lanes] for r in k_refs]
            values = [r[:, lanes] for r in v_refs]
            for i in range(count):
                rows = slice(i * block, (i + 1) * block)
                query = q_refs[i][:, lanes]
                expo, total = softmax_pieces(
                    query, keys, col_ref[rows, :], row_ref[...], i, block
                )
                mixed = functools.reduce(
                    jnp.add, [dot_nn(e.astype(LOW), v) for e, v in zip(expo, values)]
                )
                mixed = (mixed / total).astype(LOW)
                for k, ref in enumerate(out_refs):

                    @pl.when((team ^ i) == k)
                    def _():
                        ref[:, lanes] = mixed


def attend_backward_kernel(count, block, dim, heads, share, base, at_ref, *refs):
    q_refs, k_refs, v_refs = refs[:count], refs[count : 2 * count], refs[2 * count : 3 * count]
    g_refs = refs[3 * count : 4 * count]
    col_ref, row_ref, d_ref, acc_k, acc_v, grads = refs[4 * count :]
    pair = pl.program_id(0) + base
    team = at_ref[0] // 2
    scale = dim**-0.5
    d_ref[...] = jnp.zeros_like(d_ref)
    for k, ref in enumerate(g_refs):
        grads[pl.ds(pl.multiple_of((team ^ k) * block, block), block), :] = ref[...]
    for sub in range(LANES // dim):

        @pl.when(pair * (LANES // dim) + sub < heads)
        def _():
            lanes = slice(sub * dim, (sub + 1) * dim)
            column = lax.broadcasted_iota(jnp.int32, (1, dim), 1)
            column = column + at_ref[1 + team] + pair * LANES + sub * dim
            owned = (column >= share * team) & (column < share * (team + 1))
            owned = jnp.where(owned, 1.0, 0.0)
            keys = [r[:, lanes] for r in k_refs]
            values = [r[:, lanes] for r in v_refs]
            acc_k[...] = jnp.zeros_like(acc_k)
            acc_v[...] = jnp.zeros_like(acc_v)
            for i in range(count):
                rows = slice(i * block, (i + 1) * block)
                query = q_refs[i][:, lanes]
                grad = grads[rows, lanes]
                expo, total = softmax_pieces(
                    query, keys, col_ref[rows, :], row_ref[...], i, block
                )
                inverse = 1.0 / total
                probs = [e * inverse for e in expo]
                d_weights = [dot_nt(grad, v) for v in values[: i + 1]]
                delta = functools.reduce(
                    jnp.add,
                    [jnp.sum(p * d, axis=1, keepdims=True) for p, d in zip(probs, d_weights)],
                )
                d_query = jnp.zeros((block, dim), FULL)
                for j in range(i + 1):
                    cols = slice(j * block, (j + 1) * block)
                    d_scores = (probs[j] * (d_weights[j] - delta)).astype(LOW)
                    d_query = d_query + dot_nn(d_scores, keys[j])
                    acc_k[cols, :] += dot_tn(d_scores, query)
                    acc_v[cols, :] += dot_tn(probs[j].astype(LOW), grad)
                d_ref[0, rows, lanes] = (d_query * scale * owned).astype(LOW)
            d_ref[1, :, lanes] = (acc_k[...] * owned).astype(LOW)
            d_ref[2, :, lanes] = (acc_v[...] * owned).astype(LOW)


def merge_norm_kernel(at_ref, *refs, count, rows, span, share, dim, parts):
    att_refs, part_refs = refs[: 2 * count], refs[2 * count : 2 * count + parts]
    x_ref, vec_ref, hid_ref, s_ref, merge_ref, xs, buf, wide = refs[2 * count + parts :]
    core, team = at_ref[0] % 2, at_ref[0] // 2
    place_rows(at_ref[0], part_refs, wide, merge_ref)
    pair_rows([x_ref], core, rows, xs)
    hidden = xs[...].astype(FULL) + vec_ref[4:5, :]
    lane = lax.broadcasted_iota(jnp.int32, (1, span), 1)
    for k in range(count):
        other = team ^ k
        start = at_ref[1 + other]
        low = share * other - start
        owned = (lane >= low) & (lane < low + share)
        piece = jnp.concatenate([att_refs[k][...], att_refs[count + k][...]], axis=1)
        piece = jnp.where(owned, piece, jnp.zeros((), LOW))
        hidden = hidden + dot_nn(piece, merge_ref[pl.ds(pl.multiple_of(start, dim), span), :])
    hid_ref[...] = hidden
    normal, _ = norm_parts(hidden)
    buf[...] = (normal * vec_ref[5:6, :] + vec_ref[6:7, :]).astype(LOW)
    s_ref[:rows, :] = buf[row_slot(0, core, rows), :]
    s_ref[rows:, :] = buf[row_slot(1, core, rows), :]


def feed_kernel(sizes, at_ref, *refs):
    pieces = len(sizes)
    lows = [sum(sizes[:i]) for i in range(pieces)]
    sec_refs, g_refs = refs[:pieces], refs[pieces : 2 * pieces]
    weights, (bias_ref, act_ref, dpre_ref, sum_ref) = (
        refs[2 * pieces : 2 * pieces + 4],
        refs[2 * pieces + 4 : 2 * pieces + 8],
    )
    rest = refs[2 * pieces + 8 :]
    ds_refs, out_refs = rest[:pieces], rest[pieces : 2 * pieces]
    sec, g, acc_s, acc_o, e_held, s_held, sems = rest[2 * pieces :]
    step = pl.program_id(0)
    copies = [
        pltpu.make_async_copy(ref, held.at[i // 2], sems.at[i])
        for i, (ref, held) in enumerate(zip(weights, (e_held, s_held) * 2))
    ]

    @pl.when(step == 0)
    def _():
        for copy in copies:
            copy.start()
        for i in range(pieces):
            sec[lows[i] : lows[i] + sizes[i], :] = sec_refs[i][...]
            g[lows[i] : lows[i] + sizes[i], :] = g_refs[i][...]
        copies[0].wait()
        copies[1].wait()

    @pl.when(step == 1)
    def _():
        copies[2].wait()
        copies[3].wait()

    et, st = e_held[step], s_held[step]
    u = dot_nt(sec[...], et) + bias_ref[...]
    d_act = dot_nn(g[...], st)
    square = u * u
    tanh = jnp.tanh(0.7978845608028654 * u * (1.0 + 0.044715 * square))
    plus = 0.5 * (1.0 + tanh)
    act = (u * plus).astype(LOW)
    slope = plus + u * (0.5 * 0.7978845608028654) * (1.0 - tanh * tanh) * (
        1.0 + 3 * 0.044715 * square
    )
    d_pre = (d_act * slope).astype(LOW)
    act_ref[...] = act
    dpre_ref[...] = d_pre
    sum_ref[...] = jnp.broadcast_to(total_rows(d_pre.astype(FULL)), sum_ref.shape)
    part_s = dot_nn(d_pre, et)
    part_o = dot_nt(act, st)

    @pl.when(step == 0)
    def _():
        acc_s[...] = part_s
        acc_o[...] = part_o

    @pl.when(step == 1)
    def _():
        for i in range(pieces):
            here = slice(lows[i], lows[i] + sizes[i])
            ds_refs[i][...] = (acc_s[here, :] + part_s[here, :]).astype(LOW)
            out_refs[i][...] = (acc_o[here, :] + part_o[here, :]).astype(LOW)


def feed_grad_kernel(pieces, sizes, turned, at_ref, *refs):
    count = len(pieces)
    piece_refs, unit_refs = refs[:count], refs[count : count + len(sizes)]
    mine_ref, give_ref, held, units, sems = refs[count + len(sizes) :]
    step = pl.program_id(0)
    copies = [
        pltpu.make_async_copy(
            ref, held.at[sum(pieces[:i]) : sum(pieces[: i + 1]), :], sems.at[i]
        )
        for i, ref in enumerate(piece_refs)
    ]

    @pl.when(step == 0)
    def _():
        for copy in copies:
            copy.start()
        for copy in copies:
            copy.wait()

    low = 0
    for size, ref in zip(sizes, unit_refs):
        units[low : low + size, :] = ref[...]
        low += size
    if turned:
        grad = dot_tn(held[...], units[...]).astype(LOW)
    else:
        grad = dot_tn(units[...], held[...]).astype(LOW)

    @pl.when(step == 0)
    def _():
        give_ref[...] = grad

    @pl.when(step == 1)
    def _():
        mine_ref[...] = grad


def second_back_kernel(at_ref, *refs, count, rows, span, dim, terms):
    rest = refs[terms:]
    hid_ref, g_ref, merge_ref, vec_ref = rest[:4]
    dh_ref, db_ref, sum_ref = rest[4:7]
    att_refs = rest[7 : 7 + count]
    ds, g = rest[7 + count :]
    core, team = at_ref[0] % 2, at_ref[0] // 2
    pair_rows(refs[:terms], core, rows, ds)
    pair_rows([g_ref], core, rows, g)
    normal, inverse = norm_parts(hid_ref[...])
    d_second = ds[...]
    g_full = g[...].astype(FULL)
    d_hidden = g_full + norm_back(d_second, vec_ref[5:6, :], normal, inverse)
    dh_ref[...] = d_hidden
    d_branch = d_hidden.astype(LOW)
    db_ref[...] = d_branch
    sum_ref[0:1, :] = total_rows(d_second * normal)
    sum_ref[1:2, :] = total_rows(d_second)
    sum_ref[2:3, :] = total_rows(d_branch.astype(FULL))
    sum_ref[3:4, :] = total_rows(g_full)
    sum_ref[4:8, :] = jnp.zeros((4, sum_ref.shape[1]), FULL)
    for k, ref in enumerate(att_refs):
        start = pl.multiple_of(at_ref[1 + (team ^ k)], dim)
        ref[...] = dot_nt(d_branch, merge_ref[pl.ds(start, span), :]).astype(LOW)


def split_cores(core, value, mine_ref, give_ref):
    feats = mine_ref.shape[1]
    for t in range(mine_ref.shape[0]):
        low = value[2 * t * feats : (2 * t + 1) * feats, :]
        high = value[(2 * t + 1) * feats : (2 * t + 2) * feats, :]
        mine_ref[t] = jnp.where(core == 0, low, high).astype(LOW)
        give_ref[t] = jnp.where(core == 0, high, low).astype(LOW)


def merge_grad_kernel(at_ref, *refs, count, span, share, dim, step):
    att_refs = refs[: 2 * count]
    db_ref, mine_ref, give_ref, acc, held = refs[2 * count :]
    team = at_ref[0] // 2
    acc[...] = jnp.zeros_like(acc)
    lane = lax.broadcasted_iota(jnp.int32, (1, span), 1)
    for k in range(count):
        other = team ^ k
        low = share * other - at_ref[1 + other]
        owned = (lane >= low) & (lane < low + share)
        piece = jnp.concatenate([att_refs[k][...], att_refs[count + k][...]], axis=1)
        piece = jnp.where(owned, piece, jnp.zeros((), LOW))
        for c in range(span // step):
            held[k * (span // step) + c] = piece[:, c * step : (c + 1) * step]

    def add(i, carry):
        start = at_ref[1 + (team ^ (i // (span // step)))] + (i % (span // step)) * step
        acc[pl.ds(pl.multiple_of(start, dim), step), :] += dot_tn(held[i], db_ref[...])
        return carry

    lax.fori_loop(0, count * (span // step), add, 0)
    split_cores(at_ref[0] % 2, acc, mine_ref, give_ref)


def first_back_kernel(sizes, rows, span, at_ref, *refs):
    count = len(sizes)
    sides = span // LANES
    d_refs, x_refs, refs = refs[:sides], refs[sides : sides + count], refs[sides + count :]
    mix_ref, sum_ref = refs[:2]
    out_refs = refs[2 : 2 + count]
    buf, low, joined = refs[2 + count :]
    step = pl.program_id(0)
    core = at_ref[0] % 2
    load_pair(step, sizes, x_refs, buf, core, rows)
    normal, _ = norm_parts(buf[...].astype(FULL))
    for m in range(3):
        for i, d_ref in enumerate(d_refs):
            begin = m * span + i * LANES
            joined[:, begin : begin + LANES] = d_ref[m]
    d_first = dot_nt(joined[...], mix_ref[...])

    @pl.when(step == 0)
    def _():
        sum_ref[...] = jnp.zeros_like(sum_ref)

    sum_ref[0:1, :] += total_rows(d_first * normal)
    sum_ref[1:2, :] += total_rows(d_first)
    low[...] = d_first.astype(LOW)
    begin = 0
    for size, ref in zip(sizes, out_refs):
        for i in range(size // rows):
            r = begin // rows + i

            @pl.when(step == r // 2)
            def _():
                ref[i * rows : (i + 1) * rows, :] = low[row_slot(r % 2, core, rows), :]

        begin += size


def mix_grad_kernel(at_ref, *refs):
    first_ref, mine_ref, give_ref, sum_ref, first_t, held, d = refs[-7:]

    @pl.when(pl.program_id(0) == 0)
    def _():
        first_t[...] = first_ref[...].T

    for i, ref in enumerate(refs[:-7]):
        d[:, i * LANES : (i + 1) * LANES] = ref[0]
    sum_ref[...] = jnp.broadcast_to(total_rows(d[...].astype(FULL)), sum_ref.shape)
    held[...] = dot_nn(first_t[...], d[...])
    split_cores(at_ref[0] % 2, held, mine_ref, give_ref)


def block_out_kernel(at_ref, *refs, rows, terms):
    hid_ref, vec_ref, o0_ref, o1_ref = refs[terms:]
    core = at_ref[0] % 2
    for half, ref in enumerate((o0_ref, o1_ref)):
        here = slice(half * rows, (half + 1) * rows)
        value = hid_ref[row_slot(half, core, rows), :] + vec_ref[7:8, :]
        value = functools.reduce(jnp.add, [t[here, :].astype(FULL) for t in refs[:terms]], value)
        ref[...] = value.astype(LOW)


def input_grad_kernel(at_ref, *refs, rows, terms):
    dh_ref, x_ref, vec_ref, o0_ref, o1_ref = refs[terms:]
    core = at_ref[0] % 2
    for half, ref in enumerate((o0_ref, o1_ref)):
        here = slice(half * rows, (half + 1) * rows)
        d_first = functools.reduce(jnp.add, [t[here, :].astype(FULL) for t in refs[:terms]])
        normal, inverse = norm_parts(x_ref[here, :].astype(FULL))
        back = norm_back(d_first, vec_ref[0:1, :], normal, inverse)
        ref[...] = dh_ref[row_slot(half, core, rows), :] + back


def body(
    seq_n,
    dp_n,
    inputs,
    segments,
    cotangent,
    mix_weight,
    merge_weight,
    expand_weight,
    shrink_weight,
    first_gain,
    first_bias,
    query_bias,
    value_bias,
    merge_bias,
    second_gain,
    second_bias,
    expand_bias,
    shrink_bias,
):
    micro, rows, width = inputs.shape
    length = segments.shape[1]
    dim = width // HEADS
    teams = seq_n // 2
    bits = teams.bit_length() - 1
    pieces = seq_n
    own_rows = 2 * rows
    feats = width // seq_n
    share = width // teams
    begins = [share * t // dim for t in range(teams)]
    heads = max(-(-share * (t + 1) // dim) - begins[t] for t in range(teams))
    starts = [dim * min(h, HEADS - heads) for h in begins]
    span = -(-heads * dim // (2 * LANES)) * 2 * LANES
    part = span // 2
    hidden_units = expand_weight.shape[1] * dp_n
    hr = hidden_units // dp_n // teams // 2
    hp = hr
    while hp % 16 or dp_n * hp % LANES:
        hp += 1
    half = dp_n * hp
    units = 2 * half
    whole_rows = feats % 8 == 0

    place = lax.axis_index("seq")
    core = place % 2
    team = place // 2
    at = jnp.concatenate([place[None].astype(jnp.int32), jnp.asarray(starts, jnp.int32)])

    def hop(v, mask):
        shape = v.shape
        if len(shape) == 2 and shape[0] % LANES == 0 and shape[1] % LANES:
            v = v.reshape(2, shape[0] // 2, shape[1])
        return lax.ppermute(v, "seq", [(i, i ^ mask) for i in range(seq_n)]).reshape(shape)

    def pick(v, index):
        return lax.dynamic_index_in_dim(v, index, 0, keepdims=False)

    def along(v):
        return lax.all_gather(v, "dp", axis=0)

    def scatter(v):
        return lax.psum_scatter(v, "dp", scatter_dimension=0)

    def by_core(mine, other):
        return jnp.where(core == 0, jnp.stack([mine, other]), jnp.stack([other, mine]))

    def tie(v, *others):
        return lax.optimization_barrier((v, *others))[0]

    def meet(kept, moved):
        both = lax.optimization_barrier((*kept, *moved))
        return both[: len(kept)], both[len(kept) :]

    def own_pair(v, *others):
        mine = pick(v, core)
        return jnp.concatenate([mine, hop(tie(pick(v, 1 - core), *others), 1)], axis=0)

    def gather_near(own):
        if teams == 4:
            return [own, hop(own, 2), hop(own, 4)]
        return exchange([own] * teams)

    def gather_far(near, *others):
        if teams == 4:
            x, y = tie(near[1][:rows], *others), tie(near[2][rows:], *others)
            return [*near, hop(x, 4), hop(y, 2)]
        return near

    def add_low(a, b):
        return (a.astype(FULL) + b.astype(FULL)).astype(LOW)

    def reduce_far(p):
        return [hop(p[3], 2), hop(p[4], 4)] if teams == 4 else []

    def reduce_near(p, far):
        if teams == 4:
            folded = simple(
                fold_kernel, "fold", (p[1], p[2], *far), [((own_rows, width), LOW)] * 2
            )
            return [hop(folded[0], 2), hop(folded[1], 4)]
        return exchange(p)[1:]

    def exchange(parts):
        return [parts[0]] + [hop(parts[k], 2 * k) for k in range(1, teams)]

    def assemble(parts, extra=0):
        out = jnp.zeros((seq_n + extra,) + parts[0].shape, parts[0].dtype)
        for r in range(pieces):
            out = lax.dynamic_update_index_in_dim(out, parts[r], place ^ r, 0)
        return out.reshape((-1,) + parts[0].shape[1:])

    def swap_out(out0, out1):
        return by_core(out0, hop(out1, 1))

    def gather_small(v):
        cur = v[None]
        for b in range(bits + 1):
            got = hop(cur, 1 << b)
            bit = (place >> b) & 1
            cur = jnp.where(
                bit == 0, jnp.concatenate([cur, got]), jnp.concatenate([got, cur])
            )
        return cur

    def reduce_small(v):
        for b in reversed(range(bits + 1)):
            half_n = v.shape[0] // 2
            bit = (place >> b) & 1
            mine = jnp.where(bit == 0, v[:half_n], v[half_n:])
            give = jnp.where(bit == 0, v[half_n:], v[:half_n])
            v = mine + hop(give, 1 << b)
        v = v[0]
        for b in range(dp_n.bit_length() - 1):
            v = v + lax.ppermute(v, "dp", [(i, i ^ (1 << b)) for i in range(dp_n)])
        return v

    def simple(kernel, name, operands, outs, scratch=(), flops=0, nbytes=None, after=(), **named):
        if nbytes is None:
            nbytes = sum(v.size * v.dtype.itemsize for v in operands)
            nbytes += sum(4 * functools.reduce(lambda a, b: a * b, s) for s, _ in outs)
        return call(
            functools.partial(kernel, **named),
            name,
            (1,),
            at,
            operands,
            [fixed(v.shape) for v in operands],
            outs,
            [fixed(s) for s, _ in outs],
            [pltpu.VMEM(s, d) for s, d in scratch],
            flops,
            nbytes,
            after=after,
        )

    each = mix_weight.shape[1]
    mix_local = jnp.concatenate([mix_weight, merge_weight], axis=1)
    mix_rows = along(mix_local)
    small = (
        first_gain,
        first_bias,
        query_bias,
        value_bias,
        merge_bias,
        second_gain,
        second_bias,
        shrink_bias,
        expand_bias,
    )
    packed = gather_small(jnp.concatenate(small))
    vec = packed[:, : 8 * feats].reshape(seq_n, 8, feats).transpose(1, 0, 2)
    vec = vec.reshape(8, width).astype(FULL)
    e_bias = packed[:, 8 * feats :].reshape(-1).astype(FULL)
    x_own = own_pair(inputs)
    x_near = gather_near(tie(x_own, packed))

    cols = shrink_weight.shape[1]
    e_shape, s_shape = (feats, teams * hr), (hr, teams // 2 * cols)
    ek, eg, sk, sg = simple(
        cut_feed_kernel,
        "cut_feed",
        (expand_weight, shrink_weight),
        [(e_shape, LOW), (e_shape, LOW), (s_shape, LOW), (s_shape, LOW)],
        after=(mix_local,),
        teams=teams,
        hr=hr,
    )
    feed_cut = ((2, hr, cols), LOW)
    feed_cuts = simple(
        join_feed_kernel,
        "join_feed",
        (ek, hop(eg, 1), sk, hop(sg, 1)),
        [feed_cut] * teams,
        after=tuple(x_near[1:]),
        teams=teams,
        hr=hr,
    )
    feed_cuts = exchange(feed_cuts)
    x_pieces = gather_far(x_near)
    e_cut, s_cut = simple(
        lay_feed_kernel,
        "lay_feed",
        feed_cuts,
        [((hp, width), LOW), ((cols, half), LOW)],
        [((teams, 2, hr, cols), LOW)],
        teams=teams,
        hp=hp,
    )

    mix_cut = ((feats, 3 * span), LOW)
    *cuts, merge_rows = simple(
        cut_mix_kernel,
        "cut_mix",
        (mix_rows,),
        [mix_cut] * teams + [((feats, width), LOW)],
        [((feats, 3 * width + LANES), LOW)],
        after=(e_cut, s_cut, vec, *x_pieces[3:]),
        teams=teams,
        dp_n=dp_n,
        each=each,
        span=span,
        starts=starts,
        width=width,
    )
    expand_mine = along(e_cut).reshape(half, width)
    shrink_mine = along(tie(s_cut, expand_mine[0])).reshape(width, half)

    start = at[1 + team]

    def windowed(row):
        return lax.dynamic_slice_in_dim(jnp.pad(vec[row], (0, 2 * LANES)), start, span, 0)

    blank = jnp.zeros((span,), FULL)
    mix_bias = jnp.concatenate([windowed(2), blank, windowed(3)])
    shrinking = jnp.where(jnp.arange(3 * span) < span, dim**-0.5, 1.0).astype(FULL)
    mix_bias = jnp.concatenate([mix_bias[None], shrinking[None], jnp.zeros((6, 3 * span), FULL)])

    act_bytes = length * width * 2
    piece_spec = fixed((rows, width))
    vec_spec = fixed((8, width))
    mix_spec = fixed((width, 3 * span))
    team_rows = lambda n: pl.BlockSpec((own_rows, n), lambda k, a: (k ^ (a[0] // 2), 0))
    x_sizes = [v.shape[0] for v in x_pieces]
    row_specs = lambda sizes: [fixed((n, width)) for n in sizes]
    (first,) = call(
        functools.partial(norm_kernel, x_sizes, rows),
        "norm",
        (teams,),
        at,
        (*x_pieces, vec),
        row_specs(x_sizes) + [vec_spec],
        [((length, width), LOW)],
        [team_rows(width)],
        [pltpu.VMEM((own_rows, width), LOW)],
        length * width * 10,
        2 * act_bytes,
        after=(cuts[0],),
    )
    got = exchange(cuts)
    (first,), got = meet((first,), got)
    merge_rows = tie(merge_rows, *got)
    mix = [v for g in got for v in (g, hop(g, 1))]
    extra = -(-max(0, starts[-1] + span - width) // feats)
    if not whole_rows:
        mix = [assemble(mix)]
    if teams == 4:
        near = [hop(merge_rows, 2), hop(merge_rows, 4)]
    else:
        near = exchange([merge_rows] * teams)[1:]
    merge_shape = (width + extra * feats, width)

    chip_rows = lambda n: pl.BlockSpec((own_rows, n), lambda k, a: (k, 0))
    mixed, mix = call(
        functools.partial(mix_kernel, len(mix)),
        "mix",
        (teams,),
        at,
        (*mix, first, mix_bias),
        [fixed(v.shape) for v in mix] + [chip_rows(width), fixed((8, 3 * span))],
        [((length, 3 * span), LOW), ((width, 3 * span), LOW)],
        [chip_rows(3 * span), mix_spec],
        [pltpu.VMEM((width, 3 * span), FULL)],
        2 * length * width * 3 * span,
        4 * act_bytes,
    )

    (mixed, mix), near = meet((mixed, mix), near)
    merge = [merge_rows, *near]
    if teams == 4:
        merge.append(hop(merge[1], 4))
    g_own = own_pair(cotangent)
    g_near = gather_near(tie(g_own, mixed))

    seg = pick(segments, core)
    per = span // LANES
    runs = [(0, per // 2), (per // 2, per // 2)]
    seg_specs = [fixed((length, 1)), fixed((1, length))]
    segs = (seg.reshape(length, 1), seg.reshape(1, length))
    column = pl.BlockSpec((own_rows, LANES), lambda p, a: (0, p))

    def qkv_specs(base):
        return [
            pl.BlockSpec((own_rows, LANES), lambda p, a, j=j, m=m: (j, m * per + base + p))
            for m in range(3)
            for j in range(teams)
        ]

    attended, wait = [], ()
    for base, count in runs:
        got = call(
            functools.partial(attend_forward_kernel, teams, own_rows, dim, heads, base),
            "attend_forward",
            (count,),
            at,
            (*([mixed] * (3 * teams)), *segs),
            qkv_specs(base) + seg_specs,
            [((own_rows, part), LOW)] * teams,
            [column] * teams,
            [],
            length * length * dim * heads * 2,
            4 * length * part * 2,
            length * length * heads // 4,
            after=wait,
        )
        if base == 0:
            got, moved = meet(got, g_near[1:])
            g_near = [g_own, *moved]
            wait = (got[0],)
            attended = exchange(got)
            expand_mine, shrink_mine = tie(expand_mine, got[0]), tie(shrink_mine, got[0])
        else:
            got, moved = meet(got, (*attended, *merge[3:]))
            attended = [*moved[:teams], *exchange(got)]
            merge = [*merge[:3], *moved[teams:]]
    merge = [v for g in merge for v in (g, hop(g, 1))]
    if not whole_rows:
        merge = [assemble(merge, extra)]

    weights = (expand_mine, shrink_mine, hop(expand_mine, 1), hop(shrink_mine, 1))
    wide = ((own_rows, width), FULL)
    wide_low = ((own_rows, width), LOW)
    piece = ((rows, width), LOW)
    hidden, second, merge = simple(
        merge_norm_kernel,
        "merge_norm",
        (*attended, *merge, x_own, vec),
        [wide, wide_low, (merge_shape, LOW)],
        [wide_low, wide_low, (merge_shape, FULL)],
        2 * own_rows * width * span * teams,
        count=teams,
        rows=rows,
        span=span,
        share=share,
        dim=dim,
        parts=len(merge),
    )
    second = gather_near(second)
    g_pieces = g_near

    e_row = e_bias.reshape(dp_n, teams, 2, hr).transpose(1, 2, 0, 3)
    e_row = pick(e_row, team)
    e_row = jnp.stack([pick(e_row, core), pick(e_row, 1 - core)])
    e_row = jnp.pad(e_row, ((0, 0), (0, 0), (0, hp - hr))).reshape(1, units)

    groups = [[0], [1, 2], [3, 4]] if teams == 4 else [[k] for k in range(teams)]
    acts, d_pres, e_sums, d_second, out = [], [], [], [], []
    for group in groups:
        sizes = [x_sizes[i] for i in group]
        n, m = len(sizes), sum(sizes)
        half_spec = pl.BlockSpec((m, half), lambda f, a: (0, f))
        res = call(
            functools.partial(feed_kernel, sizes),
            "feed",
            (2,),
            at,
            (*[second[i] for i in group], *[g_pieces[i] for i in group], *weights, e_row),
            row_specs(sizes) * 2
            + [pl.BlockSpec(memory_space=pl.ANY)] * 4
            + [pl.BlockSpec((1, half), lambda f, a: (0, f))],
            [((m, units), LOW)] * 2
            + [((8, units), FULL)]
            + [((size, width), LOW) for size in sizes] * 2,
            [half_spec, half_spec, pl.BlockSpec((8, half), lambda f, a: (0, f))]
            + row_specs(sizes) * 2,
            [pltpu.VMEM((m, width), LOW)] * 2
            + [pltpu.VMEM((m, width), FULL)] * 2
            + [
                pltpu.VMEM((2, half, width), LOW),
                pltpu.VMEM((2, width, half), LOW),
                pltpu.SemaphoreType.DMA((4,)),
            ],
            8 * m * width * units,
            4 * width * units + 12 * m * width,
            m * units,
            after=tuple(acts[-1:]),
        )
        if len(acts) == 0:
            res, moved = meet(res, second[1:])
            second = gather_far([second[0], *moved])
            g_pieces = gather_far(g_pieces, *moved)
        elif len(acts) == 1 and teams == 4:
            res, moved = meet(res, (*second[3:], *g_pieces[3:]))
            second, g_pieces = [*second[:3], *moved[:2]], [*g_pieces[:3], *moved[2:]]
        acts.append(res[0])
        d_pres.append(res[1])
        e_sums.append(res[2])
        d_second += res[3 : 3 + n]
        out += res[3 + n :]

    sizes = [v.shape[0] for v in acts]
    def feed_grad(name, parts, units_of, turned, after):
        shape = (width, half) if turned else (half, width)
        return call(
            functools.partial(feed_grad_kernel, x_sizes, sizes, turned),
            name,
            (2,),
            at,
            (*parts, *units_of),
            [pl.BlockSpec(memory_space=pl.ANY)] * len(x_sizes)
            + [pl.BlockSpec((s, half), lambda f, a: (0, 1 - f)) for s in sizes],
            [(shape, LOW)] * 2,
            [fixed(shape)] * 2,
            [
                pltpu.VMEM((length, width), LOW),
                pltpu.VMEM((length, half), LOW),
                pltpu.SemaphoreType.DMA((len(x_sizes),)),
            ],
            2 * length * width * units,
            2 * act_bytes + 2 * width * units,
            after=after,
        )

    far = reduce_far(d_second)
    sm, sg = feed_grad("shrink_grad", g_pieces, acts, True, ())
    (sm, sg), far = meet((sm, sg), far)
    near = reduce_near(d_second, far)
    s_got = hop(sg, 1)
    em, eg = feed_grad("expand_grad", second, d_pres, False, (sm,))
    (em, eg), (s_got, *near) = meet((em, eg), (s_got, *near))
    d_second = [d_second[0], *near]
    s_sum = add_low(sm, s_got)
    e_got = hop(eg, 1)
    g_shrink = scatter(s_sum.reshape(dp_n, cols, half))

    terms = len(d_second)
    window = ((own_rows, span), LOW)
    d_hidden, d_branch, second_sums, *d_attended = simple(
        second_back_kernel,
        "second_back",
        (*d_second, hidden, g_own, merge, vec),
        [wide, wide_low, ((8, width), FULL)] + [window] * teams,
        [wide, wide_low],
        2 * own_rows * width * span * teams,
        after=(s_sum,),
        count=teams,
        rows=rows,
        span=span,
        dim=dim,
        terms=terms,
    )
    d_attended = exchange(d_attended)

    step = min(span, CHUNK)
    feat_block = ((teams, feats, width), LOW)
    mine, give = simple(
        merge_grad_kernel,
        "merge_grad",
        (*attended, d_branch),
        [feat_block, feat_block],
        [(merge_shape, FULL), ((teams * (span // step), own_rows, step), LOW)],
        2 * own_rows * width * span * teams,
        count=teams,
        span=span,
        share=share,
        dim=dim,
        step=step,
    )

    (mine, give), (e_got, *d_attended) = meet((mine, give), (e_got, *d_attended))
    e_sum = add_low(em, e_got)
    g_expand = scatter(e_sum.reshape(dp_n, hp, width))
    out_far = reduce_far([*out[:3], *[tie(v, *d_attended) for v in out[3:]]])

    def core_parts(mine, got):
        return [add_low(pick(mine, team ^ k), pick(got, team ^ k)) for k in range(teams)]

    merge_got = hop(give, 1)
    merge_mine = mine

    d_parts, g_mix, mix_sums = [], [], []
    mix_block = ((teams, feats, 3 * part), LOW)
    wait = (e_sum, mixed)
    merge_near = []
    for base in range(per):
        (d_part,) = call(
            functools.partial(attend_backward_kernel, teams, own_rows, dim, heads, share, base),
            "attend_backward",
            (1,),
            at,
            (*([mixed] * (3 * teams)), *d_attended, *segs),
            qkv_specs(base)
            + [pl.BlockSpec((own_rows, LANES), lambda p, a, base=base: (0, base + p))] * teams
            + seg_specs,
            [((3, length, LANES), LOW)],
            [pl.BlockSpec((3, length, LANES), lambda p, a: (0, 0, p))],
            [
                pltpu.VMEM((length, dim), FULL),
                pltpu.VMEM((length, dim), FULL),
                pltpu.VMEM((length, LANES), LOW),
            ],
            5 * length * length * dim * heads // per * 2,
            8 * length * LANES * 2,
            length * length * heads // per // 2,
            after=wait,
        )
        if base == 0:
            (d_part,), (merge_got, *out_far) = meet((d_part,), (merge_got, *out_far))
            out_near = reduce_near(out, out_far)
            g_merge = core_parts(merge_mine, merge_got)
        if base == per - 1:
            (d_part,), merge_near = meet((d_part,), merge_near)
        d_parts.append(d_part)
        wait = (d_part,)
        if base % (per // 2) == per // 2 - 1:
            sides = d_parts[-(per // 2) :]
            mine, give, sums = call(
                mix_grad_kernel,
                "mix_grad",
                (3,),
                at,
                (*sides, first),
                [pl.BlockSpec((1, length, LANES), lambda c, a: (c, 0, 0))] * len(sides)
                + [fixed((length, width))],
                [mix_block, mix_block, ((8, 3 * part), FULL)],
                [pl.BlockSpec((teams, feats, part), lambda c, a: (0, 0, c))] * 2
                + [pl.BlockSpec((8, part), lambda c, a: (0, c))],
                [
                    pltpu.VMEM((width, length), LOW),
                    pltpu.VMEM((width, part), FULL),
                    pltpu.VMEM((length, part), LOW),
                ],
                2 * length * width * 3 * part,
                3 * act_bytes,
            )
            if base < per - 1:
                (mine, give), out_near = meet((mine, give), out_near)
                merge_near = exchange([tie(v, give) for v in g_merge])[1:]
                mix_got = hop(give, 1)
                wait = (give,)
            else:
                (mine, give), mix_near = meet((mine, give), g_mix[1:])
                g_mix = [g_mix[0], *mix_near]
                mix_got = hop(give, 1)
            mix_sums.append(sums[0].reshape(3, part))
            g_mix += exchange(core_parts(mine, mix_got))
    out = [out[0], *out_near]
    g_merge = [g_merge[0], *merge_near]
    g_merge = functools.reduce(jnp.add, [v.astype(FULL) for v in g_merge]).astype(LOW)
    merge_each = width // dp_n
    g_merge = jnp.stack(
        [g_merge[:, d * merge_each : (d + 1) * merge_each] for d in range(dp_n)]
    )
    grad_merge = scatter(g_merge).astype(FULL)

    block_out = simple(
        block_out_kernel,
        "block_out",
        (*out, hidden, vec),
        [piece, piece],
        after=(d_parts[-1],),
        rows=rows,
        terms=terms,
    )
    block_out = swap_out(*block_out)

    feed_cuts = simple(
        split_feed_kernel,
        "split_feed",
        (g_expand, g_shrink),
        [feed_cut] * teams,
        teams=teams,
        hp=hp,
    )
    groups = [([3, 4], 3), ([1, 2], 1), ([0], 0)] if teams == 4 else [([k], k) for k in range(teams)]
    d_first, first_sums, wait = [None] * len(x_sizes), [], (give,)
    for group, low in groups:
        sizes = [x_sizes[i] for i in group]
        n = sum(sizes) // own_rows
        sums, *got = call(
            functools.partial(first_back_kernel, sizes, rows, span),
            "first_back",
            (n,),
            at,
            (*d_parts, *[x_pieces[i] for i in group], mix),
            [
                pl.BlockSpec(
                    (3, own_rows, LANES), lambda i, a, low=low: (0, (i + low) ^ (a[0] // 2), 0)
                )
            ]
            * per
            + row_specs(sizes)
            + [fixed((width, 3 * span))],
            [((8, width), FULL)] + [((size, width), LOW) for size in sizes],
            [vec_spec] + row_specs(sizes),
            [
                pltpu.VMEM((own_rows, width), LOW),
                pltpu.VMEM((own_rows, width), LOW),
                pltpu.VMEM((own_rows, 3 * span), LOW),
            ],
            2 * n * own_rows * width * 3 * span,
            n * own_rows * width * 8,
            after=wait,
        )
        wait = (sums, feed_cuts[0])
        first_sums.append(sums)
        for i, v in zip(group, got):
            d_first[i] = v
    first_sums = functools.reduce(jnp.add, first_sums)
    far = reduce_far(d_first)
    if teams == 4:
        (d_first[0], d_first[1], d_first[2]), far = meet(d_first[:3], far)
    d_first = [d_first[0], *reduce_near(d_first, far)]

    (g_mix,) = simple(
        join_mix_kernel,
        "join_mix",
        g_mix,
        [((dp_n, feats, each), LOW)],
        [((teams, feats, 3 * span), LOW), ((feats, 3 * width), LOW)],
        teams=teams,
        dp_n=dp_n,
        each=each,
        span=span,
        starts=starts,
        width=width,
    )
    grad_mix = scatter(g_mix).astype(FULL)

    ek, eg, sk, sg = simple(
        part_feed_kernel,
        "part_feed",
        exchange(feed_cuts),
        [(e_shape, LOW), (e_shape, LOW), (s_shape, LOW), (s_shape, LOW)],
        [((teams, 2, hr, cols), LOW)],
        teams=teams,
    )
    grad_expand, grad_shrink = simple(
        end_feed_kernel,
        "end_feed",
        (ek, hop(eg, 1), sk, hop(sg, 1)),
        [(expand_weight.shape, FULL), (shrink_weight.shape, FULL)],
        teams=teams,
        hr=hr,
    )

    def spread(v):
        return lax.dynamic_update_slice_in_dim(
            jnp.zeros((width + 2 * LANES,), FULL), v, start, 0
        )[:width]

    mix_sums = jnp.concatenate(mix_sums, axis=1)
    d_e = functools.reduce(jnp.add, [s[0] for s in e_sums]).reshape(2, dp_n, hp)[:, :, :hr]
    d_e = jnp.where(core == 0, d_e, d_e[::-1]).transpose(1, 0, 2)
    d_e = lax.dynamic_update_slice_in_dim(
        jnp.zeros((dp_n, teams, 2, hr), FULL), d_e[:, None], team, 1
    )
    partial = (
        first_sums[0],
        first_sums[1],
        spread(mix_sums[0]),
        spread(mix_sums[2]),
        second_sums[2],
        second_sums[0],
        second_sums[1],
        second_sums[3],
        d_e.reshape(-1),
    )
    total = reduce_small(
        jnp.concatenate([v.reshape(seq_n, -1) for v in partial], axis=1)
    )
    piece_full = ((rows, width), FULL)
    input_grad = simple(
        input_grad_kernel,
        "input_grad",
        (*d_first, d_hidden, x_own, vec),
        [piece_full, piece_full],
        after=(total, grad_expand),
        rows=rows,
        terms=terms,
    )
    input_grad = swap_out(*input_grad)

    ends = [total[i * feats : (i + 1) * feats] for i in range(8)]
    vectors = (*ends[:7], total[8 * feats :], ends[7])
    return (block_out, input_grad, grad_mix, grad_merge, grad_expand, grad_shrink, *vectors)


def solution(mesh):
    rows = P("dp", "seq", None)
    matrix = P("seq", "dp")
    vector = P("seq")
    return jax.shard_map(
        functools.partial(body, mesh.shape["seq"], mesh.shape["dp"]),
        mesh=mesh,
        in_specs=(rows, P("dp", None), rows) + (matrix,) * 4 + (vector,) * 9,
        out_specs=(rows, rows) + (matrix,) * 4 + (vector,) * 9,
        check_vma=False,
    )
```

time: 1110 us -> 717 us (0.65)
  local copies, waits for them, and re-layouts: 364 us -> 38.5 us
  Pallas kernels: 82.5 us -> 378 us
  matrix products: 177 us -> 0 us
  other arithmetic: 163 us -> 34.3 us
  blocking collectives: 33 us -> 0 us
  waiting for transfers between devices: 189 us -> 163 us
    pallas_call x2 -> x34, Pallas kernels: 82.5 us -> 378 us  [call(): pl.pallas_call(kernel, grid_spec=spec, out_shape=[jax.ShapeDtypeStruct(s,...]
    dot_general x22 -> x0, matrix products: 177 us -> none  [the longest x8 61.5 us: dot_tn(): lax.dot_general(left, right, (((0,), (0,)), ((), ())), preferred_element_...]
    convert_element_type x21 -> x4, local copies, waits for them, and re-layouts: 46.9 us -> 0.92 us  [the longest x3 0.82 us: body(): vec = vec.reshape(8, width).astype(FULL)]
    ppermute x20 -> x0, local copies, waits for them, and re-layouts: 44.8 us -> none  [hop(): return lax.ppermute(v, 'seq', [(i, i ^ mask) for i in range(seq_n)])]
    reshape x15 -> x3, local copies, waits for them, and re-layouts: 45 us -> 1.88 us  [the longest x2 1.19 us: body(): segs = (seg.reshape(length, 1), seg.reshape(1, length))]
    concatenate x20 -> x6, other arithmetic: 42.8 us -> 3.74 us  [the longest x1 2.21 us: body(): mix_local = jnp.concatenate([mix_weight, merge_weight], axis=1)]
    ppermute x78 -> x83, waiting for transfers between devices: 182 us -> 145 us  [hop(): lax.ppermute(v, 'seq', [(i, i ^ mask) for i in range(seq_n)]).reshape(shape)]
    dynamic_slice x35 -> x1, local copies, waits for them, and re-layouts: 34.9 us -> 0.6 us  [pick(): return lax.dynamic_index_in_dim(v, index, 0, keepdims=False)]
  transfers between devices with their start and end apart: 87 -> 92, of which waited for: 34 -> 38; matrix products, arithmetic and copies ran while one was open for 58% -> 6% of each run, Pallas kernels for 7% -> 51%
where the time goes in v2:
time: 717 us; the launch traced here: 708 us
  Pallas kernels  378 us (53%)
  waiting for transfers between devices  163 us (23%)
  starting transfers between devices  76.7 us (11%)
  local copies, waits for them, and re-layouts  38.5 us (5%)
  other arithmetic  34.3 us (5%)
  between operations  17.6 us (2%)
    pallas_call x34, Pallas kernels, call(): pl.pallas_call(kernel, grid_spec=spec, out_shape=[jax.ShapeDtypeStruct(s,...  378 us
    ppermute x83, waiting for transfers between devices, hop(): lax.ppermute(v, 'seq', [(i, i ^ mask) for i in range(seq_n)]).reshape(shape)  145 us
    ppermute x83, starting transfers between devices, hop(): lax.ppermute(v, 'seq', [(i, i ^ mask) for i in range(seq_n)]).reshape(shape)  74.4 us
    unnamed x153, local copies, waits for them, and re-layouts  18.7 us
    convert_element_type x5, other arithmetic, add_low(): return (a.astype(FULL) + b.astype(FULL)).astype(LOW)  16.1 us
    all_gather x3, waiting for transfers between devices, along(): return lax.all_gather(v, 'dp', axis=0)  14.6 us
  transfers between devices with their start and end apart: 92, of which 38 were waited for; matrix products, arithmetic and copies ran while one was open for 6% of the time, Pallas kernels for 51%

profile of v2, /device:TPU:0, one launch (start us, length us, event | category | flops | bytes accessed | tf_op | source)
XLA Modules:
  0.0 708.4 jit_solution(12830760432893434609)
XLA Ops:
  32.7 17.3 %collective-permute-done.4 = bf16[2,192,1600]{2,1,0:T(8,128)(2,1)S(1)} collective-permute-done((bf16[2,192,1600]{2,1,0:T(8,128)(2,1)S(1)}, bf16[2,192,1600]{2,1,0:T(8,128)(2,1)S(1)}, u32[]{:S(2)}, u32[]{:S(2)}) %collective-permute-start.4) | collective-permute-done | bytes 1228832 | tf_op jit(solution)/shard_map/ppermute | solution.py:692
  58.6 9.1 %collective-permute-done.10.refs_1_ = bf16[2,200,400]{2,1,0:T(8,128)(2,1)S(1)} collective-permute-done((bf16[2,200,400]{2,1,0:T(8,128)(2,1)}, bf16[2,200,400]{2,1,0:T(8,128)(2,1)S(1)}, u32[]{:S(2)}, u32[]{:S(2)}) %collective-permute-start.10) | collective-permute-done | bytes 320032 | tf_op jit(solution)/shard_map/ppermute | solution.py:692
  67.8 7.2 %collective-permute-done.12.refs_3_ = bf16[2,200,400]{2,1,0:T(8,128)(2,1)S(1)} collective-permute-done((bf16[2,200,400]{2,1,0:T(8,128)(2,1)}, bf16[2,200,400]{2,1,0:T(8,128)(2,1)S(1)}, u32[]{:S(2)}, u32[]{:S(2)}) %collective-permute-start.12) | collective-permute-done | bytes 320032 | tf_op jit(solution)/shard_map/ppermute | solution.py:692
  84.5 9.3 %collective-permute-done.6.refs_4_.refs_3_ = bf16[192,1600]{1,0:T(8,128)(2,1)S(1)} collective-permute-done((bf16[192,1600]{1,0:T(8,128)(2,1)S(1)}, bf16[192,1600]{1,0:T(8,128)(2,1)S(1)}, u32[]{:S(2)}, u32[]{:S(2)}) %collective-permute-start.6) | collective-permute-done | bytes 614432 | tf_op jit(solution)/shard_map/ppermute | solution.py:692
  105.5 8.5 %norm.1.refs_8_.refs_2_ = bf16[1536,1600]{1,0:T(8,128)(2,1)} custom-call(s32[5]{0:T(128)} %pad_add_fusion.at_ref, bf16[384,1600]{1,0:T(8,128)(2,1)} %copy-done.2, bf16[384,1600]{1,0:T(8,128)(2,1)} %bitcast.116, bf16[384,1600]{1,0:T(8,128)(2,1)} %bitcast.5.refs_5_.refs_2_, bf16[192,1600]{1,0:T(8,128)(2,1)} %copy-done.13, bf16[192,1600]{1,0:T(8,128)(2,1)} %copy-done.14, ...), custom_call_target="tpu_custom_call" | custom-call | flops 6144000 | bytes 2457600 | tf_op jit(solution)/shard_map/norm/pallas_call | solution.py:68
  119.1 9.3 %collective-permute-done.15.refs_6_ = bf16[200,1536]{1,0:T(8,128)(2,1)} collective-permute-done((bf16[200,1536]{1,0:T(8,128)(2,1)}, bf16[200,1536]{1,0:T(8,128)(2,1)}, u32[]{:S(2)}, u32[]{:S(2)}) %collective-permute-start.15) | collective-permute-done | bytes 614432 | tf_op jit(solution)/shard_map/ppermute | solution.py:692
  138.8 16.2 %mix.1 = (bf16[1536,1536]{1,0:T(8,128)(2,1)}, bf16[1600,1536]{1,0:T(8,128)(2,1)}) custom-call(s32[5]{0:T(128)} %pad_add_fusion.at_ref, bf16[200,1536]{1,0:T(8,128)(2,1)} %get-tuple-element.216.refs_6_.refs_0_, bf16[200,1536]{1,0:T(8,128)(2,1)} %copy-done.43, bf16[200,1536]{1,0:T(8,128)(2,1)} %collective-permute-done.13.refs_2_, ...), custom_call_target="tpu_custom_call" | custom-call | flops 1887436800 | bytes 4915200 | tf_op jit(solution)/shard_map/mix/pallas_call | solution.py:68
  159.4 18.8 %attend_forward.2 = (bf16[384,256]{1,0:T(8,128)(2,1)}, bf16[384,256]{1,0:T(8,128)(2,1)}, bf16[384,256]{1,0:T(8,128)(2,1)}, bf16[384,256]{1,0:T(8,128)(2,1)}) custom-call(s32[5]{0:T(128)} %pad_add_fusion.at_ref, bf16[1536,1536]{1,0:T(8,128)(2,1)} %get-tuple-element.225.refs_0_.refs_1_.refs_2_.refs_3_.refs_4_.refs_5_.refs_6_.refs_7_.refs_8_.refs_9_.refs_10_.refs_11_.refs_19_, ...), custom_call_target="tpu_custom_call" | custom-call | flops 528482304 | bytes 786432 | tf_op jit(solution)/shard_map/attend_forward/pallas_call | solution.py:68
  178.2 6.9 collective-permute-done.23
  186.6 14.6 %all-gather.11.cloned.1.call-done.refs_3_.refs_5_ = bf16[1600,896]{1,0:T(8,128)(2,1)} async-done(((bf16[400,896]{1,0:T(8,128)(2,1)}), bf16[1600,896]{1,0:T(8,128)(2,1)}) %all-gather.11.cloned.1.call-update) | async-done | bytes 2867216 | tf_op jit(solution)/shard_map/all_gather | solution.py:698
  215.8 15.0 %attend_forward.3 = (bf16[384,256]{1,0:T(8,128)(2,1)}, bf16[384,256]{1,0:T(8,128)(2,1)}, bf16[384,256]{1,0:T(8,128)(2,1)}, bf16[384,256]{1,0:T(8,128)(2,1)}) custom-call(s32[5]{0:T(128)} %pad_add_fusion.at_ref, bf16[1536,1536]{1,0:T(8,128)(2,1)} %get-tuple-element.225.refs_0_.refs_1_.refs_2_.refs_3_.refs_4_.refs_5_.refs_6_.refs_7_.refs_8_.refs_9_.refs_10_.refs_11_.refs_19_, ...), custom_call_target="tpu_custom_call" | custom-call | flops 528482304 | bytes 786432 | tf_op jit(solution)/shard_map/attend_forward/pallas_call | solution.py:68
  246.4 13.2 %merge_norm.1 = (f32[384,1600]{1,0:T(8,128)}, bf16[384,1600]{1,0:T(8,128)(2,1)}, bf16[1800,1600]{1,0:T(8,128)(2,1)}) custom-call(s32[5]{0:T(128)} %pad_add_fusion.at_ref, bf16[384,256]{1,0:T(8,128)(2,1)} %get-tuple-element.240.refs_14_.refs_0_, bf16[384,256]{1,0:T(8,128)(2,1)} %copy-done.29, bf16[384,256]{1,0:T(8,128)(2,1)} %copy-done.30, ...), custom_call_target="tpu_custom_call" | custom-call | flops 629145600 | bytes 6102016 | tf_op jit(solution)/shard_map/merge_norm/pallas_call | solution.py:68
  267.9 19.8 %feed.3 = (bf16[384,1792]{1,0:T(8,128)(2,1)}, bf16[384,1792]{1,0:T(8,128)(2,1)}, f32[8,1792]{1,0:T(8,128)}, bf16[384,1600]{1,0:T(8,128)(2,1)}, bf16[384,1600]{1,0:T(8,128)(2,1)}) custom-call(s32[5]{0:T(128)} %pad_add_fusion.at_ref, bf16[384,1600]{1,0:T(8,128)(2,1)} %get-tuple-element.250.refs_0_, bf16[384,1600]{1,0:T(8,128)(2,1)} %copy-done.4, ...), custom_call_target="tpu_custom_call" | custom-call | flops 2202009600 | bytes 4710400 | tf_op jit(solution)/shard_map/feed/pallas_call | solution.py:68
  297.3 34.0 %feed.4 = (bf16[768,1792]{1,0:T(8,128)(2,1)}, bf16[768,1792]{1,0:T(8,128)(2,1)}, f32[8,1792]{1,0:T(8,128)}, bf16[384,1600]{1,0:T(8,128)(2,1)}, bf16[384,1600]{1,...) custom-call(s32[5]{0:T(128)} %pad_add_fusion.at_ref, bf16[384,1600]{1,0:T(8,128)(2,1)} %bitcast.20.refs_0_.refs_1_, ...), custom_call_target="tpu_custom_call" | custom-call | flops 4404019200 | bytes 6553600 | tf_op jit(solution)/shard_map/feed/pallas_call | solution.py:68
  332.8 20.3 %feed.5 = (bf16[384,1792]{1,0:T(8,128)(2,1)}, bf16[384,1792]{1,0:T(8,128)(2,1)}, f32[8,1792]{1,0:T(8,128)}, bf16[192,1600]{1,0:T(8,128)(2,1)}, bf16[192,1600]{1,...) custom-call(s32[5]{0:T(128)} %pad_add_fusion.at_ref, bf16[192,1600]{1,0:T(8,128)(2,1)} %copy-done.17, ...), custom_call_target="tpu_custom_call" | custom-call | flops 2202009600 | bytes 4710400 | tf_op jit(solution)/shard_map/feed/pallas_call | solution.py:68
  355.2 18.8 %shrink_grad.1 = (bf16[1600,896]{1,0:T(8,128)(2,1)}, bf16[1600,896]{1,0:T(8,128)(2,1)}) custom-call(s32[5]{0:T(128)} %pad_add_fusion.at_ref, bf16[384,1600]{1,0:T(8,128)(2,1)} %copy-done.4, bf16[384,1600]{1,0:T(8,128)(2,1)} %bitcast.119, bf16[384,1600]{1,0:T(8,128)(2,1)} %bitcast.16.refs_3_.refs_2_, bf16[192,1600]{1,0:T(8,128)(2,1)} %copy-done.20, ...), custom_call_target="tpu_custom_call" | custom-call | flops 2202009600 | bytes 3891200 | tf_op jit(solution)/shard_map/shrink_grad/pallas_call | solution.py:68
  381.4 18.9 %expand_grad.1 = (bf16[896,1600]{1,0:T(8,128)(2,1)}, bf16[896,1600]{1,0:T(8,128)(2,1)}) custom-call(s32[5]{0:T(128)} %pad_add_fusion.at_ref, bf16[384,1600]{1,0:T(8,128)(2,1)} %get-tuple-element.250.refs_0_, bf16[384,1600]{1,0:T(8,128)(2,1)} %bitcast.20.refs_0_.refs_1_, bf16[384,1600]{1,0:T(8,128)(2,1)} %bitcast.21.refs_1_.refs_2_, ...), custom_call_target="tpu_custom_call" | custom-call | flops 2202009600 | bytes 3891200 | tf_op jit(solution)/shard_map/expand_grad/pallas_call | solution.py:68
  400.3 9.0 %collective-permute-done.47 = bf16[2,192,1600]{2,1,0:T(8,128)(2,1)} collective-permute-done((bf16[2,192,1600]{2,1,0:T(8,128)(2,1)}, bf16[2,192,1600]{2,1,0:T(8,128)(2,1)}, u32[]{:S(2)}, u32[]{:S(2)}) %collective-permute-start.47) | collective-permute-done | bytes 1228832 | tf_op jit(solution)/shard_map/ppermute | solution.py:692
  414.8 12.2 %second_back.1 = (f32[384,1600]{1,0:T(8,128)}, bf16[384,1600]{1,0:T(8,128)(2,1)}, f32[8,1600]{1,0:T(8,128)}, bf16[384,512]{1,0:T(8,128)(2,1)}, bf16[384,512]{1,0...) custom-call(s32[5]{0:T(128)} %pad_add_fusion.at_ref, bf16[384,1600]{1,0:T(8,128)(2,1)} %get-tuple-element.259.refs_0_, ...), custom_call_target="tpu_custom_call" | custom-call | flops 629145600 | bytes 5324032 | tf_op jit(solution)/shard_map/second_back/pallas_call | solution.py:68
  430.4 12.1 %merge_grad.1 = (bf16[4,200,1600]{2,1,0:T(8,128)(2,1)}, bf16[4,200,1600]{2,1,0:T(8,128)(2,1)}) custom-call(s32[5]{0:T(128)} %pad_add_fusion.at_ref, bf16[384,256]{1,0:T(8,128)(2,1)} %get-tuple-element.240.refs_14_.refs_0_, bf16[384,256]{1,0:T(8,128)(2,1)} %copy-done.29, bf16[384,256]{1,0:T(8,128)(2,1)} %copy-done.30, bf16[384,256]{1,0:T(8,128)(2,1)} %copy-done.31, ...), custom_call_target="tpu_custom_call" | custom-call | flops 629145600 | bytes 3260416 | tf_op jit(solution)/shard_map/merge_grad/pallas_call | solution.py:68
  455.4 16.3 %attend_backward.4.refs_18_.refs_0_ = bf16[3,1536,128]{2,1,0:T(8,128)(2,1)} custom-call(s32[5]{0:T(128)} %pad_add_fusion.at_ref, bf16[1536,1536]{1,0:T(8,128)(2,1)} %get-tuple-element.225.refs_0_.refs_1_.refs_2_.refs_3_.refs_4_.refs_5_.refs_6_.refs_7_.refs_8_.refs_9_.refs_10_.refs_11_.refs_19_, ...), custom_call_target="tpu_custom_call" | custom-call | flops 660602880 | bytes 786432 | tf_op jit(solution)/shard_map/attend_backward/pallas_call | solution.py:68
  480.4 16.6 %attend_backward.5.refs_1_ = bf16[3,1536,128]{2,1,0:T(8,128)(2,1)} custom-call(s32[5]{0:T(128)} %pad_add_fusion.at_ref, bf16[1536,1536]{1,0:T(8,128)(2,1)} %get-tuple-element.225.refs_0_.refs_1_.refs_2_.refs_3_.refs_4_.refs_5_.refs_6_.refs_7_.refs_8_.refs_9_.refs_10_.refs_11_.refs_19_, ...), custom_call_target="tpu_custom_call" | custom-call | flops 660602880 | bytes 786432 | tf_op jit(solution)/shard_map/attend_backward/pallas_call | solution.py:68
  497.0 10.6 %mix_grad.2 = (bf16[4,200,768]{2,1,0:T(8,128)(2,1)}, bf16[4,200,768]{2,1,0:T(8,128)(2,1)}, f32[8,768]{1,0:T(8,128)}) custom-call(s32[5]{0:T(128)} %pad_add_fusion.at_ref, bf16[3,1536,128]{2,1,0:T(8,128)(2,1)} %attend_backward.4.refs_18_.refs_0_, bf16[3,1536,128]{2,1,0:T(8,128)(2,1)} %attend_backward.5.refs_1_, bf16[1536,1600]{1,0:T(8,128)(2,1)} %norm.1.refs_8_.refs_2_), custom_call_target="tpu_custom_call" | custom-call | flops 943718400 | bytes 3686400 | tf_op jit(solution)/shard_map/mix_grad/pallas_call | solution.py:68
  516.1 16.4 %attend_backward.6.refs_18_.refs_0_.refs_2_ = bf16[3,1536,128]{2,1,0:T(8,128)(2,1)} custom-call(s32[5]{0:T(128)} %pad_add_fusion.at_ref, bf16[1536,1536]{1,0:T(8,128)(2,1)} %get-tuple-element.225.refs_0_.refs_1_.refs_2_.refs_3_.refs_4_.refs_5_.refs_6_.refs_7_.refs_8_.refs_9_.refs_10_.refs_11_.refs_19_, ...), custom_call_target="tpu_custom_call" | custom-call | flops 660602880 | bytes 786432 | tf_op jit(solution)/shard_map/attend_backward/pallas_call | solution.py:68
  532.5 10.1 %attend_backward.7.refs_5_.refs_1_.refs_3_ = bf16[3,1536,128]{2,1,0:T(8,128)(2,1)} custom-call(s32[5]{0:T(128)} %pad_add_fusion.at_ref, bf16[1536,1536]{1,0:T(8,128)(2,1)} %get-tuple-element.225.refs_0_.refs_1_.refs_2_.refs_3_.refs_4_.refs_5_.refs_6_.refs_7_.refs_8_.refs_9_.refs_10_.refs_11_.refs_19_, ...), custom_call_target="tpu_custom_call" | custom-call | flops 660602880 | bytes 786432 | tf_op jit(solution)/shard_map/attend_backward/pallas_call | solution.py:68
  552.1 10.6 %mix_grad.3 = (bf16[4,200,768]{2,1,0:T(8,128)(2,1)}, bf16[4,200,768]{2,1,0:T(8,128)(2,1)}, f32[8,768]{1,0:T(8,128)}) custom-call(s32[5]{0:T(128)} %pad_add_fusion.at_ref, bf16[3,1536,128]{2,1,0:T(8,128)(2,1)} %attend_backward.6.refs_18_.refs_0_.refs_2_, bf16[3,1536,128]{2,1,0:T(8,128)(2,1)} %attend_backward.7.refs_5_.refs_1_.refs_3_, ...), custom_call_target="tpu_custom_call" | custom-call | flops 943718400 | bytes 3686400 | tf_op jit(solution)/shard_map/mix_grad/pallas_call | solution.py:68
  568.1 8.4 %first_back.3 = (f32[8,1600]{1,0:T(8,128)}, bf16[192,1600]{1,0:T(8,128)(2,1)}, bf16[192,1600]{1,0:T(8,128)(2,1)}) custom-call(s32[5]{0:T(128)} %pad_add_fusion.at_ref, bf16[3,1536,128]{2,1,0:T(8,128)(2,1)} %attend_backward.4.refs_18_.refs_0_, bf16[3,1536,128]{2,1,0:T(8,128)(2,1)} %attend_backward.5.refs_1_, ...), custom_call_target="tpu_custom_call" | custom-call | flops 471859200 | bytes 1228800 | tf_op jit(solution)/shard_map/first_back/pallas_call | solution.py:68
  581.0 12.9 %first_back.4 = (f32[8,1600]{1,0:T(8,128)}, bf16[384,1600]{1,0:T(8,128)(2,1)}, bf16[384,1600]{1,0:T(8,128)(2,1)}) custom-call(s32[5]{0:T(128)} %pad_add_fusion.at_ref, bf16[3,1536,128]{2,1,0:T(8,128)(2,1)} %attend_backward.4.refs_18_.refs_0_, bf16[3,1536,128]{2,1,0:T(8,128)(2,1)} %attend_backward.5.refs_1_, ...), custom_call_target="tpu_custom_call" | custom-call | flops 943718400 | bytes 2457600 | tf_op jit(solution)/shard_map/first_back/pallas_call | solution.py:68
  594.0 8.4 %first_back.5 = (f32[8,1600]{1,0:T(8,128)}, bf16[384,1600]{1,0:T(8,128)(2,1)}) custom-call(s32[5]{0:T(128)} %pad_add_fusion.at_ref, bf16[3,1536,128]{2,1,0:T(8,128)(2,1)} %attend_backward.4.refs_18_.refs_0_, bf16[3,1536,128]{2,1,0:T(8,128)(2,1)} %attend_backward.5.refs_1_, bf16[3,1536,128]{2,1,0:T(8,128)(2,1)} %attend_backward.6.refs_18_.refs_0_.refs_2_, ...), custom_call_target="tpu_custom_call" | custom-call | flops 471859200 | bytes 1228800 | tf_op jit(solution)/shard_map/first_back/pallas_call | solution.py:68
  615.9 6.5 collective-permute-done.83.refs_6_
  644.4 9.8 %collective-permute-done.76.refs_2_ = bf16[2,200,400]{2,1,0:T(8,128)(2,1)S(1)} collective-permute-done((bf16[2,200,400]{2,1,0:T(8,128)(2,1)}, bf16[2,200,400]{2,1,0:T(8,128)(2,1)S(1)}, u32[]{:S(2)}, u32[]{:S(2)}) %collective-permute-start.76) | collective-permute-done | bytes 320032 | tf_op jit(solution)/shard_map/ppermute | solution.py:692
  682.2 7.3 %input_grad.1 = (f32[192,1600]{1,0:T(8,128)}, f32[192,1600]{1,0:T(8,128)}) custom-call(s32[5]{0:T(128)} %pad_add_fusion.at_ref, bf16[384,1600]{1,0:T(8,128)(2,1)} %get-tuple-element.354.refs_0_, bf16[384,1600]{1,0:T(8,128)(2,1)} %bitcast.125, bf16[384,1600]{1,0:T(8,128)(2,1)} %bitcast.126, f32[384,1600]{1,0:T(8,128)} %get-tuple-element.361.refs_3_, ...), custom_call_target="tpu_custom_call" | custom-call | bytes 2470400 | tf_op jit(solution)/shard_map/input_grad/pallas_call | solution.py:68
  (437 shorter events, 266.1 us)
Async XLA Ops:
  7.3 88.3 %all-gather.7.cloned.1.call-start = ((), (), s32[]{:S(2)}) async-start(), calls=%async_computation.8 | async-start | bytes 3328000 | tf_op jit(solution)/shard_map/all_gather | solution.py:698
  9.6 177.0 %all-gather.9.cloned.1.call-start = ((), (), s32[]{:S(2)}) async-start(), calls=%async_computation.9 | async-start | bytes 3727360 | tf_op jit(solution)/shard_map/all_gather | solution.py:698
  20.6 29.4 %collective-permute-start.4 = (bf16[2,192,1600]{2,1,0:T(8,128)(2,1)S(1)}, bf16[2,192,1600]{2,1,0:T(8,128)(2,1)S(1)}, u32[]{:S(2)}, u32[]{:S(2)}) collective-permute-start(bf16[2,192,1600]{2,1,0:T(8,128)(2,1)S(1)} %bitcast.105), channel_id=1, source_target_pairs={{0,2},{1,3},{2,0},{3,1},{4,6},{5,7},{6,4},{7,5},{8,10},{9,11},{10,... | collective-permute-start | bytes 3686408 | tf_op jit(solution)/shard_map/ppermute | solution.py:692
  79.7 121.5 %all-gather.11.cloned.1.call-start = ((), (), s32[]{:S(2)}) async-start(), calls=%async_computation.10 | async-start | bytes 3584000 | tf_op jit(solution)/shard_map/all_gather | solution.py:698
  80.8 495.8 %reduce-scatter.7.cloned.1.call-start = ((), (), s32[]{:S(2)}) async-start(), calls=%async_computation.5 | async-start | bytes 3584000 | tf_op jit(solution)/shard_map/reduce_scatter | solution.py:701
  155.0 30.2 %collective-permute-start.23 = (bf16[2,192,1600]{2,1,0:T(8,128)(2,1)S(1)}, bf16[2,192,1600]{2,1,0:T(8,128)(2,1)S(1)}, u32[]{:S(2)}, u32[]{:S(2)}) collective-permute-start(bf16[2,192,1600]{2,1,0:T(8,128)(2,1)S(1)} %bitcast.113), channel_id=1, source_target_pairs={{0,2},{1,3},{2,0},{3,1},{4,6},{5,7},{6,4},{7,5},{8,10},{9,11},{10,... | collective-permute-start | bytes 3686408 | tf_op jit(solution)/shard_map/ppermute | solution.py:692
  155.5 31.1 %collective-permute-start.24 = (bf16[2,192,1600]{2,1,0:T(8,128)(2,1)S(1)}, bf16[2,192,1600]{2,1,0:T(8,128)(2,1)}, u32[]{:S(2)}, u32[]{:S(2)}) collective-permute-start(bf16[2,192,1600]{2,1,0:T(8,128)(2,1)S(1)} %bitcast.114), channel_id=1, source_target_pairs={{0,4},{1,5},{2,6},{3,7},{4,0},{5,1},{6,2},{7,3},{8,12},{9,13},{10,... | collective-permute-start | bytes 3686408 | tf_op jit(solution)/shard_map/ppermute | solution.py:692
  156.9 46.2 %collective-permute-start.28 = (bf16[200,1600]{1,0:T(8,128)(2,1)}, bf16[200,1600]{1,0:T(8,128)(2,1)}, u32[]{:S(2)}, u32[]{:S(2)}) collective-permute-start(bf16[200,1600]{1,0:T(8,128)(2,1)} %collective-permute-done.20.refs_10_), channel_id=1, source_target_pairs={{0,4},{1,5},{2,6},{3,7},{4,0},{5,1},{6,2},{7,3},{8,12},{9,13},{10,... | collective-permute-start | bytes 1920008 | tf_op jit(solution)/shard_map/ppermute | solution.py:692
  186.6 79.8 %collective-permute-start.36 = (bf16[2,448,1600]{2,1,0:T(8,128)(2,1)}, bf16[2,448,1600]{2,1,0:T(8,128)(2,1)S(1)}, u32[]{:S(2)}, u32[]{:S(2)}) collective-permute-start(bf16[2,448,1600]{2,1,0:T(8,128)(2,1)} %bitcast.108), channel_id=1, source_target_pairs={{0,1},{1,0},{2,3},{3,2},{4,5},{5,4},{6,7},{7,6},{8,9},{9,8},{10,11... | collective-permute-start | bytes 8601608 | tf_op jit(solution)/shard_map/ppermute | solution.py:692
  201.2 65.1 %collective-permute-start.37 = (bf16[1600,896]{1,0:T(8,128)(2,1)}, bf16[1600,896]{1,0:T(8,128)(2,1)}, u32[]{:S(2)}, u32[]{:S(2)}) collective-permute-start(bf16[1600,896]{1,0:T(8,128)(2,1)} %all-gather.11.cloned.1.call-done.refs_3_.refs_5_), channel_id=1, source_target_pairs={{0,1},{1,0},{2,3},{3,2},{4,5},{5,4},{6,7},{7,6},{8,9},{9,8},{10,11... | collective-permute-start | bytes 8601608 | tf_op jit(solution)/shard_map/ppermute | solution.py:692
  201.2 29.6 %collective-permute-start.32 = (bf16[200,1600]{1,0:T(8,128)(2,1)}, bf16[200,1600]{1,0:T(8,128)(2,1)}, u32[]{:S(2)}, u32[]{:S(2)}) collective-permute-start(bf16[200,1600]{1,0:T(8,128)(2,1)} %get-tuple-element.224.refs_8_), channel_id=1, source_target_pairs={{0,1},{1,0},{2,3},{3,2},{4,5},{5,4},{6,7},{7,6},{8,9},{9,8},{10,11... | collective-permute-start | bytes 1920008 | tf_op jit(solution)/shard_map/ppermute | solution.py:692
  259.6 28.6 %collective-permute-start.38 = (bf16[2,192,1600]{2,1,0:T(8,128)(2,1)}, bf16[2,192,1600]{2,1,0:T(8,128)(2,1)}, u32[]{:S(2)}, u32[]{:S(2)}) collective-permute-start(bf16[2,192,1600]{2,1,0:T(8,128)(2,1)} %bitcast.121), channel_id=1, source_target_pairs={{0,2},{1,3},{2,0},{3,1},{4,6},{5,7},{6,4},{7,5},{8,10},{9,11},{10,... | collective-permute-start | bytes 3686408 | tf_op jit(solution)/shard_map/ppermute | solution.py:692
  293.3 38.1 %collective-permute-start.43 = (bf16[192,1600]{1,0:T(8,128)(2,1)}, bf16[192,1600]{1,0:T(8,128)(2,1)S(1)}, u32[]{:S(2)}, u32[]{:S(2)}) collective-permute-start(bf16[192,1600]{1,0:T(8,128)(2,1)} %slice.161), channel_id=1, source_target_pairs={{0,2},{1,3},{2,0},{3,1},{4,6},{5,7},{6,4},{7,5},{8,10},{9,11},{10,... | collective-permute-start | bytes 1843208 | tf_op jit(solution)/shard_map/ppermute | solution.py:692
  293.9 37.4 %collective-permute-start.42 = (bf16[192,1600]{1,0:T(8,128)(2,1)S(1)}, bf16[192,1600]{1,0:T(8,128)(2,1)S(1)}, u32[]{:S(2)}, u32[]{:S(2)}) collective-permute-start(bf16[192,1600]{1,0:T(8,128)(2,1)S(1)} %copy-done.42), channel_id=1, source_target_pairs={{0,4},{1,5},{2,6},{3,7},{4,0},{5,1},{6,2},{7,3},{8,12},{9,13},{10,... | collective-permute-start | bytes 1843208 | tf_op jit(solution)/shard_map/ppermute | solution.py:692
  295.3 36.1 %collective-permute-start.40 = (bf16[192,1600]{1,0:T(8,128)(2,1)}, bf16[192,1600]{1,0:T(8,128)(2,1)S(1)}, u32[]{:S(2)}, u32[]{:S(2)}) collective-permute-start(bf16[192,1600]{1,0:T(8,128)(2,1)} %slice.158), channel_id=1, source_target_pairs={{0,4},{1,5},{2,6},{3,7},{4,0},{5,1},{6,2},{7,3},{8,12},{9,13},{10,... | collective-permute-start | bytes 1843208 | tf_op jit(solution)/shard_map/ppermute | solution.py:692
  295.9 35.5 %collective-permute-start.41 = (bf16[192,1600]{1,0:T(8,128)(2,1)}, bf16[192,1600]{1,0:T(8,128)(2,1)S(1)}, u32[]{:S(2)}, u32[]{:S(2)}) collective-permute-start(bf16[192,1600]{1,0:T(8,128)(2,1)} %slice.159), channel_id=1, source_target_pairs={{0,2},{1,3},{2,0},{3,1},{4,6},{5,7},{6,4},{7,5},{8,10},{9,11},{10,... | collective-permute-start | bytes 1843208 | tf_op jit(solution)/shard_map/ppermute | solution.py:692
  374.0 36.4 %collective-permute-start.46 = (bf16[1600,896]{1,0:T(8,128)(2,1)}, bf16[1600,896]{1,0:T(8,128)(2,1)}, u32[]{:S(2)}, u32[]{:S(2)}) collective-permute-start(bf16[1600,896]{1,0:T(8,128)(2,1)} %get-tuple-element.290), channel_id=1, source_target_pairs={{0,1},{1,0},{2,3},{3,2},{4,5},{5,4},{6,7},{7,6},{8,9},{9,8},{10,11... | collective-permute-start | bytes 8601608 | tf_op jit(solution)/shard_map/ppermute | solution.py:692
  379.4 29.8 %collective-permute-start.47 = (bf16[2,192,1600]{2,1,0:T(8,128)(2,1)}, bf16[2,192,1600]{2,1,0:T(8,128)(2,1)}, u32[]{:S(2)}, u32[]{:S(2)}) collective-permute-start(bf16[2,192,1600]{2,1,0:T(8,128)(2,1)} %bitcast.145), channel_id=1, source_target_pairs={{0,2},{1,3},{2,0},{3,1},{4,6},{5,7},{6,4},{7,5},{8,10},{9,11},{10,... | collective-permute-start | bytes 3686408 | tf_op jit(solution)/shard_map/ppermute | solution.py:692
  380.9 29.6 %collective-permute-start.48 = (bf16[2,192,1600]{2,1,0:T(8,128)(2,1)}, bf16[2,192,1600]{2,1,0:T(8,128)(2,1)}, u32[]{:S(2)}, u32[]{:S(2)}) collective-permute-start(bf16[2,192,1600]{2,1,0:T(8,128)(2,1)} %bitcast.144), channel_id=1, source_target_pairs={{0,4},{1,5},{2,6},{3,7},{4,0},{5,1},{6,2},{7,3},{8,12},{9,13},{10,... | collective-permute-start | bytes 3686408 | tf_op jit(solution)/shard_map/ppermute | solution.py:692
  414.6 161.9 %reduce-scatter.5.cloned.1.call-start = ((), (), s32[]{:S(2)}) async-start(), calls=%async_computation.4 | async-start | bytes 3727360 | tf_op jit(solution)/shard_map/reduce_scatter | solution.py:701
  414.7 32.7 %collective-permute-start.49 = (bf16[2,448,1600]{2,1,0:T(8,128)(2,1)}, bf16[2,448,1600]{2,1,0:T(8,128)(2,1)}, u32[]{:S(2)}, u32[]{:S(2)}) collective-permute-start(bf16[2,448,1600]{2,1,0:T(8,128)(2,1)} %bitcast.139), channel_id=1, source_target_pairs={{0,1},{1,0},{2,3},{3,2},{4,5},{5,4},{6,7},{7,6},{8,9},{9,8},{10,11... | collective-permute-start | bytes 8601608 | tf_op jit(solution)/shard_map/ppermute | solution.py:692
  452.9 237.9 %reduce-scatter.11.cloned.1.call-start = ((), (), s32[]{:S(2)}) async-start(), calls=%async_computation.7 | async-start | bytes 1024000 | tf_op jit(solution)/shard_map/reduce_scatter | solution.py:701
  477.2 30.4 %collective-permute-start.56 = (bf16[2,192,1600]{2,1,0:T(8,128)(2,1)}, bf16[2,192,1600]{2,1,0:T(8,128)(2,1)}, u32[]{:S(2)}, u32[]{:S(2)}) collective-permute-start(bf16[2,192,1600]{2,1,0:T(8,128)(2,1)} %bitcast.143), channel_id=1, source_target_pairs={{0,2},{1,3},{2,0},{3,1},{4,6},{5,7},{6,4},{7,5},{8,10},{9,11},{10,... | collective-permute-start | bytes 3686408 | tf_op jit(solution)/shard_map/ppermute | solution.py:692
  478.2 29.9 %collective-permute-start.57 = (bf16[2,192,1600]{2,1,0:T(8,128)(2,1)}, bf16[2,192,1600]{2,1,0:T(8,128)(2,1)}, u32[]{:S(2)}, u32[]{:S(2)}) collective-permute-start(bf16[2,192,1600]{2,1,0:T(8,128)(2,1)} %bitcast.142), channel_id=1, source_target_pairs={{0,4},{1,5},{2,6},{3,7},{4,0},{5,1},{6,2},{7,3},{8,12},{9,13},{10,... | collective-permute-start | bytes 3686408 | tf_op jit(solution)/shard_map/ppermute | solution.py:692
  508.1 38.1 %collective-permute-start.62 = (bf16[4,200,768]{2,1,0:T(8,128)(2,1)}, bf16[4,200,768]{2,1,0:T(8,128)(2,1)}, u32[]{:S(2)}, u32[]{:S(2)}) collective-permute-start(bf16[4,200,768]{2,1,0:T(8,128)(2,1)} %get-tuple-element.332.refs_18_), channel_id=1, source_target_pairs={{0,1},{1,0},{2,3},{3,2},{4,5},{5,4},{6,7},{7,6},{8,9},{9,8},{10,11... | collective-permute-start | bytes 3686408 | tf_op jit(solution)/shard_map/ppermute | solution.py:692
  511.3 31.4 %collective-permute-start.60 = (bf16[200,1600]{1,0:T(8,128)(2,1)}, bf16[200,1600]{1,0:T(8,128)(2,1)S(1)}, u32[]{:S(2)}, u32[]{:S(2)}) collective-permute-start(bf16[200,1600]{1,0:T(8,128)(2,1)} %get-tuple-element.337), channel_id=1, source_target_pairs={{0,6},{1,7},{2,4},{3,5},{4,2},{5,3},{6,0},{7,1},{8,14},{9,15},{10,... | collective-permute-start | bytes 1920008 | tf_op jit(solution)/shard_map/ppermute | solution.py:692
  513.0 31.0 %collective-permute-start.59 = (bf16[200,1600]{1,0:T(8,128)(2,1)}, bf16[200,1600]{1,0:T(8,128)(2,1)}, u32[]{:S(2)}, u32[]{:S(2)}) collective-permute-start(bf16[200,1600]{1,0:T(8,128)(2,1)} %get-tuple-element.336), channel_id=1, source_target_pairs={{0,4},{1,5},{2,6},{3,7},{4,0},{5,1},{6,2},{7,3},{8,12},{9,13},{10,... | collective-permute-start | bytes 1920008 | tf_op jit(solution)/shard_map/ppermute | solution.py:692
  513.7 30.4 %collective-permute-start.58 = (bf16[200,1600]{1,0:T(8,128)(2,1)}, bf16[200,1600]{1,0:T(8,128)(2,1)}, u32[]{:S(2)}, u32[]{:S(2)}) collective-permute-start(bf16[200,1600]{1,0:T(8,128)(2,1)} %get-tuple-element.335), channel_id=1, source_target_pairs={{0,2},{1,3},{2,0},{3,1},{4,6},{5,7},{6,4},{7,5},{8,10},{9,11},{10,... | collective-permute-start | bytes 1920008 | tf_op jit(solution)/shard_map/ppermute | solution.py:692
  565.9 37.6 %collective-permute-start.81 = (bf16[4,200,768]{2,1,0:T(8,128)(2,1)}, bf16[4,200,768]{2,1,0:T(8,128)(2,1)S(1)}, u32[]{:S(2)}, u32[]{:S(2)}) collective-permute-start(bf16[4,200,768]{2,1,0:T(8,128)(2,1)} %get-tuple-element.345.refs_7_), channel_id=1, source_target_pairs={{0,1},{1,0},{2,3},{3,2},{4,5},{5,4},{6,7},{7,6},{8,9},{9,8},{10,11... | collective-permute-start | bytes 3686408 | tf_op jit(solution)/shard_map/ppermute | solution.py:692
  568.1 130.9 %reduce-scatter.9.cloned.1.call-start = ((), (), s32[]{:S(2)}) async-start(), calls=%async_computation.6 | async-start | bytes 2560000 | tf_op jit(solution)/shard_map/reduce_scatter | solution.py:701
  642.2 37.9 %collective-permute-start.68 = (bf16[2,192,1600]{2,1,0:T(8,128)(2,1)}, bf16[2,192,1600]{2,1,0:T(8,128)(2,1)S(1)}, u32[]{:S(2)}, u32[]{:S(2)}) collective-permute-start(bf16[2,192,1600]{2,1,0:T(8,128)(2,1)} %bitcast.141), channel_id=1, source_target_pairs={{0,2},{1,3},{2,0},{3,1},{4,6},{5,7},{6,4},{7,5},{8,10},{9,11},{10,... | collective-permute-start | bytes 3686408 | tf_op jit(solution)/shard_map/ppermute | solution.py:692
  643.3 37.8 %collective-permute-start.69 = (bf16[2,192,1600]{2,1,0:T(8,128)(2,1)}, bf16[2,192,1600]{2,1,0:T(8,128)(2,1)S(1)}, u32[]{:S(2)}, u32[]{:S(2)}) collective-permute-start(bf16[2,192,1600]{2,1,0:T(8,128)(2,1)} %bitcast.140), channel_id=1, source_target_pairs={{0,4},{1,5},{2,6},{3,7},{4,0},{5,1},{6,2},{7,3},{8,12},{9,13},{10,... | collective-permute-start | bytes 3686408 | tf_op jit(solution)/shard_map/ppermute | solution.py:692
  (134 other events, 1419.3 us)
Sparse Core Ops, SparseCore 0:
  10.3 58.1 all-gather.6
  79.8 61.4 all-gather.8
  143.5 57.6 all-gather.10
  414.8 52.9 reduce-scatter.6
  469.9 57.5 reduce-scatter.4
  568.2 21.1 reduce-scatter.10
  627.9 41.0 reduce-scatter.8

commit v3 on v2

--- a/solution.py
+++ b/solution.py
@@ -11,6 +11,8 @@
 COST = 0.25
 LANES = 128
 CHUNK = 256
+QUERY_ROWS = 384
+KEY_ROWS = 384
 LOW = jnp.bfloat16
 FULL = jnp.float32
 VMEM_BYTES = 60 * 1024 * 1024
@@ -97,19 +99,24 @@
         low += size
 
 
+def half_sum(refs, half, rows):
+    parts = []
+    for i, ref in enumerate(refs):
+        if ref.shape[0] > rows:
+            parts.append(ref[half * rows : (half + 1) * rows, :])
+        elif (i + 1) % 2 == half:
+            parts.append(ref[...])
+    return functools.reduce(jnp.add, [v.astype(FULL) for v in parts])
+
+
 def pair_rows(refs, core, rows, buf):
     for half in range(2):
-        here = slice(half * rows, (half + 1) * rows)
-        value = functools.reduce(jnp.add, [ref[here, :].astype(FULL) for ref in refs])
-        buf[row_slot(half, core, rows), :] = value.astype(buf.dtype)
+        buf[row_slot(half, core, rows), :] = half_sum(refs, half, rows).astype(buf.dtype)
 
 
 def fold_kernel(at_ref, x_ref, y_ref, far0_ref, far1_ref, xo_ref, yo_ref):
-    rows = far0_ref.shape[0]
-    xo_ref[:rows, :] = x_ref[:rows, :]
-    xo_ref[rows:, :] = (x_ref[rows:, :].astype(FULL) + far1_ref[...].astype(FULL)).astype(LOW)
-    yo_ref[:rows, :] = (y_ref[:rows, :].astype(FULL) + far0_ref[...].astype(FULL)).astype(LOW)
-    yo_ref[rows:, :] = y_ref[rows:, :]
+    xo_ref[...] = (x_ref[...].astype(FULL) + far1_ref[...].astype(FULL)).astype(LOW)
+    yo_ref[...] = (y_ref[...].astype(FULL) + far0_ref[...].astype(FULL)).astype(LOW)
 
 
 def place_rows(place, refs, wide, out):
@@ -253,13 +260,11 @@
 
 
 def join_mix_kernel(at_ref, *refs, teams, dp_n, each, span, starts, width):
-    part_refs, out_ref, whole, flat = refs[: 2 * teams], *refs[2 * teams :]
+    part_refs, out_ref, whole, flat = refs[:teams], *refs[teams:]
     team = at_ref[0] // 2
-    share, half = width // teams, span // 2
-    for i, ref in enumerate(part_refs):
-        for m in range(3):
-            low = m * span + (i // teams) * half
-            whole[team ^ (i % teams), :, low : low + half] = ref[:, m * half : (m + 1) * half]
+    share = width // teams
+    for k, ref in enumerate(part_refs):
+        whole[team ^ k] = ref[...]
     for m in range(3):
         for t in range(teams):
             low = m * span + share * t - starts[t]
@@ -269,12 +274,21 @@
         out_ref[d] = flat[:, d * each : (d + 1) * each]
 
 
+def add_parts_kernel(at_ref, mine_ref, got_ref, *out_refs):
+    team = at_ref[0] // 2
+    for k, ref in enumerate(out_refs):
+        total = mine_ref[team ^ k].astype(FULL) + got_ref[team ^ k].astype(FULL)
+        ref[...] = total.astype(LOW)
+
+
 def norm_kernel(sizes, rows, at_ref, *refs):
     count = len(sizes)
-    vec_ref, first_ref, buf = refs[count:]
+    vec_ref, first_ref, turned_ref, buf = refs[count:]
     load_pair(pl.program_id(0), sizes, refs[:count], buf, at_ref[0] % 2, rows)
     normal, _ = norm_parts(buf[...].astype(FULL))
-    first_ref[...] = (normal * vec_ref[0:1, :] + vec_ref[1:2, :]).astype(LOW)
+    first = (normal * vec_ref[0:1, :] + vec_ref[1:2, :]).astype(LOW)
+    first_ref[...] = first
+    turned_ref[...] = first.T
 
 
 def mix_kernel(parts, at_ref, *refs):
@@ -288,26 +302,25 @@
     mixed_ref[...] = (mixed * bias_ref[1:2, :]).astype(LOW)
 
 
-def softmax_pieces(query, keys, seg_col, seg_row, index, block):
-    scores = []
-    for j in range(index + 1):
-        piece = dot_nt(query, keys[j])
-        seen = seg_col == seg_row[:, j * block : (j + 1) * block]
-        if j == index:
-            row_id = lax.broadcasted_iota(jnp.int32, (block, block), 0)
-            col_id = lax.broadcasted_iota(jnp.int32, (block, block), 1)
-            seen = seen & (col_id <= row_id)
-        scores.append(jnp.where(seen, piece, -1e30))
-    top = functools.reduce(jnp.maximum, [jnp.max(p, axis=1, keepdims=True) for p in scores])
-    expo = [jnp.exp(p - top) for p in scores]
-    total = functools.reduce(jnp.add, [jnp.sum(p, axis=1, keepdims=True) for p in expo])
-    return expo, total
+def causal_chunks(length, begin):
+    stop = begin + QUERY_ROWS
+    return [(low, min(low + KEY_ROWS, stop)) for low in range(0, stop, KEY_ROWS)]
+
+
+def visible_scores(query, key, begin, low, col_ref, row_ref):
+    scores = dot_nt(query, key)
+    rows, cols = scores.shape
+    seen = col_ref[begin : begin + rows, :] == row_ref[:, low : low + cols]
+    if low + cols > begin:
+        row_id = lax.broadcasted_iota(jnp.int32, (rows, cols), 0) + begin
+        col_id = lax.broadcasted_iota(jnp.int32, (rows, cols), 1) + low
+        seen = seen & (col_id <= row_id)
+    return jnp.where(seen, scores, -1e30)
 
 
 def attend_forward_kernel(count, block, dim, heads, base, at_ref, *refs):
-    q_refs, k_refs, v_refs = refs[:count], refs[count : 2 * count], refs[2 * count : 3 * count]
-    col_ref, row_ref = refs[3 * count : 3 * count + 2]
-    out_refs = refs[3 * count + 2 :]
+    q_ref, k_ref, v_ref, col_ref, row_ref = refs[:5]
+    out_refs, log_ref = refs[5:-1], refs[-1]
     pair = pl.program_id(0) + base
     team = at_ref[0] // 2
     for ref in out_refs:
@@ -317,33 +330,48 @@
         @pl.when(pair * (LANES // dim) + sub < heads)
         def _():
             lanes = slice(sub * dim, (sub + 1) * dim)
-            keys = [r[:, lanes] for r in k_refs]
-            values = [r[:, lanes] for r in v_refs]
-            for i in range(count):
-                rows = slice(i * block, (i + 1) * block)
-                query = q_refs[i][:, lanes]
-                expo, total = softmax_pieces(
-                    query, keys, col_ref[rows, :], row_ref[...], i, block
+            for begin in range(0, count * block, QUERY_ROWS):
+                rows = slice(begin, begin + QUERY_ROWS)
+                query = q_ref[rows, lanes]
+                chunks = causal_chunks(count * block, begin)
+                scores = [
+                    visible_scores(
+                        query, k_ref[low:high, lanes], begin, low, col_ref, row_ref
+                    )
+                    for low, high in chunks
+                ]
+                top = functools.reduce(
+                    jnp.maximum, [jnp.max(p, axis=1, keepdims=True) for p in scores]
+                )
+                expo = [jnp.exp(p - top) for p in scores]
+                total = functools.reduce(
+                    jnp.add, [jnp.sum(p, axis=1, keepdims=True) for p in expo]
                 )
                 mixed = functools.reduce(
-                    jnp.add, [dot_nn(e.astype(LOW), v) for e, v in zip(expo, values)]
+                    jnp.add,
+                    [
+                        dot_nn(e.astype(LOW), v_ref[low:high, lanes])
+                        for e, (low, high) in zip(expo, chunks)
+                    ],
                 )
                 mixed = (mixed / total).astype(LOW)
+                log_ref[rows, lanes] = jnp.broadcast_to(top + jnp.log(total), (QUERY_ROWS, dim))
+                place = slice(begin % block, begin % block + QUERY_ROWS)
                 for k, ref in enumerate(out_refs):
 
-                    @pl.when((team ^ i) == k)
+                    @pl.when((team ^ (begin // block)) == k)
                     def _():
-                        ref[:, lanes] = mixed
+                        ref[place, lanes] = mixed
 
 
 def attend_backward_kernel(count, block, dim, heads, share, base, at_ref, *refs):
-    q_refs, k_refs, v_refs = refs[:count], refs[count : 2 * count], refs[2 * count : 3 * count]
-    g_refs = refs[3 * count : 4 * count]
-    col_ref, row_ref, d_ref, acc_k, acc_v, grads = refs[4 * count :]
+    q_ref, k_ref, v_ref, *g_refs = refs[: 3 + count]
+    col_ref, row_ref, log_ref, d_ref, acc_k, acc_v, grads, logs = refs[3 + count :]
     pair = pl.program_id(0) + base
     team = at_ref[0] // 2
     scale = dim**-0.5
     d_ref[...] = jnp.zeros_like(d_ref)
+    logs[...] = log_ref[...].T
     for k, ref in enumerate(g_refs):
         grads[pl.ds(pl.multiple_of((team ^ k) * block, block), block), :] = ref[...]
     for sub in range(LANES // dim):
@@ -355,31 +383,33 @@
             column = column + at_ref[1 + team] + pair * LANES + sub * dim
             owned = (column >= share * team) & (column < share * (team + 1))
             owned = jnp.where(owned, 1.0, 0.0)
-            keys = [r[:, lanes] for r in k_refs]
-            values = [r[:, lanes] for r in v_refs]
             acc_k[...] = jnp.zeros_like(acc_k)
             acc_v[...] = jnp.zeros_like(acc_v)
-            for i in range(count):
-                rows = slice(i * block, (i + 1) * block)
-                query = q_refs[i][:, lanes]
+            for begin in range(0, count * block, QUERY_ROWS):
+                rows = slice(begin, begin + QUERY_ROWS)
+                query = q_ref[rows, lanes]
                 grad = grads[rows, lanes]
-                expo, total = softmax_pieces(
-                    query, keys, col_ref[rows, :], row_ref[...], i, block
+                log_total = logs[sub * dim : sub * dim + 1, rows]
+                chunks = causal_chunks(count * block, begin)
+                probs, d_weights = [], []
+                for low, high in chunks:
+                    scores = dot_nt(k_ref[low:high, lanes], query)
+                    seen = col_ref[low:high, :] == row_ref[:, rows]
+                    if high > begin:
+                        key_id = lax.broadcasted_iota(jnp.int32, scores.shape, 0) + low
+                        query_id = lax.broadcasted_iota(jnp.int32, scores.shape, 1) + begin
+                        seen = seen & (key_id <= query_id)
+                    probs.append(jnp.exp(jnp.where(seen, scores, -1e30) - log_total))
+                    d_weights.append(dot_nt(v_ref[low:high, lanes], grad))
+                delta = functools.reduce(
+                    jnp.add, [total_rows(p * d) for p, d in zip(probs, d_weights)]
                 )
-                inverse = 1.0 / total
-                probs = [e * inverse for e in expo]
-                d_weights = [dot_nt(grad, v) for v in values[: i + 1]]
-                delta = functools.reduce(
-                    jnp.add,
-                    [jnp.sum(p * d, axis=1, keepdims=True) for p, d in zip(probs, d_weights)],
-                )
-                d_query = jnp.zeros((block, dim), FULL)
-                for j in range(i + 1):
-                    cols = slice(j * block, (j + 1) * block)
-                    d_scores = (probs[j] * (d_weights[j] - delta)).astype(LOW)
-                    d_query = d_query + dot_nn(d_scores, keys[j])
-                    acc_k[cols, :] += dot_tn(d_scores, query)
-                    acc_v[cols, :] += dot_tn(probs[j].astype(LOW), grad)
+                d_query = jnp.zeros((QUERY_ROWS, dim), FULL)
+                for prob, d_weight, (low, high) in zip(probs, d_weights, chunks):
+                    d_scores = (prob * (d_weight - delta)).astype(LOW)
+                    d_query = d_query + dot_tn(d_scores, k_ref[low:high, lanes])
+                    acc_k[low:high, :] += dot_nn(d_scores, query)
+                    acc_v[low:high, :] += dot_nn(prob.astype(LOW), grad)
                 d_ref[0, rows, lanes] = (d_query * scale * owned).astype(LOW)
             d_ref[1, :, lanes] = (acc_k[...] * owned).astype(LOW)
             d_ref[2, :, lanes] = (acc_v[...] * owned).astype(LOW)
@@ -408,8 +438,8 @@
     s_ref[rows:, :] = buf[row_slot(1, core, rows), :]
 
 
-def feed_kernel(sizes, at_ref, *refs):
-    pieces = len(sizes)
+def feed_kernel(sizes, out_sizes, at_ref, *refs):
+    pieces, count = len(sizes), len(out_sizes)
     lows = [sum(sizes[:i]) for i in range(pieces)]
     sec_refs, g_refs = refs[:pieces], refs[pieces : 2 * pieces]
     weights, (bias_ref, act_ref, dpre_ref, sum_ref) = (
@@ -417,8 +447,8 @@
         refs[2 * pieces + 4 : 2 * pieces + 8],
     )
     rest = refs[2 * pieces + 8 :]
-    ds_refs, out_refs = rest[:pieces], rest[pieces : 2 * pieces]
-    sec, g, acc_s, acc_o, e_held, s_held, sems = rest[2 * pieces :]
+    ds_refs, out_refs = rest[:count], rest[count : 2 * count]
+    sec, g, acc_s, acc_o, e_held, s_held, sems = rest[2 * count :]
     step = pl.program_id(0)
     copies = [
         pltpu.make_async_copy(ref, held.at[i // 2], sems.at[i])
@@ -464,8 +494,8 @@
 
     @pl.when(step == 1)
     def _():
-        for i in range(pieces):
-            here = slice(lows[i], lows[i] + sizes[i])
+        for i in range(count):
+            here = slice(sum(out_sizes[:i]), sum(out_sizes[: i + 1]))
             ds_refs[i][...] = (acc_s[here, :] + part_s[here, :]).astype(LOW)
             out_refs[i][...] = (acc_o[here, :] + part_o[here, :]).astype(LOW)
 
@@ -566,21 +596,22 @@
     split_cores(at_ref[0] % 2, acc, mine_ref, give_ref)
 
 
-def first_back_kernel(sizes, rows, span, at_ref, *refs):
-    count = len(sizes)
-    sides = span // LANES
+def first_back_kernel(sizes, out_sizes, rows, span, at_ref, *refs):
+    count, out_count = len(sizes), len(out_sizes)
+    sides = 2
     d_refs, x_refs, refs = refs[:sides], refs[sides : sides + count], refs[sides + count :]
     mix_ref, sum_ref = refs[:2]
-    out_refs = refs[2 : 2 + count]
-    buf, low, joined = refs[2 + count :]
+    out_refs = refs[2 : 2 + out_count]
+    buf, low, joined = refs[2 + out_count :]
     step = pl.program_id(0)
     core = at_ref[0] % 2
     load_pair(step, sizes, x_refs, buf, core, rows)
     normal, _ = norm_parts(buf[...].astype(FULL))
     for m in range(3):
         for i, d_ref in enumerate(d_refs):
-            begin = m * span + i * LANES
-            joined[:, begin : begin + LANES] = d_ref[m]
+            n = span // sides
+            begin = m * span + i * n
+            joined[:, begin : begin + n] = d_ref[m]
     d_first = dot_nt(joined[...], mix_ref[...])
 
     @pl.when(step == 0)
@@ -591,7 +622,7 @@
     sum_ref[1:2, :] += total_rows(d_first)
     low[...] = d_first.astype(LOW)
     begin = 0
-    for size, ref in zip(sizes, out_refs):
+    for size, ref in zip(out_sizes, out_refs):
         for i in range(size // rows):
             r = begin // rows + i
 
@@ -603,16 +634,12 @@
 
 
 def mix_grad_kernel(at_ref, *refs):
-    first_ref, mine_ref, give_ref, sum_ref, first_t, held, d = refs[-7:]
-
-    @pl.when(pl.program_id(0) == 0)
-    def _():
-        first_t[...] = first_ref[...].T
-
-    for i, ref in enumerate(refs[:-7]):
-        d[:, i * LANES : (i + 1) * LANES] = ref[0]
+    turned_ref, mine_ref, give_ref, sum_ref, held, d = refs[-6:]
+    for i, ref in enumerate(refs[:-6]):
+        n = ref.shape[2]
+        d[:, i * n : (i + 1) * n] = ref[0]
     sum_ref[...] = jnp.broadcast_to(total_rows(d[...].astype(FULL)), sum_ref.shape)
-    held[...] = dot_nn(first_t[...], d[...])
+    held[...] = dot_nn(turned_ref[...], d[...])
     split_cores(at_ref[0] % 2, held, mine_ref, give_ref)
 
 
@@ -620,19 +647,16 @@
     hid_ref, vec_ref, o0_ref, o1_ref = refs[terms:]
     core = at_ref[0] % 2
     for half, ref in enumerate((o0_ref, o1_ref)):
-        here = slice(half * rows, (half + 1) * rows)
         value = hid_ref[row_slot(half, core, rows), :] + vec_ref[7:8, :]
-        value = functools.reduce(jnp.add, [t[here, :].astype(FULL) for t in refs[:terms]], value)
-        ref[...] = value.astype(LOW)
+        ref[...] = (value + half_sum(refs[:terms], half, rows)).astype(LOW)
 
 
 def input_grad_kernel(at_ref, *refs, rows, terms):
     dh_ref, x_ref, vec_ref, o0_ref, o1_ref = refs[terms:]
     core = at_ref[0] % 2
     for half, ref in enumerate((o0_ref, o1_ref)):
-        here = slice(half * rows, (half + 1) * rows)
-        d_first = functools.reduce(jnp.add, [t[here, :].astype(FULL) for t in refs[:terms]])
-        normal, inverse = norm_parts(x_ref[here, :].astype(FULL))
+        d_first = half_sum(refs[:terms], half, rows)
+        normal, inverse = norm_parts(x_ref[half * rows : (half + 1) * rows, :].astype(FULL))
         back = norm_back(d_first, vec_ref[0:1, :], normal, inverse)
         ref[...] = dh_ref[row_slot(half, core, rows), :] + back
 
@@ -728,16 +752,24 @@
     def add_low(a, b):
         return (a.astype(FULL) + b.astype(FULL)).astype(LOW)
 
+    def reduce_early(p):
+        return [hop(p[1], 2), hop(p[4], 4)] if teams == 4 else exchange(p)[1:]
+
     def reduce_far(p):
-        return [hop(p[3], 2), hop(p[4], 4)] if teams == 4 else []
-
-    def reduce_near(p, far):
+        return [hop(p[5], 2), hop(p[6], 4)] if teams == 4 else []
+
+    def reduce_late(p, far, after=()):
+        if teams != 4:
+            return [], ()
+        folded = simple(
+            fold_kernel, "fold", (p[2], p[3], *far), [((rows, width), LOW)] * 2, after=after
+        )
+        return [hop(folded[0], 2), hop(folded[1], 4)], folded
+
+    def reduce_terms(p, early, late):
         if teams == 4:
-            folded = simple(
-                fold_kernel, "fold", (p[1], p[2], *far), [((own_rows, width), LOW)] * 2
-            )
-            return [hop(folded[0], 2), hop(folded[1], 4)]
-        return exchange(p)[1:]
+            return [p[0], early[0], late[0], late[1], early[1]]
+        return [p[0], *early]
 
     def exchange(parts):
         return [parts[0]] + [hop(parts[k], 2 * k) for k in range(1, teams)]
@@ -761,14 +793,14 @@
             )
         return cur
 
-    def reduce_small(v):
+    def reduce_small(v, *others):
         for b in reversed(range(bits + 1)):
             half_n = v.shape[0] // 2
             bit = (place >> b) & 1
             mine = jnp.where(bit == 0, v[:half_n], v[half_n:])
             give = jnp.where(bit == 0, v[half_n:], v[:half_n])
             v = mine + hop(give, 1 << b)
-        v = v[0]
+        v = tie(v[0], *others)
         for b in range(dp_n.bit_length() - 1):
             v = v + lax.ppermute(v, "dp", [(i, i ^ (1 << b)) for i in range(dp_n)])
         return v
@@ -806,10 +838,7 @@
         shrink_bias,
         expand_bias,
     )
-    packed = gather_small(jnp.concatenate(small))
-    vec = packed[:, : 8 * feats].reshape(seq_n, 8, feats).transpose(1, 0, 2)
-    vec = vec.reshape(8, width).astype(FULL)
-    e_bias = packed[:, 8 * feats :].reshape(-1).astype(FULL)
+    packed = gather_small(jnp.concatenate([v.reshape(-1, feats) for v in small], axis=0))
     x_own = own_pair(inputs)
     x_near = gather_near(tie(x_own, packed))
 
@@ -830,22 +859,14 @@
         "join_feed",
         (ek, hop(eg, 1), sk, hop(sg, 1)),
         [feed_cut] * teams,
-        after=tuple(x_near[1:]),
         teams=teams,
         hr=hr,
     )
-    feed_cuts = exchange(feed_cuts)
+    feed_cuts, x_near = meet(exchange(feed_cuts), x_near)
     x_pieces = gather_far(x_near)
-    e_cut, s_cut = simple(
-        lay_feed_kernel,
-        "lay_feed",
-        feed_cuts,
-        [((hp, width), LOW), ((cols, half), LOW)],
-        [((teams, 2, hr, cols), LOW)],
-        teams=teams,
-        hp=hp,
-    )
-
+    vec = packed[:, :8].transpose(1, 0, 2)
+    vec = vec.reshape(8, width).astype(FULL)
+    e_bias = packed[:, 8:].reshape(-1).astype(FULL)
     mix_cut = ((feats, 3 * span), LOW)
     *cuts, merge_rows = simple(
         cut_mix_kernel,
@@ -853,7 +874,7 @@
         (mix_rows,),
         [mix_cut] * teams + [((feats, width), LOW)],
         [((feats, 3 * width + LANES), LOW)],
-        after=(e_cut, s_cut, vec, *x_pieces[3:]),
+        after=(*feed_cuts, vec),
         teams=teams,
         dp_n=dp_n,
         each=each,
@@ -861,6 +882,17 @@
         starts=starts,
         width=width,
     )
+    e_cut, s_cut = simple(
+        lay_feed_kernel,
+        "lay_feed",
+        feed_cuts,
+        [((hp, width), LOW), ((cols, half), LOW)],
+        [((teams, 2, hr, cols), LOW)],
+        after=(cuts[0],),
+        teams=teams,
+        hp=hp,
+    )
+
     expand_mine = along(e_cut).reshape(half, width)
     shrink_mine = along(tie(s_cut, expand_mine[0])).reshape(width, half)
 
@@ -881,22 +913,26 @@
     team_rows = lambda n: pl.BlockSpec((own_rows, n), lambda k, a: (k ^ (a[0] // 2), 0))
     x_sizes = [v.shape[0] for v in x_pieces]
     row_specs = lambda sizes: [fixed((n, width)) for n in sizes]
-    (first,) = call(
+    first, first_t = call(
         functools.partial(norm_kernel, x_sizes, rows),
         "norm",
         (teams,),
         at,
         (*x_pieces, vec),
         row_specs(x_sizes) + [vec_spec],
-        [((length, width), LOW)],
-        [team_rows(width)],
+        [((length, width), LOW), ((width, length), LOW)],
+        [
+            team_rows(width),
+            pl.BlockSpec((width, own_rows), lambda k, a: (0, k ^ (a[0] // 2))),
+        ],
         [pltpu.VMEM((own_rows, width), LOW)],
         length * width * 10,
         2 * act_bytes,
         after=(cuts[0],),
     )
     got = exchange(cuts)
-    (first,), got = meet((first,), got)
+    (first, first_t), moved = meet((first, first_t), got[1:])
+    got = [got[0], *moved]
     merge_rows = tie(merge_rows, *got)
     mix = [v for g in got for v in (g, hop(g, 1))]
     extra = -(-max(0, starts[-1] + span - width) // feats)
@@ -925,8 +961,6 @@
 
     (mixed, mix), near = meet((mixed, mix), near)
     merge = [merge_rows, *near]
-    if teams == 4:
-        merge.append(hop(merge[1], 4))
     g_own = own_pair(cotangent)
     g_near = gather_near(tie(g_own, mixed))
 
@@ -939,43 +973,49 @@
 
     def qkv_specs(base):
         return [
-            pl.BlockSpec((own_rows, LANES), lambda p, a, j=j, m=m: (j, m * per + base + p))
+            pl.BlockSpec((length, LANES), lambda p, a, m=m: (0, m * per + base + p))
             for m in range(3)
-            for j in range(teams)
         ]
 
     attended, wait = [], ()
+    logs = []
     for base, count in runs:
-        got = call(
+        *got, log = call(
             functools.partial(attend_forward_kernel, teams, own_rows, dim, heads, base),
             "attend_forward",
             (count,),
             at,
-            (*([mixed] * (3 * teams)), *segs),
+            (mixed, mixed, mixed, *segs),
             qkv_specs(base) + seg_specs,
-            [((own_rows, part), LOW)] * teams,
-            [column] * teams,
+            [((own_rows, part), LOW)] * teams + [((length, part), FULL)],
+            [column] * teams + [pl.BlockSpec((length, LANES), lambda p, a: (0, p))],
             [],
             length * length * dim * heads * 2,
             4 * length * part * 2,
             length * length * heads // 4,
             after=wait,
         )
+        logs.append(log)
         if base == 0:
-            got, moved = meet(got, g_near[1:])
-            g_near = [g_own, *moved]
+            other = [hop(v, 1) for v in merge]
+            got, (*other, g_x, g_y) = meet(got, (*other, *g_near[1:3]))
+            g_near = [g_own, g_x, g_y, *g_near[3:]]
             wait = (got[0],)
             attended = exchange(got)
-            expand_mine, shrink_mine = tie(expand_mine, got[0]), tie(shrink_mine, got[0])
+            expand_other = hop(tie(expand_mine, got[0]), 1)
+            if teams == 4:
+                merge.append(hop(tie(merge[1], got[0]), 4))
         else:
-            got, moved = meet(got, (*attended, *merge[3:]))
+            got, (expand_other, *moved) = meet(got, (expand_other, *attended, *merge[3:]))
             attended = [*moved[:teams], *exchange(got)]
+            shrink_other = hop(tie(shrink_mine, got[0]), 1)
             merge = [*merge[:3], *moved[teams:]]
-    merge = [v for g in merge for v in (g, hop(g, 1))]
+            other += [hop(v, 1) for v in merge[len(other) :]]
+    merge = [v for both in zip(merge, other) for v in both]
     if not whole_rows:
         merge = [assemble(merge, extra)]
 
-    weights = (expand_mine, shrink_mine, hop(expand_mine, 1), hop(shrink_mine, 1))
+    weights = (expand_mine, shrink_mine, expand_other, shrink_other)
     wide = ((own_rows, width), FULL)
     wide_low = ((own_rows, width), LOW)
     piece = ((rows, width), LOW)
@@ -1005,10 +1045,11 @@
     acts, d_pres, e_sums, d_second, out = [], [], [], [], []
     for group in groups:
         sizes = [x_sizes[i] for i in group]
-        n, m = len(sizes), sum(sizes)
+        out_sizes = sizes if len(sizes) == 1 else [rows] * (sum(sizes) // rows)
+        n, m = len(out_sizes), sum(sizes)
         half_spec = pl.BlockSpec((m, half), lambda f, a: (0, f))
         res = call(
-            functools.partial(feed_kernel, sizes),
+            functools.partial(feed_kernel, sizes, out_sizes),
             "feed",
             (2,),
             at,
@@ -1018,9 +1059,9 @@
             + [pl.BlockSpec((1, half), lambda f, a: (0, f))],
             [((m, units), LOW)] * 2
             + [((8, units), FULL)]
-            + [((size, width), LOW) for size in sizes] * 2,
+            + [((size, width), LOW) for size in out_sizes] * 2,
             [half_spec, half_spec, pl.BlockSpec((8, half), lambda f, a: (0, f))]
-            + row_specs(sizes) * 2,
+            + row_specs(out_sizes) * 2,
             [pltpu.VMEM((m, width), LOW)] * 2
             + [pltpu.VMEM((m, width), FULL)] * 2
             + [
@@ -1040,6 +1081,9 @@
         elif len(acts) == 1 and teams == 4:
             res, moved = meet(res, (*second[3:], *g_pieces[3:]))
             second, g_pieces = [*second[:3], *moved[:2]], [*g_pieces[:3], *moved[2:]]
+            early = reduce_early([None, *res[3 : 3 + n]])
+        elif teams == 4:
+            res, early = meet(res, early)
         acts.append(res[0])
         d_pres.append(res[1])
         e_sums.append(res[2])
@@ -1069,14 +1113,17 @@
             after=after,
         )
 
+    if teams != 4:
+        early = reduce_early(d_second)
     far = reduce_far(d_second)
     sm, sg = feed_grad("shrink_grad", g_pieces, acts, True, ())
     (sm, sg), far = meet((sm, sg), far)
-    near = reduce_near(d_second, far)
+    late, folded = reduce_late(d_second, far)
     s_got = hop(sg, 1)
-    em, eg = feed_grad("expand_grad", second, d_pres, False, (sm,))
-    (em, eg), (s_got, *near) = meet((em, eg), (s_got, *near))
-    d_second = [d_second[0], *near]
+    out_early = reduce_early([tie(v, *folded[:1]) for v in out])
+    em, eg = feed_grad("expand_grad", second, d_pres, False, (sm, *folded))
+    (em, eg), (s_got, *late) = meet((em, eg), (s_got, *late))
+    d_second = reduce_terms(d_second, early, late)
     s_sum = add_low(sm, s_got)
     e_got = hop(eg, 1)
     g_shrink = scatter(s_sum.reshape(dp_n, cols, half))
@@ -1115,132 +1162,130 @@
         step=step,
     )
 
-    (mine, give), (e_got, *d_attended) = meet((mine, give), (e_got, *d_attended))
+    (mine, give), (e_got, *moved) = meet((mine, give), (e_got, *d_attended, *out_early))
+    d_attended, out_early = moved[:teams], moved[teams:]
     e_sum = add_low(em, e_got)
     g_expand = scatter(e_sum.reshape(dp_n, hp, width))
-    out_far = reduce_far([*out[:3], *[tie(v, *d_attended) for v in out[3:]]])
 
     def core_parts(mine, got):
-        return [add_low(pick(mine, team ^ k), pick(got, team ^ k)) for k in range(teams)]
-
-    merge_got = hop(give, 1)
-    merge_mine = mine
-
-    d_parts, g_mix, mix_sums = [], [], []
-    mix_block = ((teams, feats, 3 * part), LOW)
-    wait = (e_sum, mixed)
-    merge_near = []
-    for base in range(per):
+        return simple(
+            add_parts_kernel,
+            "add_parts",
+            (mine, got),
+            [(mine.shape[1:], LOW)] * teams,
+        )
+
+    g_merge = core_parts(mine, hop(give, 1))
+    merge_near = exchange([tie(v, *d_attended) for v in g_merge])[1:]
+
+    d_parts, wait = [], (e_sum, mixed, g_merge[0])
+    for base, count in runs:
         (d_part,) = call(
             functools.partial(attend_backward_kernel, teams, own_rows, dim, heads, share, base),
             "attend_backward",
-            (1,),
+            (count,),
             at,
-            (*([mixed] * (3 * teams)), *d_attended, *segs),
+            (mixed, mixed, mixed, *d_attended, *segs, logs[len(d_parts)]),
             qkv_specs(base)
             + [pl.BlockSpec((own_rows, LANES), lambda p, a, base=base: (0, base + p))] * teams
-            + seg_specs,
-            [((3, length, LANES), LOW)],
+            + seg_specs
+            + [pl.BlockSpec((length, LANES), lambda p, a: (0, p))],
+            [((3, length, part), LOW)],
             [pl.BlockSpec((3, length, LANES), lambda p, a: (0, 0, p))],
             [
                 pltpu.VMEM((length, dim), FULL),
                 pltpu.VMEM((length, dim), FULL),
                 pltpu.VMEM((length, LANES), LOW),
+                pltpu.VMEM((LANES, length), FULL),
             ],
-            5 * length * length * dim * heads // per * 2,
-            8 * length * LANES * 2,
-            length * length * heads // per // 2,
+            5 * length * length * dim * heads,
+            8 * length * part * 2,
+            length * length * heads // 4,
             after=wait,
         )
         if base == 0:
-            (d_part,), (merge_got, *out_far) = meet((d_part,), (merge_got, *out_far))
-            out_near = reduce_near(out, out_far)
-            g_merge = core_parts(merge_mine, merge_got)
-        if base == per - 1:
             (d_part,), merge_near = meet((d_part,), merge_near)
+            out_far = reduce_far([*out[:5], *[tie(v, d_part) for v in out[5:]]])
+            wait = (d_part,)
+        else:
+            (d_part,), out_far = meet((d_part,), out_far)
+            out_late, folded = reduce_late(out, out_far)
         d_parts.append(d_part)
-        wait = (d_part,)
-        if base % (per // 2) == per // 2 - 1:
-            sides = d_parts[-(per // 2) :]
-            mine, give, sums = call(
-                mix_grad_kernel,
-                "mix_grad",
-                (3,),
-                at,
-                (*sides, first),
-                [pl.BlockSpec((1, length, LANES), lambda c, a: (c, 0, 0))] * len(sides)
-                + [fixed((length, width))],
-                [mix_block, mix_block, ((8, 3 * part), FULL)],
-                [pl.BlockSpec((teams, feats, part), lambda c, a: (0, 0, c))] * 2
-                + [pl.BlockSpec((8, part), lambda c, a: (0, c))],
-                [
-                    pltpu.VMEM((width, length), LOW),
-                    pltpu.VMEM((width, part), FULL),
-                    pltpu.VMEM((length, part), LOW),
-                ],
-                2 * length * width * 3 * part,
-                3 * act_bytes,
-            )
-            if base < per - 1:
-                (mine, give), out_near = meet((mine, give), out_near)
-                merge_near = exchange([tie(v, give) for v in g_merge])[1:]
-                mix_got = hop(give, 1)
-                wait = (give,)
-            else:
-                (mine, give), mix_near = meet((mine, give), g_mix[1:])
-                g_mix = [g_mix[0], *mix_near]
-                mix_got = hop(give, 1)
-            mix_sums.append(sums[0].reshape(3, part))
-            g_mix += exchange(core_parts(mine, mix_got))
-    out = [out[0], *out_near]
-    g_merge = [g_merge[0], *merge_near]
-    g_merge = functools.reduce(jnp.add, [v.astype(FULL) for v in g_merge]).astype(LOW)
-    merge_each = width // dp_n
-    g_merge = jnp.stack(
-        [g_merge[:, d * merge_each : (d + 1) * merge_each] for d in range(dp_n)]
-    )
-    grad_merge = scatter(g_merge).astype(FULL)
-
-    block_out = simple(
-        block_out_kernel,
-        "block_out",
-        (*out, hidden, vec),
-        [piece, piece],
-        after=(d_parts[-1],),
-        rows=rows,
-        terms=terms,
-    )
-    block_out = swap_out(*block_out)
-
+
+    mix_block = ((teams, feats, 3 * span), LOW)
+    mine, give, mix_sums = call(
+        mix_grad_kernel,
+        "mix_grad",
+        (3,),
+        at,
+        (*d_parts, first_t),
+        [pl.BlockSpec((1, length, part), lambda c, a: (c, 0, 0))] * 2 + [fixed((width, length))],
+        [mix_block, mix_block, ((8, 3 * span), FULL)],
+        [pl.BlockSpec((teams, feats, span), lambda c, a: (0, 0, c))] * 2
+        + [pl.BlockSpec((8, span), lambda c, a: (0, c))],
+        [pltpu.VMEM((width, span), FULL), pltpu.VMEM((length, span), LOW)],
+        2 * length * width * 3 * span,
+        3 * act_bytes,
+        after=tuple(folded[:1]),
+    )
+    mix_sums = mix_sums[0].reshape(3, span)
+    (mine, give), out_late = meet((mine, give), out_late)
+    mix_got = hop(give, 1)
     feed_cuts = simple(
         split_feed_kernel,
         "split_feed",
         (g_expand, g_shrink),
         [feed_cut] * teams,
         teams=teams,
+        after=(give,),
         hp=hp,
     )
+    out = reduce_terms(out, out_early, out_late)
+    block_out = simple(
+        block_out_kernel,
+        "block_out",
+        (*out, hidden, vec),
+        [piece, piece],
+        after=(give,),
+        rows=rows,
+        terms=terms,
+    )
+    g_merge = [g_merge[0], *merge_near]
+    g_merge = functools.reduce(jnp.add, [v.astype(FULL) for v in g_merge]).astype(LOW)
+    merge_each = width // dp_n
+    g_merge = jnp.stack(
+        [g_merge[:, d * merge_each : (d + 1) * merge_each] for d in range(dp_n)]
+    )
+    grad_merge = scatter(g_merge).astype(FULL)
+
     groups = [([3, 4], 3), ([1, 2], 1), ([0], 0)] if teams == 4 else [([k], k) for k in range(teams)]
-    d_first, first_sums, wait = [None] * len(x_sizes), [], (give,)
+    kept, (mix_got,) = meet((*block_out, *feed_cuts), (mix_got,))
+    block_out, feed_cuts = kept[:2], kept[2:]
+    g_mix = core_parts(mine, mix_got)
+    d_first, first_sums, wait = [], [], (g_mix[0], g_merge)
+    feed_cuts, g_mix = exchange(feed_cuts), exchange(g_mix)
+    block_out = swap_out(*block_out)
+    far = early = ()
     for group, low in groups:
         sizes = [x_sizes[i] for i in group]
+        out_sizes = sizes if len(sizes) == 1 else [rows] * (sum(sizes) // rows)
         n = sum(sizes) // own_rows
         sums, *got = call(
-            functools.partial(first_back_kernel, sizes, rows, span),
+            functools.partial(first_back_kernel, sizes, out_sizes, rows, span),
             "first_back",
             (n,),
             at,
             (*d_parts, *[x_pieces[i] for i in group], mix),
             [
                 pl.BlockSpec(
-                    (3, own_rows, LANES), lambda i, a, low=low: (0, (i + low) ^ (a[0] // 2), 0)
+                    (3, own_rows, part), lambda i, a, low=low: (0, (i + low) ^ (a[0] // 2), 0)
                 )
             ]
-            * per
+            * 2
             + row_specs(sizes)
             + [fixed((width, 3 * span))],
-            [((8, width), FULL)] + [((size, width), LOW) for size in sizes],
-            [vec_spec] + row_specs(sizes),
+            [((8, width), FULL)] + [((size, width), LOW) for size in out_sizes],
+            [vec_spec] + row_specs(out_sizes),
             [
                 pltpu.VMEM((own_rows, width), LOW),
                 pltpu.VMEM((own_rows, width), LOW),
@@ -1250,16 +1295,21 @@
             n * own_rows * width * 8,
             after=wait,
         )
-        wait = (sums, feed_cuts[0])
         first_sums.append(sums)
-        for i, v in zip(group, got):
-            d_first[i] = v
-    first_sums = functools.reduce(jnp.add, first_sums)
-    far = reduce_far(d_first)
-    if teams == 4:
-        (d_first[0], d_first[1], d_first[2]), far = meet(d_first[:3], far)
-    d_first = [d_first[0], *reduce_near(d_first, far)]
-
+        if not d_first:
+            got, moved = meet(got, feed_cuts[1:])
+            feed_cuts = [feed_cuts[0], *moved]
+            wait = (sums,)
+            far = reduce_far([None] * 5 + list(got))
+        elif len(first_sums) == 2:
+            got, moved = meet(got, g_mix[1:])
+            g_mix = [g_mix[0], *moved]
+            wait = (sums,)
+            if teams == 4:
+                early = reduce_early([None, *got])
+        else:
+            got, far = meet(got, far)
+        d_first.append(got)
     (g_mix,) = simple(
         join_mix_kernel,
         "join_mix",
@@ -1274,30 +1324,26 @@
         width=width,
     )
     grad_mix = scatter(g_mix).astype(FULL)
-
+    first_sums = functools.reduce(jnp.add, first_sums)
+    if teams == 4:
+        d_first = [*d_first[2], *d_first[1], *d_first[0]]
+    else:
+        d_first = [v for got in d_first for v in got]
+        early = reduce_early(d_first)
     ek, eg, sk, sg = simple(
         part_feed_kernel,
         "part_feed",
-        exchange(feed_cuts),
+        feed_cuts,
         [(e_shape, LOW), (e_shape, LOW), (s_shape, LOW), (s_shape, LOW)],
         [((teams, 2, hr, cols), LOW)],
         teams=teams,
     )
-    grad_expand, grad_shrink = simple(
-        end_feed_kernel,
-        "end_feed",
-        (ek, hop(eg, 1), sk, hop(sg, 1)),
-        [(expand_weight.shape, FULL), (shrink_weight.shape, FULL)],
-        teams=teams,
-        hr=hr,
-    )
-
+    late, folded = reduce_late(d_first, far, (g_mix, ek))
     def spread(v):
         return lax.dynamic_update_slice_in_dim(
             jnp.zeros((width + 2 * LANES,), FULL), v, start, 0
         )[:width]
 
-    mix_sums = jnp.concatenate(mix_sums, axis=1)
     d_e = functools.reduce(jnp.add, [s[0] for s in e_sums]).reshape(2, dp_n, hp)[:, :, :hr]
     d_e = jnp.where(core == 0, d_e, d_e[::-1]).transpose(1, 0, 2)
     d_e = lax.dynamic_update_slice_in_dim(
@@ -1314,16 +1360,26 @@
         second_sums[3],
         d_e.reshape(-1),
     )
-    total = reduce_small(
-        jnp.concatenate([v.reshape(seq_n, -1) for v in partial], axis=1)
-    )
+    partial = jnp.concatenate([v.reshape(seq_n, -1) for v in partial], axis=1)
+    total = reduce_small(tie(partial, *folded[:1]))
+    (ek, sk), (total, *early) = meet((ek, sk), (total, *early))
+    d_first = reduce_terms(d_first, early, late)
+    grad_expand, grad_shrink = simple(
+        end_feed_kernel,
+        "end_feed",
+        (ek, hop(eg, 1), sk, hop(sg, 1)),
+        [(expand_weight.shape, FULL), (shrink_weight.shape, FULL)],
+        teams=teams,
+        hr=hr,
+    )
+
     piece_full = ((rows, width), FULL)
     input_grad = simple(
         input_grad_kernel,
         "input_grad",
         (*d_first, d_hidden, x_own, vec),
         [piece_full, piece_full],
-        after=(total, grad_expand),
+        after=(grad_expand,),
         rows=rows,
         terms=terms,
     )

time: 717 us -> 659 us (0.919)
  waiting for transfers between devices: 163 us -> 121 us
    ppermute x83 -> x85, waiting for transfers between devices: 145 us -> 112 us  [hop(): lax.ppermute(v, 'seq', [(i, i ^ mask) for i in range(seq_n)]).reshape(shape)]
    all_gather x3, waiting for transfers between devices: 14.6 us -> 0.02 us  [along(): return lax.all_gather(v, 'dp', axis=0)]
    convert_element_type x5 -> x2, other arithmetic: 16.1 us -> 8.7 us  [add_low(): return (a.astype(FULL) + b.astype(FULL)).astype(LOW)]
    pallas_call x34 -> x33, Pallas kernels: 378 us -> 372 us  [call(): pl.pallas_call(kernel, grid_spec=spec, out_shape=[jax.ShapeDtypeStruct(s,...]
    unnamed x153 -> x152, local copies, waits for them, and re-layouts: 18.7 us -> 15.9 us
    ppermute x83 -> x85, starting transfers between devices: 74.4 us -> 72.8 us  [hop(): lax.ppermute(v, 'seq', [(i, i ^ mask) for i in range(seq_n)]).reshape(shape)]
  transfers between devices with their start and end apart: 92 -> 94, of which waited for: 38 -> 41; matrix products, arithmetic and copies ran while one was open for 6% -> 6% of each run, Pallas kernels for 51% -> 56%
where the time goes in v3:
time: 659 us; the launch traced here: 649 us
  Pallas kernels  372 us (56%)
  waiting for transfers between devices  121 us (18%)
  starting transfers between devices  75.6 us (11%)
  local copies, waits for them, and re-layouts  34 us (5%)
  other arithmetic  28.6 us (4%)
  between operations  17.7 us (3%)
    pallas_call x33, Pallas kernels, call(): pl.pallas_call(kernel, grid_spec=spec, out_shape=[jax.ShapeDtypeStruct(s,...  372 us
    ppermute x85, waiting for transfers between devices, hop(): lax.ppermute(v, 'seq', [(i, i ^ mask) for i in range(seq_n)]).reshape(shape)  112 us
    ppermute x85, starting transfers between devices, hop(): lax.ppermute(v, 'seq', [(i, i ^ mask) for i in range(seq_n)]).reshape(shape)  72.8 us
    unnamed x152, local copies, waits for them, and re-layouts  15.9 us
  transfers between devices with their start and end apart: 94, of which 41 were waited for; matrix products, arithmetic and copies ran while one was open for 6% of the time, Pallas kernels for 56%

profile of v3, /device:TPU:0, one launch (start us, length us, event | category | flops | bytes accessed | tf_op | source)
XLA Modules:
  0.0 649.1 jit_solution(18161572462144440824)
XLA Ops:
  45.2 17.9 %collective-permute-done.2.refs_2_.refs_1_ = bf16[2,200,400]{2,1,0:T(8,128)(2,1)S(1)} collective-permute-done((bf16[2,200,400]{2,1,0:T(8,128)(2,1)}, bf16[2,200,400]{2,1,0:T(8,128)(2,1)S(1)}, u32[]{:S(2)}, u32[]{:S(2)}) %collective-permute-start.2) | collective-permute-done | bytes 320032 | tf_op jit(solution)/shard_map/ppermute | solution.py:716
  63.2 7.4 %collective-permute-done.3.refs_3_.refs_2_ = bf16[2,200,400]{2,1,0:T(8,128)(2,1)} collective-permute-done((bf16[2,200,400]{2,1,0:T(8,128)(2,1)}, bf16[2,200,400]{2,1,0:T(8,128)(2,1)}, u32[]{:S(2)}, u32[]{:S(2)}) %collective-permute-start.3) | collective-permute-done | bytes 320032 | tf_op jit(solution)/shard_map/ppermute | solution.py:716
  70.6 5.4 cut_mix.1
  87.0 10.6 %collective-permute-done.12.refs_3_.refs_2_ = bf16[192,1600]{1,0:T(8,128)(2,1)S(1)} collective-permute-done((bf16[192,1600]{1,0:T(8,128)(2,1)S(1)}, bf16[192,1600]{1,0:T(8,128)(2,1)S(1)}, u32[]{:S(2)}, u32[]{:S(2)}) %collective-permute-start.12) | collective-permute-done | bytes 614432 | tf_op jit(solution)/shard_map/ppermute | solution.py:716
  103.5 9.7 %norm.1 = (bf16[1536,1600]{1,0:T(8,128)(2,1)}, bf16[1600,1536]{1,0:T(8,128)(2,1)}) custom-call(s32[5]{0:T(128)} %pad_add_fusion.at_ref, bf16[384,1600]{1,0:T(8,128)(2,1)} %copy-done.2, bf16[384,1600]{1,0:T(8,128)(2,1)} %bitcast.84, bf16[384,1600]{1,0:T(8,128)(2,1)} %bitcast.7.refs_2_.refs_3_, bf16[192,1600]{1,0:T(8,128)(2,1)} %copy-done.14, ...), custom_call_target="tpu_custom_call" | custom-call | flops 6144000 | bytes 2457600 | tf_op jit(solution)/shard_map/norm/pallas_call | solution.py:70
  113.6 9.4 %collective-permute-done.16.refs_6_ = bf16[200,1536]{1,0:T(8,128)(2,1)} collective-permute-done((bf16[200,1536]{1,0:T(8,128)(2,1)}, bf16[200,1536]{1,0:T(8,128)(2,1)}, u32[]{:S(2)}, u32[]{:S(2)}) %collective-permute-start.16) | collective-permute-done | bytes 614432 | tf_op jit(solution)/shard_map/ppermute | solution.py:716
  130.7 16.3 %mix.1 = (bf16[1536,1536]{1,0:T(8,128)(2,1)}, bf16[1600,1536]{1,0:T(8,128)(2,1)}) custom-call(s32[5]{0:T(128)} %pad_add_fusion.at_ref, bf16[200,1536]{1,0:T(8,128)(2,1)} %get-tuple-element.275.refs_6_.refs_0_.refs_4_, bf16[200,1536]{1,0:T(8,128)(2,1)} %collective-permute-done.11.refs_1_, bf16[200,1536]{1,0:T(8,128)(2,1)} %collective-permute-done.14.refs_2_, ...), custom_call_target="tpu_custom_call" | custom-call | flops 1887436800 | bytes 4915200 | tf_op jit(solution)/shard_map/mix/pallas_call | solution.py:70
  150.3 19.8 %attend_forward.2 = (bf16[384,256]{1,0:T(8,128)(2,1)}, bf16[384,256]{1,0:T(8,128)(2,1)}, bf16[384,256]{1,0:T(8,128)(2,1)}, bf16[384,256]{1,0:T(8,128)(2,1)}, f32[1536,256]{1,0:T(8,128)}) custom-call(s32[5]{0:T(128)} %pad_add_fusion.at_ref, bf16[1536,1536]{1,0:T(8,128)(2,1)} %get-tuple-element.292.refs_0_.refs_1_.refs_2_.refs_11_, ...), custom_call_target="tpu_custom_call" | custom-call | flops 528482304 | bytes 786432 | tf_op jit(solution)/shard_map/attend_forward/pallas_call | solution.py:70
  170.1 7.1 %collective-permute-done.26 = bf16[2,192,1600]{2,1,0:T(8,128)(2,1)S(1)} collective-permute-done((bf16[2,192,1600]{2,1,0:T(8,128)(2,1)S(1)}, bf16[2,192,1600]{2,1,0:T(8,128)(2,1)S(1)}, u32[]{:S(2)}, u32[]{:S(2)}) %collective-permute-start.26) | collective-permute-done | bytes 1228832 | tf_op jit(solution)/shard_map/ppermute | solution.py:716
  181.7 15.7 %attend_forward.3 = (bf16[384,256]{1,0:T(8,128)(2,1)}, bf16[384,256]{1,0:T(8,128)(2,1)}, bf16[384,256]{1,0:T(8,128)(2,1)}, bf16[384,256]{1,0:T(8,128)(2,1)}, f32[1536,256]{1,0:T(8,128)}) custom-call(s32[5]{0:T(128)} %pad_add_fusion.at_ref, bf16[1536,1536]{1,0:T(8,128)(2,1)} %get-tuple-element.292.refs_0_.refs_1_.refs_2_.refs_11_, ...), custom_call_target="tpu_custom_call" | custom-call | flops 528482304 | bytes 786432 | tf_op jit(solution)/shard_map/attend_forward/pallas_call | solution.py:70
  197.4 6.8 %collective-permute-done.30.refs_2_ = bf16[384,256]{1,0:T(8,128)(2,1)S(1)} collective-permute-done((bf16[384,256]{1,0:T(8,128)(2,1)}, bf16[384,256]{1,0:T(8,128)(2,1)S(1)}, u32[]{:S(2)}, u32[]{:S(2)}) %collective-permute-start.30) | collective-permute-done | bytes 196640 | tf_op jit(solution)/shard_map/ppermute | solution.py:716
  218.0 13.2 %merge_norm.1 = (f32[384,1600]{1,0:T(8,128)}, bf16[384,1600]{1,0:T(8,128)(2,1)}, bf16[1800,1600]{1,0:T(8,128)(2,1)}) custom-call(s32[5]{0:T(128)} %pad_add_fusion.at_ref, bf16[384,256]{1,0:T(8,128)(2,1)} %get-tuple-element.311.refs_5_.refs_0_, bf16[384,256]{1,0:T(8,128)(2,1)} %copy-done.24, bf16[384,256]{1,0:T(8,128)(2,1)} %copy-done.25, ...), custom_call_target="tpu_custom_call" | custom-call | flops 629145600 | bytes 6102016 | tf_op jit(solution)/shard_map/merge_norm/pallas_call | solution.py:70
  237.2 19.8 %feed.3 = (bf16[384,1792]{1,0:T(8,128)(2,1)}, bf16[384,1792]{1,0:T(8,128)(2,1)}, f32[8,1792]{1,0:T(8,128)}, bf16[384,1600]{1,0:T(8,128)(2,1)}, bf16[384,1600]{1,0:T(8,128)(2,1)}) custom-call(s32[5]{0:T(128)} %pad_add_fusion.at_ref, bf16[384,1600]{1,0:T(8,128)(2,1)} %get-tuple-element.323.refs_0_, bf16[384,1600]{1,0:T(8,128)(2,1)} %copy-done.4, ...), custom_call_target="tpu_custom_call" | custom-call | flops 2202009600 | bytes 4710400 | tf_op jit(solution)/shard_map/feed/pallas_call | solution.py:70
  265.8 34.1 %feed.4 = (bf16[768,1792]{1,0:T(8,128)(2,1)}, bf16[768,1792]{1,0:T(8,128)(2,1)}, f32[8,1792]{1,0:T(8,128)}, bf16[192,1600]{1,0:T(8,128)(2,1)}, bf16[192,1600]{1,...) custom-call(s32[5]{0:T(128)} %pad_add_fusion.at_ref, ...), custom_call_target="tpu_custom_call" | custom-call | flops 4404019200 | bytes 6553600 | tf_op jit(solution)/shard_map/feed/pallas_call | solution.py:70
  302.8 20.4 %feed.5 = (bf16[384,1792]{1,0:T(8,128)(2,1)}, bf16[384,1792]{1,0:T(8,128)(2,1)}, f32[8,1792]{1,0:T(8,128)}, bf16[192,1600]{1,0:T(8,128)(2,1)}, bf16[192,1600]{1,...) custom-call(s32[5]{0:T(128)} %pad_add_fusion.at_ref, bf16[192,1600]{1,0:T(8,128)(2,1)} %copy-done.16, ...), custom_call_target="tpu_custom_call" | custom-call | flops 2202009600 | bytes 4710400 | tf_op jit(solution)/shard_map/feed/pallas_call | solution.py:70
  325.5 18.8 %shrink_grad.1 = (bf16[1600,896]{1,0:T(8,128)(2,1)}, bf16[1600,896]{1,0:T(8,128)(2,1)}) custom-call(s32[5]{0:T(128)} %pad_add_fusion.at_ref, bf16[384,1600]{1,0:T(8,128)(2,1)} %copy-done.4, bf16[384,1600]{1,0:T(8,128)(2,1)} %bitcast.82, bf16[384,1600]{1,0:T(8,128)(2,1)} %bitcast.15.refs_3_.refs_2_, ...), custom_call_target="tpu_custom_call" | custom-call | flops 2202009600 | bytes 3891200 | tf_op jit(solution)/shard_map/shrink_grad/pallas_call | solution.py:70
  351.8 18.8 %expand_grad.1 = (bf16[896,1600]{1,0:T(8,128)(2,1)}, bf16[896,1600]{1,0:T(8,128)(2,1)}) custom-call(s32[5]{0:T(128)} %pad_add_fusion.at_ref, bf16[384,1600]{1,0:T(8,128)(2,1)} %get-tuple-element.323.refs_0_, bf16[384,1600]{1,0:T(8,128)(2,1)} %bitcast.76, bf16[384,1600]{1,0:T(8,128)(2,1)} %bitcast.79, bf16[192,1600]{1,0:T(8,128)(2,1)} %copy-done.16, ...), custom_call_target="tpu_custom_call" | custom-call | flops 2202009600 | bytes 3891200 | tf_op jit(solution)/shard_map/expand_grad/pallas_call | solution.py:70
  376.6 12.4 %second_back.1 = (f32[384,1600]{1,0:T(8,128)}, bf16[384,1600]{1,0:T(8,128)(2,1)}, f32[8,1600]{1,0:T(8,128)}, bf16[384,512]{1,0:T(8,128)(2,1)}, bf16[384,512]{1,0...) custom-call(s32[5]{0:T(128)} %pad_add_fusion.at_ref, bf16[384,1600]{1,0:T(8,128)(2,1)} %get-tuple-element.333.refs_0_, ...), custom_call_target="tpu_custom_call" | custom-call | flops 629145600 | bytes 5324032 | tf_op jit(solution)/shard_map/second_back/pallas_call | solution.py:70
  393.0 12.0 %merge_grad.1 = (bf16[4,200,1600]{2,1,0:T(8,128)(2,1)}, bf16[4,200,1600]{2,1,0:T(8,128)(2,1)}) custom-call(s32[5]{0:T(128)} %pad_add_fusion.at_ref, bf16[384,256]{1,0:T(8,128)(2,1)} %get-tuple-element.311.refs_5_.refs_0_, bf16[384,256]{1,0:T(8,128)(2,1)} %copy-done.24, bf16[384,256]{1,0:T(8,128)(2,1)} %copy-done.25, bf16[384,256]{1,0:T(8,128)(2,1)} %copy-done.26, ...), custom_call_target="tpu_custom_call" | custom-call | flops 629145600 | bytes 3260416 | tf_op jit(solution)/shard_map/merge_grad/pallas_call | solution.py:70
  405.1 5.2 collective-permute-done.54.refs_6_
  415.6 4.9 add_parts.2
  424.0 28.4 %attend_backward.2.refs_10_.refs_0_ = bf16[3,1536,256]{2,1,0:T(8,128)(2,1)} custom-call(s32[5]{0:T(128)} %pad_add_fusion.at_ref, bf16[1536,1536]{1,0:T(8,128)(2,1)} %get-tuple-element.292.refs_0_.refs_1_.refs_2_.refs_11_, bf16[1536,1536]{1,0:T(8,128)(2,1)} %get-tuple-element.292.refs_0_.refs_1_.refs_2_.refs_11_, ...), custom_call_target="tpu_custom_call" | custom-call | flops 1321205760 | bytes 1572864 | tf_op jit(solution)/shard_map/attend_backward/pallas_call | solution.py:70
  454.5 22.6 %attend_backward.3.refs_1_ = bf16[3,1536,256]{2,1,0:T(8,128)(2,1)} custom-call(s32[5]{0:T(128)} %pad_add_fusion.at_ref, bf16[1536,1536]{1,0:T(8,128)(2,1)} %get-tuple-element.292.refs_0_.refs_1_.refs_2_.refs_11_, bf16[1536,1536]{1,0:T(8,128)(2,1)} %get-tuple-element.292.refs_0_.refs_1_.refs_2_.refs_11_, ...), custom_call_target="tpu_custom_call" | custom-call | flops 1321205760 | bytes 1572864 | tf_op jit(solution)/shard_map/attend_backward/pallas_call | solution.py:70
  484.7 13.2 %mix_grad.1 = (bf16[4,200,1536]{2,1,0:T(8,128)(2,1)}, bf16[4,200,1536]{2,1,0:T(8,128)(2,1)}, f32[8,1536]{1,0:T(8,128)}) custom-call(s32[5]{0:T(128)} %pad_add_fusion.at_ref, bf16[3,1536,256]{2,1,0:T(8,128)(2,1)} %attend_backward.2.refs_10_.refs_0_, bf16[3,1536,256]{2,1,0:T(8,128)(2,1)} %attend_backward.3.refs_1_, ...), custom_call_target="tpu_custom_call" | custom-call | flops 1887436800 | bytes 3686400 | tf_op jit(solution)/shard_map/mix_grad/pallas_call | solution.py:70
  505.0 5.0 block_out.1
  519.5 5.1 add_parts.3
  526.7 8.3 %first_back.3 = (f32[8,1600]{1,0:T(8,128)}, bf16[192,1600]{1,0:T(8,128)(2,1)}, bf16[192,1600]{1,0:T(8,128)(2,1)}) custom-call(s32[5]{0:T(128)} %pad_add_fusion.at_ref, bf16[3,1536,256]{2,1,0:T(8,128)(2,1)} %attend_backward.2.refs_10_.refs_0_, bf16[3,1536,256]{2,1,0:T(8,128)(2,1)} %attend_backward.3.refs_1_, bf16[192,1600]{1,0:T(8,128)(2,1)} %copy-done.14, ...), custom_call_target="tpu_custom_call" | custom-call | flops 471859200 | bytes 1228800 | tf_op jit(solution)/shard_map/first_back/pallas_call | solution.py:70
  535.0 13.0 %first_back.4 = (f32[8,1600]{1,0:T(8,128)}, bf16[192,1600]{1,0:T(8,128)(2,1)}, bf16[192,1600]{1,0:T(8,128)(2,1)}, bf16[192,1600]{1,0:T(8,128)(2,1)}, bf16[192,1600]{1,0:T(8,128)(2,1)}) custom-call(s32[5]{0:T(128)} %pad_add_fusion.at_ref, bf16[3,1536,256]{2,1,0:T(8,128)(2,1)} %attend_backward.2.refs_10_.refs_0_, ...), custom_call_target="tpu_custom_call" | custom-call | flops 943718400 | bytes 2457600 | tf_op jit(solution)/shard_map/first_back/pallas_call | solution.py:70
  552.3 8.3 %first_back.5 = (f32[8,1600]{1,0:T(8,128)}, bf16[384,1600]{1,0:T(8,128)(2,1)}) custom-call(s32[5]{0:T(128)} %pad_add_fusion.at_ref, bf16[3,1536,256]{2,1,0:T(8,128)(2,1)} %attend_backward.2.refs_10_.refs_0_, bf16[3,1536,256]{2,1,0:T(8,128)(2,1)} %attend_backward.3.refs_1_, bf16[384,1600]{1,0:T(8,128)(2,1)} %copy-done.2, ...), custom_call_target="tpu_custom_call" | custom-call | flops 471859200 | bytes 1228800 | tf_op jit(solution)/shard_map/first_back/pallas_call | solution.py:70
  572.1 5.9 collective-permute-done.70.refs_2_
  599.5 5.2 collective-permute-done.79
  618.1 7.4 %input_grad.1 = (f32[192,1600]{1,0:T(8,128)}, f32[192,1600]{1,0:T(8,128)}) custom-call(s32[5]{0:T(128)} %pad_add_fusion.at_ref, bf16[384,1600]{1,0:T(8,128)(2,1)} %get-tuple-element.465.refs_0_, bf16[192,1600]{1,0:T(8,128)(2,1)} %copy-done.40, bf16[192,1600]{1,0:T(8,128)(2,1)} %copy-done.42, bf16[192,1600]{1,0:T(8,128)(2,1)} %copy-done.43, ...), custom_call_target="tpu_custom_call" | custom-call | bytes 2470400 | tf_op jit(solution)/shard_map/input_grad/pallas_call | solution.py:70
  (438 shorter events, 223.3 us)
Async XLA Ops:
  7.2 63.4 %all-gather.7.cloned.1.call-start = ((), (), s32[]{:S(2)}) async-start(), calls=%async_computation.8 | async-start | bytes 3328000 | tf_op jit(solution)/shard_map/all_gather | solution.py:722
  9.5 168.4 %all-gather.9.cloned.1.call-start = ((), (), s32[]{:S(2)}) async-start(), calls=%async_computation.9 | async-start | bytes 3727360 | tf_op jit(solution)/shard_map/all_gather | solution.py:722
  23.3 47.3 %collective-permute-start.9 = (bf16[2,192,1600]{2,1,0:T(8,128)(2,1)S(1)}, bf16[2,192,1600]{2,1,0:T(8,128)(2,1)S(1)}, u32[]{:S(2)}, u32[]{:S(2)}) collective-permute-start(bf16[2,192,1600]{2,1,0:T(8,128)(2,1)S(1)} %bitcast.64), channel_id=1, source_target_pairs={{0,2},{1,3},{2,0},{3,1},{4,6},{5,7},{6,4},{7,5},{8,10},{9,11},{10,... | collective-permute-start | bytes 3686408 | tf_op jit(solution)/shard_map/ppermute | solution.py:716
  25.4 45.2 %collective-permute-start.10 = (bf16[2,192,1600]{2,1,0:T(8,128)(2,1)S(1)}, bf16[2,192,1600]{2,1,0:T(8,128)(2,1)}, u32[]{:S(2)}, u32[]{:S(2)}) collective-permute-start(bf16[2,192,1600]{2,1,0:T(8,128)(2,1)S(1)} %bitcast.65), channel_id=1, source_target_pairs={{0,4},{1,5},{2,6},{3,7},{4,0},{5,1},{6,2},{7,3},{8,12},{9,13},{10,... | collective-permute-start | bytes 3686408 | tf_op jit(solution)/shard_map/ppermute | solution.py:716
  41.5 29.1 %collective-permute-start.3 = (bf16[2,200,400]{2,1,0:T(8,128)(2,1)}, bf16[2,200,400]{2,1,0:T(8,128)(2,1)}, u32[]{:S(2)}, u32[]{:S(2)}) collective-permute-start(bf16[2,200,400]{2,1,0:T(8,128)(2,1)} %get-tuple-element.268), channel_id=1, source_target_pairs={{0,4},{1,5},{2,6},{3,7},{4,0},{5,1},{6,2},{7,3},{8,12},{9,13},{10,... | collective-permute-start | bytes 960008 | tf_op jit(solution)/shard_map/ppermute | solution.py:716
  41.6 29.0 %collective-permute-start.4 = (bf16[2,200,400]{2,1,0:T(8,128)(2,1)}, bf16[2,200,400]{2,1,0:T(8,128)(2,1)}, u32[]{:S(2)}, u32[]{:S(2)}) collective-permute-start(bf16[2,200,400]{2,1,0:T(8,128)(2,1)} %get-tuple-element.269), channel_id=1, source_target_pairs={{0,6},{1,7},{2,4},{3,5},{4,2},{5,3},{6,0},{7,1},{8,14},{9,15},{10,... | collective-permute-start | bytes 960008 | tf_op jit(solution)/shard_map/ppermute | solution.py:716
  80.1 124.9 %all-gather.11.cloned.1.call-start = ((), (), s32[]{:S(2)}) async-start(), calls=%async_computation.10 | async-start | bytes 3584000 | tf_op jit(solution)/shard_map/all_gather | solution.py:722
  83.5 30.1 %collective-permute-start.14 = (bf16[200,1536]{1,0:T(8,128)(2,1)}, bf16[200,1536]{1,0:T(8,128)(2,1)}, u32[]{:S(2)}, u32[]{:S(2)}) collective-permute-start(bf16[200,1536]{1,0:T(8,128)(2,1)} %get-tuple-element.281), channel_id=1, source_target_pairs={{0,2},{1,3},{2,0},{3,1},{4,6},{5,7},{6,4},{7,5},{8,10},{9,11},{10,... | collective-permute-start | bytes 1843208 | tf_op jit(solution)/shard_map/ppermute | solution.py:716
  85.0 28.6 %collective-permute-start.15 = (bf16[200,1536]{1,0:T(8,128)(2,1)}, bf16[200,1536]{1,0:T(8,128)(2,1)}, u32[]{:S(2)}, u32[]{:S(2)}) collective-permute-start(bf16[200,1536]{1,0:T(8,128)(2,1)} %get-tuple-element.282), channel_id=1, source_target_pairs={{0,4},{1,5},{2,6},{3,7},{4,0},{5,1},{6,2},{7,3},{8,12},{9,13},{10,... | collective-permute-start | bytes 1843208 | tf_op jit(solution)/shard_map/ppermute | solution.py:716
  85.5 37.4 %collective-permute-start.16 = (bf16[200,1536]{1,0:T(8,128)(2,1)}, bf16[200,1536]{1,0:T(8,128)(2,1)}, u32[]{:S(2)}, u32[]{:S(2)}) collective-permute-start(bf16[200,1536]{1,0:T(8,128)(2,1)} %get-tuple-element.283), channel_id=1, source_target_pairs={{0,6},{1,7},{2,4},{3,5},{4,2},{5,3},{6,0},{7,1},{8,14},{9,15},{10,... | collective-permute-start | bytes 1843208 | tf_op jit(solution)/shard_map/ppermute | solution.py:716
  97.6 28.9 %collective-permute-start.25 = (bf16[192,1600]{1,0:T(8,128)(2,1)}, bf16[192,1600]{1,0:T(8,128)(2,1)}, u32[]{:S(2)}, u32[]{:S(2)}) collective-permute-start(bf16[192,1600]{1,0:T(8,128)(2,1)} %get-tuple-element.548), channel_id=1, source_target_pairs={{0,1},{1,0},{2,3},{3,2},{4,5},{5,4},{6,7},{7,6},{8,9},{9,8},{10,11... | collective-permute-start | bytes 1843208 | tf_op jit(solution)/shard_map/ppermute | solution.py:716
  127.8 382.2 %reduce-scatter.7.cloned.1.call-start = ((), (), s32[]{:S(2)}) async-start(), calls=%async_computation.5 | async-start | bytes 3584000 | tf_op jit(solution)/shard_map/reduce_scatter | solution.py:725
  147.0 30.2 %collective-permute-start.26 = (bf16[2,192,1600]{2,1,0:T(8,128)(2,1)S(1)}, bf16[2,192,1600]{2,1,0:T(8,128)(2,1)S(1)}, u32[]{:S(2)}, u32[]{:S(2)}) collective-permute-start(bf16[2,192,1600]{2,1,0:T(8,128)(2,1)S(1)} %bitcast.72), channel_id=1, source_target_pairs={{0,2},{1,3},{2,0},{3,1},{4,6},{5,7},{6,4},{7,5},{8,10},{9,11},{10,... | collective-permute-start | bytes 3686408 | tf_op jit(solution)/shard_map/ppermute | solution.py:716
  147.9 29.9 %collective-permute-start.27 = (bf16[2,192,1600]{2,1,0:T(8,128)(2,1)S(1)}, bf16[2,192,1600]{2,1,0:T(8,128)(2,1)}, u32[]{:S(2)}, u32[]{:S(2)}) collective-permute-start(bf16[2,192,1600]{2,1,0:T(8,128)(2,1)S(1)} %bitcast.73), channel_id=1, source_target_pairs={{0,4},{1,5},{2,6},{3,7},{4,0},{5,1},{6,2},{7,3},{8,12},{9,13},{10,... | collective-permute-start | bytes 3686408 | tf_op jit(solution)/shard_map/ppermute | solution.py:716
  205.0 32.2 %collective-permute-start.37 = (bf16[1600,896]{1,0:T(8,128)(2,1)}, bf16[1600,896]{1,0:T(8,128)(2,1)}, u32[]{:S(2)}, u32[]{:S(2)}) collective-permute-start(bf16[1600,896]{1,0:T(8,128)(2,1)} %all-gather.11.cloned.1.call-done.refs_3_.refs_5_), channel_id=1, source_target_pairs={{0,1},{1,0},{2,3},{3,2},{4,5},{5,4},{6,7},{7,6},{8,9},{9,8},{10,11... | collective-permute-start | bytes 8601608 | tf_op jit(solution)/shard_map/ppermute | solution.py:716
  261.7 38.1 %collective-permute-start.43 = (bf16[192,1600]{1,0:T(8,128)(2,1)}, bf16[192,1600]{1,0:T(8,128)(2,1)}, u32[]{:S(2)}, u32[]{:S(2)}) collective-permute-start(bf16[192,1600]{1,0:T(8,128)(2,1)} %slice.152), channel_id=1, source_target_pairs={{0,2},{1,3},{2,0},{3,1},{4,6},{5,7},{6,4},{7,5},{8,10},{9,11},{10,... | collective-permute-start | bytes 1843208 | tf_op jit(solution)/shard_map/ppermute | solution.py:716
  262.9 37.0 %collective-permute-start.42 = (bf16[192,1600]{1,0:T(8,128)(2,1)}, bf16[192,1600]{1,0:T(8,128)(2,1)}, u32[]{:S(2)}, u32[]{:S(2)}) collective-permute-start(bf16[192,1600]{1,0:T(8,128)(2,1)} %slice.151), channel_id=1, source_target_pairs={{0,4},{1,5},{2,6},{3,7},{4,0},{5,1},{6,2},{7,3},{8,12},{9,13},{10,... | collective-permute-start | bytes 1843208 | tf_op jit(solution)/shard_map/ppermute | solution.py:716
  264.6 35.3 %collective-permute-start.40 = (bf16[192,1600]{1,0:T(8,128)(2,1)}, bf16[192,1600]{1,0:T(8,128)(2,1)S(1)}, u32[]{:S(2)}, u32[]{:S(2)}) collective-permute-start(bf16[192,1600]{1,0:T(8,128)(2,1)} %slice.149), channel_id=1, source_target_pairs={{0,4},{1,5},{2,6},{3,7},{4,0},{5,1},{6,2},{7,3},{8,12},{9,13},{10,... | collective-permute-start | bytes 1843208 | tf_op jit(solution)/shard_map/ppermute | solution.py:716
  264.9 35.0 %collective-permute-start.41 = (bf16[192,1600]{1,0:T(8,128)(2,1)}, bf16[192,1600]{1,0:T(8,128)(2,1)}, u32[]{:S(2)}, u32[]{:S(2)}) collective-permute-start(bf16[192,1600]{1,0:T(8,128)(2,1)} %slice.150), channel_id=1, source_target_pairs={{0,2},{1,3},{2,0},{3,1},{4,6},{5,7},{6,4},{7,5},{8,10},{9,11},{10,... | collective-permute-start | bytes 1843208 | tf_op jit(solution)/shard_map/ppermute | solution.py:716
  375.0 135.0 %reduce-scatter.5.cloned.1.call-start = ((), (), s32[]{:S(2)}) async-start(), calls=%async_computation.4 | async-start | bytes 3727360 | tf_op jit(solution)/shard_map/reduce_scatter | solution.py:725
  375.1 35.2 %collective-permute-start.51 = (bf16[2,448,1600]{2,1,0:T(8,128)(2,1)}, bf16[2,448,1600]{2,1,0:T(8,128)(2,1)}, u32[]{:S(2)}, u32[]{:S(2)}) collective-permute-start(bf16[2,448,1600]{2,1,0:T(8,128)(2,1)} %bitcast.102), channel_id=1, source_target_pairs={{0,1},{1,0},{2,3},{3,2},{4,5},{5,4},{6,7},{7,6},{8,9},{9,8},{10,11... | collective-permute-start | bytes 8601608 | tf_op jit(solution)/shard_map/ppermute | solution.py:716
  375.7 29.3 %collective-permute-start.55 = (bf16[192,1600]{1,0:T(8,128)(2,1)}, bf16[192,1600]{1,0:T(8,128)(2,1)}, u32[]{:S(2)}, u32[]{:S(2)}) collective-permute-start(bf16[192,1600]{1,0:T(8,128)(2,1)} %get-tuple-element.400), channel_id=1, source_target_pairs={{0,2},{1,3},{2,0},{3,1},{4,6},{5,7},{6,4},{7,5},{8,10},{9,11},{10,... | collective-permute-start | bytes 1843208 | tf_op jit(solution)/shard_map/ppermute | solution.py:716
  414.7 211.4 %reduce-scatter.11.cloned.1.call-start = ((), (), s32[]{:S(2)}) async-start(), calls=%async_computation.7 | async-start | bytes 1024000 | tf_op jit(solution)/shard_map/reduce_scatter | solution.py:725
  420.5 31.9 %collective-permute-start.60 = (bf16[200,1600]{1,0:T(8,128)(2,1)}, bf16[200,1600]{1,0:T(8,128)(2,1)S(1)}, u32[]{:S(2)}, u32[]{:S(2)}) collective-permute-start(bf16[200,1600]{1,0:T(8,128)(2,1)} %get-tuple-element.419), channel_id=1, source_target_pairs={{0,6},{1,7},{2,4},{3,5},{4,2},{5,3},{6,0},{7,1},{8,14},{9,15},{10,... | collective-permute-start | bytes 1920008 | tf_op jit(solution)/shard_map/ppermute | solution.py:716
  421.5 31.2 %collective-permute-start.59 = (bf16[200,1600]{1,0:T(8,128)(2,1)}, bf16[200,1600]{1,0:T(8,128)(2,1)S(1)}, u32[]{:S(2)}, u32[]{:S(2)}) collective-permute-start(bf16[200,1600]{1,0:T(8,128)(2,1)} %get-tuple-element.417), channel_id=1, source_target_pairs={{0,4},{1,5},{2,6},{3,7},{4,0},{5,1},{6,2},{7,3},{8,12},{9,13},{10,... | collective-permute-start | bytes 1920008 | tf_op jit(solution)/shard_map/ppermute | solution.py:716
  422.8 29.9 %collective-permute-start.58 = (bf16[200,1600]{1,0:T(8,128)(2,1)}, bf16[200,1600]{1,0:T(8,128)(2,1)S(1)}, u32[]{:S(2)}, u32[]{:S(2)}) collective-permute-start(bf16[200,1600]{1,0:T(8,128)(2,1)} %get-tuple-element.415), channel_id=1, source_target_pairs={{0,2},{1,3},{2,0},{3,1},{4,6},{5,7},{6,4},{7,5},{8,10},{9,11},{10,... | collective-permute-start | bytes 1920008 | tf_op jit(solution)/shard_map/ppermute | solution.py:716
  505.0 134.8 %reduce-scatter.9.cloned.1.call-start = ((), (), s32[]{:S(2)}) async-start(), calls=%async_computation.6 | async-start | bytes 2560000 | tf_op jit(solution)/shard_map/reduce_scatter | solution.py:725
  514.6 33.4 %collective-permute-start.67 = (bf16[2,200,400]{2,1,0:T(8,128)(2,1)}, bf16[2,200,400]{2,1,0:T(8,128)(2,1)S(1)}, u32[]{:S(2)}, u32[]{:S(2)}) collective-permute-start(bf16[2,200,400]{2,1,0:T(8,128)(2,1)} %get-tuple-element.460), channel_id=1, source_target_pairs={{0,2},{1,3},{2,0},{3,1},{4,6},{5,7},{6,4},{7,5},{8,10},{9,11},{10,... | collective-permute-start | bytes 960008 | tf_op jit(solution)/shard_map/ppermute | solution.py:716
  515.6 34.6 %collective-permute-start.68 = (bf16[2,200,400]{2,1,0:T(8,128)(2,1)}, bf16[2,200,400]{2,1,0:T(8,128)(2,1)}, u32[]{:S(2)}, u32[]{:S(2)}) collective-permute-start(bf16[2,200,400]{2,1,0:T(8,128)(2,1)} %get-tuple-element.461), channel_id=1, source_target_pairs={{0,4},{1,5},{2,6},{3,7},{4,0},{5,1},{6,2},{7,3},{8,12},{9,13},{10,... | collective-permute-start | bytes 960008 | tf_op jit(solution)/shard_map/ppermute | solution.py:716
  516.8 33.3 %collective-permute-start.69 = (bf16[2,200,400]{2,1,0:T(8,128)(2,1)}, bf16[2,200,400]{2,1,0:T(8,128)(2,1)}, u32[]{:S(2)}, u32[]{:S(2)}) collective-permute-start(bf16[2,200,400]{2,1,0:T(8,128)(2,1)} %get-tuple-element.462), channel_id=1, source_target_pairs={{0,6},{1,7},{2,4},{3,5},{4,2},{5,3},{6,0},{7,1},{8,14},{9,15},{10,... | collective-permute-start | bytes 960008 | tf_op jit(solution)/shard_map/ppermute | solution.py:716
  524.6 41.0 %collective-permute-start.72 = (bf16[200,1536]{1,0:T(8,128)(2,1)}, bf16[200,1536]{1,0:T(8,128)(2,1)S(1)}, u32[]{:S(2)}, u32[]{:S(2)}) collective-permute-start(bf16[200,1536]{1,0:T(8,128)(2,1)} %get-tuple-element.482), channel_id=1, source_target_pairs={{0,2},{1,3},{2,0},{3,1},{4,6},{5,7},{6,4},{7,5},{8,10},{9,11},{10,... | collective-permute-start | bytes 1843208 | tf_op jit(solution)/shard_map/ppermute | solution.py:716
  525.5 40.0 %collective-permute-start.73 = (bf16[200,1536]{1,0:T(8,128)(2,1)}, bf16[200,1536]{1,0:T(8,128)(2,1)S(1)}, u32[]{:S(2)}, u32[]{:S(2)}) collective-permute-start(bf16[200,1536]{1,0:T(8,128)(2,1)} %get-tuple-element.483), channel_id=1, source_target_pairs={{0,4},{1,5},{2,6},{3,7},{4,0},{5,1},{6,2},{7,3},{8,12},{9,13},{10,... | collective-permute-start | bytes 1843208 | tf_op jit(solution)/shard_map/ppermute | solution.py:716
  (136 other events, 1691.6 us)
Sparse Core Ops, SparseCore 0:
  10.2 58.1 all-gather.6
  80.2 61.1 all-gather.8
  143.5 57.5 all-gather.10
  375.1 56.0 reduce-scatter.6
  433.4 57.5 reduce-scatter.4
  505.1 23.9 reduce-scatter.10
  583.9 43.8 reduce-scatter.8

commit v4 on v3

--- a/solution.py
+++ b/solution.py
@@ -8,7 +8,7 @@
 from jax.sharding import PartitionSpec as P
 
 HEADS = 25
-COST = 0.25
+COST = 0.12
 LANES = 128
 CHUNK = 256
 QUERY_ROWS = 384
@@ -417,7 +417,7 @@
 
 def merge_norm_kernel(at_ref, *refs, count, rows, span, share, dim, parts):
     att_refs, part_refs = refs[: 2 * count], refs[2 * count : 2 * count + parts]
-    x_ref, vec_ref, hid_ref, s_ref, merge_ref, xs, buf, wide = refs[2 * count + parts :]
+    x_ref, vec_ref, hid_ref, s0_ref, s1_ref, merge_ref, xs, buf, wide = refs[2 * count + parts :]
     core, team = at_ref[0] % 2, at_ref[0] // 2
     place_rows(at_ref[0], part_refs, wide, merge_ref)
     pair_rows([x_ref], core, rows, xs)
@@ -434,19 +434,16 @@
     hid_ref[...] = hidden
     normal, _ = norm_parts(hidden)
     buf[...] = (normal * vec_ref[5:6, :] + vec_ref[6:7, :]).astype(LOW)
-    s_ref[:rows, :] = buf[row_slot(0, core, rows), :]
-    s_ref[rows:, :] = buf[row_slot(1, core, rows), :]
-
-
-def feed_kernel(sizes, out_sizes, at_ref, *refs):
+    s0_ref[...] = buf[row_slot(0, core, rows), :]
+    s1_ref[...] = buf[row_slot(1, core, rows), :]
+
+
+def feed_kernel(rows, sizes, out_sizes, at_ref, *refs):
     pieces, count = len(sizes), len(out_sizes)
     lows = [sum(sizes[:i]) for i in range(pieces)]
-    sec_refs, g_refs = refs[:pieces], refs[pieces : 2 * pieces]
-    weights, (bias_ref, act_ref, dpre_ref, sum_ref) = (
-        refs[2 * pieces : 2 * pieces + 4],
-        refs[2 * pieces + 4 : 2 * pieces + 8],
-    )
-    rest = refs[2 * pieces + 8 :]
+    halves = sum(sizes) // rows
+    sec_refs, g_refs, refs = refs[:halves], refs[halves : halves + pieces], refs[halves + pieces :]
+    weights, (bias_ref, act_ref, dpre_ref, sum_ref), rest = refs[:4], refs[4:8], refs[8:]
     ds_refs, out_refs = rest[:count], rest[count : 2 * count]
     sec, g, acc_s, acc_o, e_held, s_held, sems = rest[2 * count :]
     step = pl.program_id(0)
@@ -459,8 +456,9 @@
     def _():
         for copy in copies:
             copy.start()
+        for i in range(halves):
+            sec[i * rows : (i + 1) * rows, :] = sec_refs[i][...]
         for i in range(pieces):
-            sec[lows[i] : lows[i] + sizes[i], :] = sec_refs[i][...]
             g[lows[i] : lows[i] + sizes[i], :] = g_refs[i][...]
         copies[0].wait()
         copies[1].wait()
@@ -911,6 +909,8 @@
     vec_spec = fixed((8, width))
     mix_spec = fixed((width, 3 * span))
     team_rows = lambda n: pl.BlockSpec((own_rows, n), lambda k, a: (k ^ (a[0] // 2), 0))
+    kept, moved = meet((*cuts, merge_rows), x_pieces[3:])
+    cuts, merge_rows, x_pieces = kept[:-1], kept[-1], [*x_near, *moved]
     x_sizes = [v.shape[0] for v in x_pieces]
     row_specs = lambda sizes: [fixed((n, width)) for n in sizes]
     first, first_t = call(
@@ -1019,11 +1019,11 @@
     wide = ((own_rows, width), FULL)
     wide_low = ((own_rows, width), LOW)
     piece = ((rows, width), LOW)
-    hidden, second, merge = simple(
+    hidden, *second, merge = simple(
         merge_norm_kernel,
         "merge_norm",
         (*attended, *merge, x_own, vec),
-        [wide, wide_low, (merge_shape, LOW)],
+        [wide, piece, piece, (merge_shape, LOW)],
         [wide_low, wide_low, (merge_shape, FULL)],
         2 * own_rows * width * span * teams,
         count=teams,
@@ -1033,7 +1033,8 @@
         dim=dim,
         parts=len(merge),
     )
-    second = gather_near(second)
+    near = [hop(v, 2 * k) for k in range(1, teams) if teams != 4 or k < 3 for v in second]
+    second = [*second, *near]
     g_pieces = g_near
 
     e_row = e_bias.reshape(dp_n, teams, 2, hr).transpose(1, 2, 0, 3)
@@ -1042,19 +1043,21 @@
     e_row = jnp.pad(e_row, ((0, 0), (0, 0), (0, hp - hr))).reshape(1, units)
 
     groups = [[0], [1, 2], [3, 4]] if teams == 4 else [[k] for k in range(teams)]
+    halves = [[0, 1], [2, 3, 4, 5], [6, 7]] if teams == 4 else [[2 * k, 2 * k + 1] for k in range(teams)]
     acts, d_pres, e_sums, d_second, out = [], [], [], [], []
-    for group in groups:
+    for group, halved in zip(groups, halves):
         sizes = [x_sizes[i] for i in group]
         out_sizes = sizes if len(sizes) == 1 else [rows] * (sum(sizes) // rows)
         n, m = len(out_sizes), sum(sizes)
         half_spec = pl.BlockSpec((m, half), lambda f, a: (0, f))
         res = call(
-            functools.partial(feed_kernel, sizes, out_sizes),
+            functools.partial(feed_kernel, rows, sizes, out_sizes),
             "feed",
             (2,),
             at,
-            (*[second[i] for i in group], *[g_pieces[i] for i in group], *weights, e_row),
-            row_specs(sizes) * 2
+            (*[second[i] for i in halved], *[g_pieces[i] for i in group], *weights, e_row),
+            [piece_spec] * len(halved)
+            + row_specs(sizes)
             + [pl.BlockSpec(memory_space=pl.ANY)] * 4
             + [pl.BlockSpec((1, half), lambda f, a: (0, f))],
             [((m, units), LOW)] * 2
@@ -1075,12 +1078,14 @@
             after=tuple(acts[-1:]),
         )
         if len(acts) == 0:
-            res, moved = meet(res, second[1:])
-            second = gather_far([second[0], *moved])
+            res, moved = meet(res, second[2:])
+            second = [*second[:2], *moved]
+            if teams == 4:
+                second += [hop(moved[0], 4), hop(moved[3], 2)]
             g_pieces = gather_far(g_pieces, *moved)
         elif len(acts) == 1 and teams == 4:
-            res, moved = meet(res, (*second[3:], *g_pieces[3:]))
-            second, g_pieces = [*second[:3], *moved[:2]], [*g_pieces[:3], *moved[2:]]
+            res, moved = meet(res, (*second[6:], *g_pieces[3:]))
+            second, g_pieces = [*second[:6], *moved[:2]], [*g_pieces[:3], *moved[2:]]
             early = reduce_early([None, *res[3 : 3 + n]])
         elif teams == 4:
             res, early = meet(res, early)
@@ -1094,19 +1099,19 @@
     def feed_grad(name, parts, units_of, turned, after):
         shape = (width, half) if turned else (half, width)
         return call(
-            functools.partial(feed_grad_kernel, x_sizes, sizes, turned),
+            functools.partial(feed_grad_kernel, [v.shape[0] for v in parts], sizes, turned),
             name,
             (2,),
             at,
             (*parts, *units_of),
-            [pl.BlockSpec(memory_space=pl.ANY)] * len(x_sizes)
+            [pl.BlockSpec(memory_space=pl.ANY)] * len(parts)
             + [pl.BlockSpec((s, half), lambda f, a: (0, 1 - f)) for s in sizes],
             [(shape, LOW)] * 2,
             [fixed(shape)] * 2,
             [
                 pltpu.VMEM((length, width), LOW),
                 pltpu.VMEM((length, half), LOW),
-                pltpu.SemaphoreType.DMA((len(x_sizes),)),
+                pltpu.SemaphoreType.DMA((len(parts),)),
             ],
             2 * length * width * units,
             2 * act_bytes + 2 * width * units,

time: 659 us -> 655 us (level)
    ppermute x85 -> x87, waiting for transfers between devices: 112 us -> 108 us  [hop(): lax.ppermute(v, 'seq', [(i, i ^ mask) for i in range(seq_n)]).reshape(shape)]
    ppermute x85 -> x87, starting transfers between devices: 72.8 us -> 75.9 us  [hop(): lax.ppermute(v, 'seq', [(i, i ^ mask) for i in range(seq_n)]).reshape(shape)]
    unnamed x152 -> x150, local copies, waits for them, and re-layouts: 15.9 us -> 15.1 us
  transfers between devices with their start and end apart: 94 -> 96, of which waited for: 41 -> 39; matrix products, arithmetic and copies ran while one was open for 6% -> 6% of each run, Pallas kernels for 56% -> 56%
where the time goes in v4:
time: 655 us; the launch traced here: 645 us
  Pallas kernels  372 us (57%)
  waiting for transfers between devices  117 us (18%)
  starting transfers between devices  78.3 us (12%)
  local copies, waits for them, and re-layouts  31.3 us (5%)
  other arithmetic  28.7 us (4%)
  between operations  17.7 us (3%)
    pallas_call x33, Pallas kernels, call(): pl.pallas_call(kernel, grid_spec=spec, out_shape=[jax.ShapeDtypeStruct(s,...  372 us
    ppermute x87, waiting for transfers between devices, hop(): lax.ppermute(v, 'seq', [(i, i ^ mask) for i in range(seq_n)]).reshape(shape)  108 us
    ppermute x87, starting transfers between devices, hop(): lax.ppermute(v, 'seq', [(i, i ^ mask) for i in range(seq_n)]).reshape(shape)  75.9 us
    unnamed x150, local copies, waits for them, and re-layouts  15.1 us
  transfers between devices with their start and end apart: 96, of which 39 were waited for; matrix products, arithmetic and copies ran while one was open for 6% of the time, Pallas kernels for 56%

profile of v4, /device:TPU:0, one launch (start us, length us, event | category | flops | bytes accessed | tf_op | source)
XLA Modules:
  0.0 645.2 jit_solution(8154028763125864300)
XLA Ops:
  45.2 18.0 %collective-permute-done.2.refs_2_.refs_1_ = bf16[2,200,400]{2,1,0:T(8,128)(2,1)S(1)} collective-permute-done((bf16[2,200,400]{2,1,0:T(8,128)(2,1)}, bf16[2,200,400]{2,1,0:T(8,128)(2,1)S(1)}, u32[]{:S(2)}, u32[]{:S(2)}) %collective-permute-start.2) | collective-permute-done | bytes 320032 | tf_op jit(solution)/shard_map/ppermute | solution.py:714
  63.2 7.4 %collective-permute-done.3.refs_3_.refs_2_ = bf16[2,200,400]{2,1,0:T(8,128)(2,1)} collective-permute-done((bf16[2,200,400]{2,1,0:T(8,128)(2,1)}, bf16[2,200,400]{2,1,0:T(8,128)(2,1)}, u32[]{:S(2)}, u32[]{:S(2)}) %collective-permute-start.3) | collective-permute-done | bytes 320032 | tf_op jit(solution)/shard_map/ppermute | solution.py:714
  70.6 5.4 cut_mix.1
  83.5 10.6 %collective-permute-done.11.refs_3_.refs_2_ = bf16[192,1600]{1,0:T(8,128)(2,1)S(1)} collective-permute-done((bf16[192,1600]{1,0:T(8,128)(2,1)S(1)}, bf16[192,1600]{1,0:T(8,128)(2,1)S(1)}, u32[]{:S(2)}, u32[]{:S(2)}) %collective-permute-start.11) | collective-permute-done | bytes 614432 | tf_op jit(solution)/shard_map/ppermute | solution.py:714
  103.6 9.6 %norm.1 = (bf16[1536,1600]{1,0:T(8,128)(2,1)}, bf16[1600,1536]{1,0:T(8,128)(2,1)}) custom-call(s32[5]{0:T(128)} %pad_add_fusion.at_ref, bf16[384,1600]{1,0:T(8,128)(2,1)} %copy-done.2, bf16[384,1600]{1,0:T(8,128)(2,1)} %bitcast.75, bf16[384,1600]{1,0:T(8,128)(2,1)} %bitcast.7.refs_2_.refs_3_, bf16[192,1600]{1,0:T(8,128)(2,1)} %copy-done.16, ...), custom_call_target="tpu_custom_call" | custom-call | flops 2949120 | bytes 1179648 | tf_op jit(solution)/shard_map/norm/pallas_call | solution.py:70
  113.7 11.7 %collective-permute-done.15.refs_4_ = bf16[200,1536]{1,0:T(8,128)(2,1)} collective-permute-done((bf16[200,1536]{1,0:T(8,128)(2,1)}, bf16[200,1536]{1,0:T(8,128)(2,1)}, u32[]{:S(2)}, u32[]{:S(2)}) %collective-permute-start.15) | collective-permute-done | bytes 614432 | tf_op jit(solution)/shard_map/ppermute | solution.py:714
  131.7 16.3 %mix.1 = (bf16[1536,1536]{1,0:T(8,128)(2,1)}, bf16[1600,1536]{1,0:T(8,128)(2,1)}) custom-call(s32[5]{0:T(128)} %pad_add_fusion.at_ref, bf16[200,1536]{1,0:T(8,128)(2,1)} %get-tuple-element.292.refs_6_.refs_0_.refs_4_, bf16[200,1536]{1,0:T(8,128)(2,1)} %collective-permute-done.13.refs_1_, bf16[200,1536]{1,0:T(8,128)(2,1)} %collective-permute-done.14.refs_2_, ...), custom_call_target="tpu_custom_call" | custom-call | flops 905969664 | bytes 2359296 | tf_op jit(solution)/shard_map/mix/pallas_call | solution.py:70
  152.3 19.7 %attend_forward.2 = (bf16[384,256]{1,0:T(8,128)(2,1)}, bf16[384,256]{1,0:T(8,128)(2,1)}, bf16[384,256]{1,0:T(8,128)(2,1)}, bf16[384,256]{1,0:T(8,128)(2,1)}, f32[1536,256]{1,0:T(8,128)}) custom-call(s32[5]{0:T(128)} %pad_add_fusion.at_ref, bf16[1536,1536]{1,0:T(8,128)(2,1)} %get-tuple-element.309.refs_0_.refs_1_.refs_2_.refs_11_, ...), custom_call_target="tpu_custom_call" | custom-call | flops 253671504 | bytes 377487 | tf_op jit(solution)/shard_map/attend_forward/pallas_call | solution.py:70
  172.0 6.2 collective-permute-done.26
  183.5 15.6 %attend_forward.3 = (bf16[384,256]{1,0:T(8,128)(2,1)}, bf16[384,256]{1,0:T(8,128)(2,1)}, bf16[384,256]{1,0:T(8,128)(2,1)}, bf16[384,256]{1,0:T(8,128)(2,1)}, f32[1536,256]{1,0:T(8,128)}) custom-call(s32[5]{0:T(128)} %pad_add_fusion.at_ref, bf16[1536,1536]{1,0:T(8,128)(2,1)} %get-tuple-element.309.refs_0_.refs_1_.refs_2_.refs_11_, ...), custom_call_target="tpu_custom_call" | custom-call | flops 253671504 | bytes 377487 | tf_op jit(solution)/shard_map/attend_forward/pallas_call | solution.py:70
  199.1 6.1 collective-permute-done.30.refs_2_
  210.0 4.6 collective-permute-done.33.refs_5_
  218.3 13.3 %merge_norm.1 = (f32[384,1600]{1,0:T(8,128)}, bf16[192,1600]{1,0:T(8,128)(2,1)}, bf16[192,1600]{1,0:T(8,128)(2,1)}, bf16[1800,1600]{1,0:T(8,128)(2,1)}) custom-call(s32[5]{0:T(128)} %pad_add_fusion.at_ref, bf16[384,256]{1,0:T(8,128)(2,1)} %get-tuple-element.328.refs_5_.refs_0_, bf16[384,256]{1,0:T(8,128)(2,1)} %copy-done.26, bf16[384,256]{1,0:T(8,128)(2,1)} %copy-done.27, ...), custom_call_target="tpu_custom_call" | custom-call | flops 301989888 | bytes 2928967 | tf_op jit(solution)/shard_map/merge_norm/pallas_call | solution.py:70
  240.5 19.9 %feed.3 = (bf16[384,1792]{1,0:T(8,128)(2,1)}, bf16[384,1792]{1,0:T(8,128)(2,1)}, f32[8,1792]{1,0:T(8,128)}, bf16[384,1600]{1,0:T(8,128)(2,1)}, bf16[384,1600]{1,0:T(8,128)(2,1)}) custom-call(s32[5]{0:T(128)} %pad_add_fusion.at_ref, bf16[192,1600]{1,0:T(8,128)(2,1)} %get-tuple-element.340.refs_0_, bf16[192,1600]{1,0:T(8,128)(2,1)} %get-tuple-element.341.refs_1_, ...), custom_call_target="tpu_custom_call" | custom-call | flops 1056964608 | bytes 2260992 | tf_op jit(solution)/shard_map/feed/pallas_call | solution.py:70
  265.7 34.1 %feed.4 = (bf16[768,1792]{1,0:T(8,128)(2,1)}, bf16[768,1792]{1,0:T(8,128)(2,1)}, f32[8,1792]{1,0:T(8,128)}, bf16[192,1600]{1,0:T(8,128)(2,1)}, bf16[192,1600]{1,...) custom-call(s32[5]{0:T(128)} %pad_add_fusion.at_ref, ...), custom_call_target="tpu_custom_call" | custom-call | flops 2113929216 | bytes 3145728 | tf_op jit(solution)/shard_map/feed/pallas_call | solution.py:70
  302.1 20.2 %feed.5 = (bf16[384,1792]{1,0:T(8,128)(2,1)}, bf16[384,1792]{1,0:T(8,128)(2,1)}, f32[8,1792]{1,0:T(8,128)}, bf16[192,1600]{1,0:T(8,128)(2,1)}, bf16[192,1600]{1,...) custom-call(s32[5]{0:T(128)} %pad_add_fusion.at_ref, bf16[192,1600]{1,0:T(8,128)(2,1)} %copy-done.18, ...), custom_call_target="tpu_custom_call" | custom-call | flops 1056964608 | bytes 2260992 | tf_op jit(solution)/shard_map/feed/pallas_call | solution.py:70
  325.3 18.8 %shrink_grad.1 = (bf16[1600,896]{1,0:T(8,128)(2,1)}, bf16[1600,896]{1,0:T(8,128)(2,1)}) custom-call(s32[5]{0:T(128)} %pad_add_fusion.at_ref, bf16[384,1600]{1,0:T(8,128)(2,1)} %copy-done.4, bf16[384,1600]{1,0:T(8,128)(2,1)} %bitcast.73, bf16[384,1600]{1,0:T(8,128)(2,1)} %bitcast.15.refs_5_.refs_2_, ...), custom_call_target="tpu_custom_call" | custom-call | flops 1056964608 | bytes 1867776 | tf_op jit(solution)/shard_map/shrink_grad/pallas_call | solution.py:70
  350.8 18.8 %expand_grad.1 = (bf16[896,1600]{1,0:T(8,128)(2,1)}, bf16[896,1600]{1,0:T(8,128)(2,1)}) custom-call(s32[5]{0:T(128)} %pad_add_fusion.at_ref, bf16[192,1600]{1,0:T(8,128)(2,1)} %get-tuple-element.340.refs_0_, bf16[192,1600]{1,0:T(8,128)(2,1)} %get-tuple-element.341.refs_1_, bf16[192,1600]{1,0:T(8,128)(2,1)} %copy-done.11, bf16[192,1600]{1,0:T(8,128)(2,1)} %copy-done.13, ...), custom_call_target="tpu_custom_call" | custom-call | flops 1056964608 | bytes 1867776 | tf_op jit(solution)/shard_map/expand_grad/pallas_call | solution.py:70
  376.2 12.4 %second_back.1 = (f32[384,1600]{1,0:T(8,128)}, bf16[384,1600]{1,0:T(8,128)(2,1)}, f32[8,1600]{1,0:T(8,128)}, bf16[384,512]{1,0:T(8,128)(2,1)}, bf16[384,512]{1,0...) custom-call(s32[5]{0:T(128)} %pad_add_fusion.at_ref, bf16[384,1600]{1,0:T(8,128)(2,1)} %get-tuple-element.351.refs_0_, ...), custom_call_target="tpu_custom_call" | custom-call | flops 301989888 | bytes 2555535 | tf_op jit(solution)/shard_map/second_back/pallas_call | solution.py:70
  392.7 12.1 %merge_grad.1 = (bf16[4,200,1600]{2,1,0:T(8,128)(2,1)}, bf16[4,200,1600]{2,1,0:T(8,128)(2,1)}) custom-call(s32[5]{0:T(128)} %pad_add_fusion.at_ref, bf16[384,256]{1,0:T(8,128)(2,1)} %get-tuple-element.328.refs_5_.refs_0_, bf16[384,256]{1,0:T(8,128)(2,1)} %copy-done.26, bf16[384,256]{1,0:T(8,128)(2,1)} %copy-done.27, bf16[384,256]{1,0:T(8,128)(2,1)} %copy-done.28, ...), custom_call_target="tpu_custom_call" | custom-call | flops 301989888 | bytes 1564999 | tf_op jit(solution)/shard_map/merge_grad/pallas_call | solution.py:70
  414.7 4.9 add_parts.2
  423.1 28.4 %attend_backward.2.refs_10_.refs_0_ = bf16[3,1536,256]{2,1,0:T(8,128)(2,1)} custom-call(s32[5]{0:T(128)} %pad_add_fusion.at_ref, bf16[1536,1536]{1,0:T(8,128)(2,1)} %get-tuple-element.309.refs_0_.refs_1_.refs_2_.refs_11_, bf16[1536,1536]{1,0:T(8,128)(2,1)} %get-tuple-element.309.refs_0_.refs_1_.refs_2_.refs_11_, ...), custom_call_target="tpu_custom_call" | custom-call | flops 634178752 | bytes 754974 | tf_op jit(solution)/shard_map/attend_backward/pallas_call | solution.py:70
  453.9 22.6 %attend_backward.3.refs_1_ = bf16[3,1536,256]{2,1,0:T(8,128)(2,1)} custom-call(s32[5]{0:T(128)} %pad_add_fusion.at_ref, bf16[1536,1536]{1,0:T(8,128)(2,1)} %get-tuple-element.309.refs_0_.refs_1_.refs_2_.refs_11_, bf16[1536,1536]{1,0:T(8,128)(2,1)} %get-tuple-element.309.refs_0_.refs_1_.refs_2_.refs_11_, ...), custom_call_target="tpu_custom_call" | custom-call | flops 634178752 | bytes 754974 | tf_op jit(solution)/shard_map/attend_backward/pallas_call | solution.py:70
  483.9 13.2 %mix_grad.1 = (bf16[4,200,1536]{2,1,0:T(8,128)(2,1)}, bf16[4,200,1536]{2,1,0:T(8,128)(2,1)}, f32[8,1536]{1,0:T(8,128)}) custom-call(s32[5]{0:T(128)} %pad_add_fusion.at_ref, bf16[3,1536,256]{2,1,0:T(8,128)(2,1)} %attend_backward.2.refs_10_.refs_0_, bf16[3,1536,256]{2,1,0:T(8,128)(2,1)} %attend_backward.3.refs_1_, ...), custom_call_target="tpu_custom_call" | custom-call | flops 905969664 | bytes 1769472 | tf_op jit(solution)/shard_map/mix_grad/pallas_call | solution.py:70
  503.2 5.0 block_out.1
  518.8 5.1 add_parts.3
  525.8 8.2 %first_back.3 = (f32[8,1600]{1,0:T(8,128)}, bf16[192,1600]{1,0:T(8,128)(2,1)}, bf16[192,1600]{1,0:T(8,128)(2,1)}) custom-call(s32[5]{0:T(128)} %pad_add_fusion.at_ref, bf16[3,1536,256]{2,1,0:T(8,128)(2,1)} %attend_backward.2.refs_10_.refs_0_, bf16[3,1536,256]{2,1,0:T(8,128)(2,1)} %attend_backward.3.refs_1_, bf16[192,1600]{1,0:T(8,128)(2,1)} %copy-done.16, ...), custom_call_target="tpu_custom_call" | custom-call | flops 226492416 | bytes 589824 | tf_op jit(solution)/shard_map/first_back/pallas_call | solution.py:70
  537.5 13.0 %first_back.4 = (f32[8,1600]{1,0:T(8,128)}, bf16[192,1600]{1,0:T(8,128)(2,1)}, bf16[192,1600]{1,0:T(8,128)(2,1)}, bf16[192,1600]{1,0:T(8,128)(2,1)}, bf16[192,1600]{1,0:T(8,128)(2,1)}) custom-call(s32[5]{0:T(128)} %pad_add_fusion.at_ref, bf16[3,1536,256]{2,1,0:T(8,128)(2,1)} %attend_backward.2.refs_10_.refs_0_, ...), custom_call_target="tpu_custom_call" | custom-call | flops 452984832 | bytes 1179648 | tf_op jit(solution)/shard_map/first_back/pallas_call | solution.py:70
  550.5 8.4 %first_back.5 = (f32[8,1600]{1,0:T(8,128)}, bf16[384,1600]{1,0:T(8,128)(2,1)}) custom-call(s32[5]{0:T(128)} %pad_add_fusion.at_ref, bf16[3,1536,256]{2,1,0:T(8,128)(2,1)} %attend_backward.2.refs_10_.refs_0_, bf16[3,1536,256]{2,1,0:T(8,128)(2,1)} %attend_backward.3.refs_1_, bf16[384,1600]{1,0:T(8,128)(2,1)} %copy-done.2, ...), custom_call_target="tpu_custom_call" | custom-call | flops 226492416 | bytes 589824 | tf_op jit(solution)/shard_map/first_back/pallas_call | solution.py:70
  594.9 5.2 collective-permute-done.81
  608.0 4.8 collective-permute-done.84.refs_2_
  614.2 7.4 %input_grad.1 = (f32[192,1600]{1,0:T(8,128)}, f32[192,1600]{1,0:T(8,128)}) custom-call(s32[5]{0:T(128)} %pad_add_fusion.at_ref, bf16[384,1600]{1,0:T(8,128)(2,1)} %get-tuple-element.485.refs_0_, bf16[192,1600]{1,0:T(8,128)(2,1)} %copy-done.40, bf16[192,1600]{1,0:T(8,128)(2,1)} %copy-done.42, bf16[192,1600]{1,0:T(8,128)(2,1)} %copy-done.43, ...), custom_call_target="tpu_custom_call" | custom-call | bytes 1185792 | tf_op jit(solution)/shard_map/input_grad/pallas_call | solution.py:70
  (438 shorter events, 220.4 us)
Async XLA Ops:
  7.2 63.4 %all-gather.7.cloned.1.call-start = ((), (), s32[]{:S(2)}) async-start(), calls=%async_computation.8 | async-start | bytes 3328000 | tf_op jit(solution)/shard_map/all_gather | solution.py:720
  9.5 169.1 %all-gather.9.cloned.1.call-start = ((), (), s32[]{:S(2)}) async-start(), calls=%async_computation.9 | async-start | bytes 3727360 | tf_op jit(solution)/shard_map/all_gather | solution.py:720
  23.3 47.3 %collective-permute-start.9 = (bf16[2,192,1600]{2,1,0:T(8,128)(2,1)S(1)}, bf16[2,192,1600]{2,1,0:T(8,128)(2,1)S(1)}, u32[]{:S(2)}, u32[]{:S(2)}) collective-permute-start(bf16[2,192,1600]{2,1,0:T(8,128)(2,1)S(1)} %bitcast.61), channel_id=1, source_target_pairs={{0,2},{1,3},{2,0},{3,1},{4,6},{5,7},{6,4},{7,5},{8,10},{9,11},{10,... | collective-permute-start | bytes 3686408 | tf_op jit(solution)/shard_map/ppermute | solution.py:714
  25.4 45.2 %collective-permute-start.10 = (bf16[2,192,1600]{2,1,0:T(8,128)(2,1)S(1)}, bf16[2,192,1600]{2,1,0:T(8,128)(2,1)}, u32[]{:S(2)}, u32[]{:S(2)}) collective-permute-start(bf16[2,192,1600]{2,1,0:T(8,128)(2,1)S(1)} %bitcast.62), channel_id=1, source_target_pairs={{0,4},{1,5},{2,6},{3,7},{4,0},{5,1},{6,2},{7,3},{8,12},{9,13},{10,... | collective-permute-start | bytes 3686408 | tf_op jit(solution)/shard_map/ppermute | solution.py:714
  41.5 29.1 %collective-permute-start.3 = (bf16[2,200,400]{2,1,0:T(8,128)(2,1)}, bf16[2,200,400]{2,1,0:T(8,128)(2,1)}, u32[]{:S(2)}, u32[]{:S(2)}) collective-permute-start(bf16[2,200,400]{2,1,0:T(8,128)(2,1)} %get-tuple-element.278), channel_id=1, source_target_pairs={{0,4},{1,5},{2,6},{3,7},{4,0},{5,1},{6,2},{7,3},{8,12},{9,13},{10,... | collective-permute-start | bytes 960008 | tf_op jit(solution)/shard_map/ppermute | solution.py:714
  41.6 29.0 %collective-permute-start.4 = (bf16[2,200,400]{2,1,0:T(8,128)(2,1)}, bf16[2,200,400]{2,1,0:T(8,128)(2,1)}, u32[]{:S(2)}, u32[]{:S(2)}) collective-permute-start(bf16[2,200,400]{2,1,0:T(8,128)(2,1)} %get-tuple-element.279), channel_id=1, source_target_pairs={{0,6},{1,7},{2,4},{3,5},{4,2},{5,3},{6,0},{7,1},{8,14},{9,15},{10,... | collective-permute-start | bytes 960008 | tf_op jit(solution)/shard_map/ppermute | solution.py:714
  80.1 125.9 %all-gather.11.cloned.1.call-start = ((), (), s32[]{:S(2)}) async-start(), calls=%async_computation.10 | async-start | bytes 3584000 | tf_op jit(solution)/shard_map/all_gather | solution.py:720
  100.1 27.5 %collective-permute-start.25 = (bf16[192,1600]{1,0:T(8,128)(2,1)}, bf16[192,1600]{1,0:T(8,128)(2,1)}, u32[]{:S(2)}, u32[]{:S(2)}) collective-permute-start(bf16[192,1600]{1,0:T(8,128)(2,1)} %get-tuple-element.568), channel_id=1, source_target_pairs={{0,1},{1,0},{2,3},{3,2},{4,5},{5,4},{6,7},{7,6},{8,9},{9,8},{10,11... | collective-permute-start | bytes 1843208 | tf_op jit(solution)/shard_map/ppermute | solution.py:714
  100.1 28.0 %collective-permute-start.13 = (bf16[200,1536]{1,0:T(8,128)(2,1)S(1)}, bf16[200,1536]{1,0:T(8,128)(2,1)}, u32[]{:S(2)}, u32[]{:S(2)}) collective-permute-start(bf16[200,1536]{1,0:T(8,128)(2,1)S(1)} %copy-done.8), channel_id=1, source_target_pairs={{0,1},{1,0},{2,3},{3,2},{4,5},{5,4},{6,7},{7,6},{8,9},{9,8},{10,11... | collective-permute-start | bytes 1843208 | tf_op jit(solution)/shard_map/ppermute | solution.py:714
  128.8 379.4 %reduce-scatter.7.cloned.1.call-start = ((), (), s32[]{:S(2)}) async-start(), calls=%async_computation.5 | async-start | bytes 3584000 | tf_op jit(solution)/shard_map/reduce_scatter | solution.py:723
  148.0 30.2 %collective-permute-start.26 = (bf16[2,192,1600]{2,1,0:T(8,128)(2,1)S(1)}, bf16[2,192,1600]{2,1,0:T(8,128)(2,1)S(1)}, u32[]{:S(2)}, u32[]{:S(2)}) collective-permute-start(bf16[2,192,1600]{2,1,0:T(8,128)(2,1)S(1)} %bitcast.69), channel_id=1, source_target_pairs={{0,2},{1,3},{2,0},{3,1},{4,6},{5,7},{6,4},{7,5},{8,10},{9,11},{10,... | collective-permute-start | bytes 3686408 | tf_op jit(solution)/shard_map/ppermute | solution.py:714
  148.7 29.9 %collective-permute-start.27 = (bf16[2,192,1600]{2,1,0:T(8,128)(2,1)S(1)}, bf16[2,192,1600]{2,1,0:T(8,128)(2,1)}, u32[]{:S(2)}, u32[]{:S(2)}) collective-permute-start(bf16[2,192,1600]{2,1,0:T(8,128)(2,1)S(1)} %bitcast.70), channel_id=1, source_target_pairs={{0,4},{1,5},{2,6},{3,7},{4,0},{5,1},{6,2},{7,3},{8,12},{9,13},{10,... | collective-permute-start | bytes 3686408 | tf_op jit(solution)/shard_map/ppermute | solution.py:714
  206.0 34.6 %collective-permute-start.37 = (bf16[1600,896]{1,0:T(8,128)(2,1)}, bf16[1600,896]{1,0:T(8,128)(2,1)}, u32[]{:S(2)}, u32[]{:S(2)}) collective-permute-start(bf16[1600,896]{1,0:T(8,128)(2,1)} %all-gather.11.cloned.1.call-done.refs_4_.refs_7_.refs_5_), channel_id=1, source_target_pairs={{0,1},{1,0},{2,3},{3,2},{4,5},{5,4},{6,7},{7,6},{8,9},{9,8},{10,11... | collective-permute-start | bytes 8601608 | tf_op jit(solution)/shard_map/ppermute | solution.py:714
  231.6 28.7 %collective-permute-start.38 = (bf16[192,1600]{1,0:T(8,128)(2,1)}, bf16[192,1600]{1,0:T(8,128)(2,1)S(1)}, u32[]{:S(2)}, u32[]{:S(2)}) collective-permute-start(bf16[192,1600]{1,0:T(8,128)(2,1)} %get-tuple-element.340.refs_0_), channel_id=1, source_target_pairs={{0,2},{1,3},{2,0},{3,1},{4,6},{5,7},{6,4},{7,5},{8,10},{9,11},{10,... | collective-permute-start | bytes 1843208 | tf_op jit(solution)/shard_map/ppermute | solution.py:714
  232.9 27.7 %collective-permute-start.40 = (bf16[192,1600]{1,0:T(8,128)(2,1)}, bf16[192,1600]{1,0:T(8,128)(2,1)S(1)}, u32[]{:S(2)}, u32[]{:S(2)}) collective-permute-start(bf16[192,1600]{1,0:T(8,128)(2,1)} %get-tuple-element.340.refs_0_), channel_id=1, source_target_pairs={{0,4},{1,5},{2,6},{3,7},{4,0},{5,1},{6,2},{7,3},{8,12},{9,13},{10,... | collective-permute-start | bytes 1843208 | tf_op jit(solution)/shard_map/ppermute | solution.py:714
  261.6 38.2 %collective-permute-start.45 = (bf16[192,1600]{1,0:T(8,128)(2,1)}, bf16[192,1600]{1,0:T(8,128)(2,1)}, u32[]{:S(2)}, u32[]{:S(2)}) collective-permute-start(bf16[192,1600]{1,0:T(8,128)(2,1)} %slice.144), channel_id=1, source_target_pairs={{0,2},{1,3},{2,0},{3,1},{4,6},{5,7},{6,4},{7,5},{8,10},{9,11},{10,... | collective-permute-start | bytes 1843208 | tf_op jit(solution)/shard_map/ppermute | solution.py:714
  262.4 37.4 %collective-permute-start.44 = (bf16[192,1600]{1,0:T(8,128)(2,1)}, bf16[192,1600]{1,0:T(8,128)(2,1)}, u32[]{:S(2)}, u32[]{:S(2)}) collective-permute-start(bf16[192,1600]{1,0:T(8,128)(2,1)} %slice.143), channel_id=1, source_target_pairs={{0,4},{1,5},{2,6},{3,7},{4,0},{5,1},{6,2},{7,3},{8,12},{9,13},{10,... | collective-permute-start | bytes 1843208 | tf_op jit(solution)/shard_map/ppermute | solution.py:714
  263.8 36.1 %collective-permute-start.42 = (bf16[192,1600]{1,0:T(8,128)(2,1)S(1)}, bf16[192,1600]{1,0:T(8,128)(2,1)S(1)}, u32[]{:S(2)}, u32[]{:S(2)}) collective-permute-start(bf16[192,1600]{1,0:T(8,128)(2,1)S(1)} %collective-permute-done.38.refs_0_.refs_2_), channel_id=1, source_target_pairs={{0,4},{1,5},{2,6},{3,7},{4,0},{5,1},{6,2},{7,3},{8,12},{9,13},{10,... | collective-permute-start | bytes 1843208 | tf_op jit(solution)/shard_map/ppermute | solution.py:714
  264.4 35.4 %collective-permute-start.43 = (bf16[192,1600]{1,0:T(8,128)(2,1)S(1)}, bf16[192,1600]{1,0:T(8,128)(2,1)}, u32[]{:S(2)}, u32[]{:S(2)}) collective-permute-start(bf16[192,1600]{1,0:T(8,128)(2,1)S(1)} %collective-permute-done.41.refs_3_.refs_5_), channel_id=1, source_target_pairs={{0,2},{1,3},{2,0},{3,1},{4,6},{5,7},{6,4},{7,5},{8,10},{9,11},{10,... | collective-permute-start | bytes 1843208 | tf_op jit(solution)/shard_map/ppermute | solution.py:714
  374.1 134.1 %reduce-scatter.5.cloned.1.call-start = ((), (), s32[]{:S(2)}) async-start(), calls=%async_computation.4 | async-start | bytes 3727360 | tf_op jit(solution)/shard_map/reduce_scatter | solution.py:723
  374.2 35.2 %collective-permute-start.53 = (bf16[2,448,1600]{2,1,0:T(8,128)(2,1)}, bf16[2,448,1600]{2,1,0:T(8,128)(2,1)}, u32[]{:S(2)}, u32[]{:S(2)}) collective-permute-start(bf16[2,448,1600]{2,1,0:T(8,128)(2,1)} %bitcast.91), channel_id=1, source_target_pairs={{0,1},{1,0},{2,3},{3,2},{4,5},{5,4},{6,7},{7,6},{8,9},{9,8},{10,11... | collective-permute-start | bytes 8601608 | tf_op jit(solution)/shard_map/ppermute | solution.py:714
  375.1 29.7 %collective-permute-start.57 = (bf16[192,1600]{1,0:T(8,128)(2,1)}, bf16[192,1600]{1,0:T(8,128)(2,1)}, u32[]{:S(2)}, u32[]{:S(2)}) collective-permute-start(bf16[192,1600]{1,0:T(8,128)(2,1)} %get-tuple-element.420), channel_id=1, source_target_pairs={{0,2},{1,3},{2,0},{3,1},{4,6},{5,7},{6,4},{7,5},{8,10},{9,11},{10,... | collective-permute-start | bytes 1843208 | tf_op jit(solution)/shard_map/ppermute | solution.py:714
  413.8 208.4 %reduce-scatter.11.cloned.1.call-start = ((), (), s32[]{:S(2)}) async-start(), calls=%async_computation.7 | async-start | bytes 1024000 | tf_op jit(solution)/shard_map/reduce_scatter | solution.py:723
  419.6 31.9 %collective-permute-start.62 = (bf16[200,1600]{1,0:T(8,128)(2,1)}, bf16[200,1600]{1,0:T(8,128)(2,1)S(1)}, u32[]{:S(2)}, u32[]{:S(2)}) collective-permute-start(bf16[200,1600]{1,0:T(8,128)(2,1)} %get-tuple-element.439), channel_id=1, source_target_pairs={{0,6},{1,7},{2,4},{3,5},{4,2},{5,3},{6,0},{7,1},{8,14},{9,15},{10,... | collective-permute-start | bytes 1920008 | tf_op jit(solution)/shard_map/ppermute | solution.py:714
  420.9 31.0 %collective-permute-start.61 = (bf16[200,1600]{1,0:T(8,128)(2,1)}, bf16[200,1600]{1,0:T(8,128)(2,1)S(1)}, u32[]{:S(2)}, u32[]{:S(2)}) collective-permute-start(bf16[200,1600]{1,0:T(8,128)(2,1)} %get-tuple-element.437), channel_id=1, source_target_pairs={{0,4},{1,5},{2,6},{3,7},{4,0},{5,1},{6,2},{7,3},{8,12},{9,13},{10,... | collective-permute-start | bytes 1920008 | tf_op jit(solution)/shard_map/ppermute | solution.py:714
  421.9 30.1 %collective-permute-start.60 = (bf16[200,1600]{1,0:T(8,128)(2,1)}, bf16[200,1600]{1,0:T(8,128)(2,1)S(1)}, u32[]{:S(2)}, u32[]{:S(2)}) collective-permute-start(bf16[200,1600]{1,0:T(8,128)(2,1)} %get-tuple-element.435), channel_id=1, source_target_pairs={{0,2},{1,3},{2,0},{3,1},{4,6},{5,7},{6,4},{7,5},{8,10},{9,11},{10,... | collective-permute-start | bytes 1920008 | tf_op jit(solution)/shard_map/ppermute | solution.py:714
  517.3 118.6 %reduce-scatter.9.cloned.1.call-start = ((), (), s32[]{:S(2)}) async-start(), calls=%async_computation.6 | async-start | bytes 2560000 | tf_op jit(solution)/shard_map/reduce_scatter | solution.py:723
  523.8 40.0 %collective-permute-start.74 = (bf16[200,1536]{1,0:T(8,128)(2,1)}, bf16[200,1536]{1,0:T(8,128)(2,1)S(1)}, u32[]{:S(2)}, u32[]{:S(2)}) collective-permute-start(bf16[200,1536]{1,0:T(8,128)(2,1)} %get-tuple-element.502), channel_id=1, source_target_pairs={{0,2},{1,3},{2,0},{3,1},{4,6},{5,7},{6,4},{7,5},{8,10},{9,11},{10,... | collective-permute-start | bytes 1843208 | tf_op jit(solution)/shard_map/ppermute | solution.py:714
  525.0 38.9 %collective-permute-start.75 = (bf16[200,1536]{1,0:T(8,128)(2,1)}, bf16[200,1536]{1,0:T(8,128)(2,1)S(1)}, u32[]{:S(2)}, u32[]{:S(2)}) collective-permute-start(bf16[200,1536]{1,0:T(8,128)(2,1)} %get-tuple-element.503), channel_id=1, source_target_pairs={{0,4},{1,5},{2,6},{3,7},{4,0},{5,1},{6,2},{7,3},{8,12},{9,13},{10,... | collective-permute-start | bytes 1843208 | tf_op jit(solution)/shard_map/ppermute | solution.py:714
  534.0 29.8 %collective-permute-start.76 = (bf16[200,1536]{1,0:T(8,128)(2,1)}, bf16[200,1536]{1,0:T(8,128)(2,1)S(1)}, u32[]{:S(2)}, u32[]{:S(2)}) collective-permute-start(bf16[200,1536]{1,0:T(8,128)(2,1)} %get-tuple-element.504), channel_id=1, source_target_pairs={{0,6},{1,7},{2,4},{3,5},{4,2},{5,3},{6,0},{7,1},{8,14},{9,15},{10,... | collective-permute-start | bytes 1843208 | tf_op jit(solution)/shard_map/ppermute | solution.py:714
  535.6 38.2 %collective-permute-start.72 = (bf16[192,1600]{1,0:T(8,128)(2,1)}, bf16[192,1600]{1,0:T(8,128)(2,1)S(1)}, u32[]{:S(2)}, u32[]{:S(2)}) collective-permute-start(bf16[192,1600]{1,0:T(8,128)(2,1)} %get-tuple-element.483), channel_id=1, source_target_pairs={{0,2},{1,3},{2,0},{3,1},{4,6},{5,7},{6,4},{7,5},{8,10},{9,11},{10,... | collective-permute-start | bytes 1843208 | tf_op jit(solution)/shard_map/ppermute | solution.py:714
  536.7 37.8 %collective-permute-start.73 = (bf16[192,1600]{1,0:T(8,128)(2,1)}, bf16[192,1600]{1,0:T(8,128)(2,1)S(1)}, u32[]{:S(2)}, u32[]{:S(2)}) collective-permute-start(bf16[192,1600]{1,0:T(8,128)(2,1)} %get-tuple-element.484), channel_id=1, source_target_pairs={{0,4},{1,5},{2,6},{3,7},{4,0},{5,1},{6,2},{7,3},{8,12},{9,13},{10,... | collective-permute-start | bytes 1843208 | tf_op jit(solution)/shard_map/ppermute | solution.py:714
  (137 other events, 1724.1 us)
Sparse Core Ops, SparseCore 0:
  10.2 58.1 all-gather.6
  80.2 61.1 all-gather.8
  143.5 57.5 all-gather.10
  374.2 55.8 reduce-scatter.6
  432.2 57.5 reduce-scatter.4
  517.4 23.3 reduce-scatter.10
  580.0 43.2 reduce-scatter.8

commit v5 on v4

--- a/solution.py
+++ b/solution.py
@@ -1019,6 +1019,7 @@
     wide = ((own_rows, width), FULL)
     wide_low = ((own_rows, width), LOW)
     piece = ((rows, width), LOW)
+    g_half = [g_near[1][:rows], g_near[2][rows:]] if teams == 4 else []
     hidden, *second, merge = simple(
         merge_norm_kernel,
         "merge_norm",
@@ -1026,6 +1027,7 @@
         [wide, piece, piece, (merge_shape, LOW)],
         [wide_low, wide_low, (merge_shape, FULL)],
         2 * own_rows * width * span * teams,
+        after=tuple(g_half),
         count=teams,
         rows=rows,
         span=span,
@@ -1082,7 +1084,8 @@
             second = [*second[:2], *moved]
             if teams == 4:
                 second += [hop(moved[0], 4), hop(moved[3], 2)]
-            g_pieces = gather_far(g_pieces, *moved)
+                x, y = (tie(v, *moved) for v in g_half)
+                g_pieces = [*g_pieces, hop(x, 4), hop(y, 2)]
         elif len(acts) == 1 and teams == 4:
             res, moved = meet(res, (*second[6:], *g_pieces[3:]))
             second, g_pieces = [*second[:6], *moved[:2]], [*g_pieces[:3], *moved[2:]]

time: 655 us -> 655 us (level)
  no operation moved by 1% of the time
where the time goes in v5:
time: 655 us; the launch traced here: 645 us
  Pallas kernels  372 us (57%)
  waiting for transfers between devices  117 us (18%)
  starting transfers between devices  78.3 us (12%)
  local copies, waits for them, and re-layouts  31.2 us (5%)
  other arithmetic  28.7 us (4%)
  between operations  17.7 us (3%)
    pallas_call x33, Pallas kernels, call(): pl.pallas_call(kernel, grid_spec=spec, out_shape=[jax.ShapeDtypeStruct(s,...  372 us
    ppermute x87, waiting for transfers between devices, hop(): lax.ppermute(v, 'seq', [(i, i ^ mask) for i in range(seq_n)]).reshape(shape)  108 us
    ppermute x87, starting transfers between devices, hop(): lax.ppermute(v, 'seq', [(i, i ^ mask) for i in range(seq_n)]).reshape(shape)  75.9 us
    unnamed x150, local copies, waits for them, and re-layouts  15 us
  transfers between devices with their start and end apart: 96, of which 39 were waited for; matrix products, arithmetic and copies ran while one was open for 6% of the time, Pallas kernels for 56%

profile of v5, /device:TPU:0, one launch (start us, length us, event | category | flops | bytes accessed | tf_op | source)
XLA Modules:
  0.0 645.0 jit_solution(4777089696745791665)
XLA Ops:
  45.2 18.0 %collective-permute-done.2.refs_2_.refs_1_ = bf16[2,200,400]{2,1,0:T(8,128)(2,1)S(1)} collective-permute-done((bf16[2,200,400]{2,1,0:T(8,128)(2,1)}, bf16[2,200,400]{2,1,0:T(8,128)(2,1)S(1)}, u32[]{:S(2)}, u32[]{:S(2)}) %collective-permute-start.2) | collective-permute-done | bytes 320032 | tf_op jit(solution)/shard_map/ppermute | solution.py:714
  63.2 7.4 %collective-permute-done.3.refs_3_.refs_2_ = bf16[2,200,400]{2,1,0:T(8,128)(2,1)} collective-permute-done((bf16[2,200,400]{2,1,0:T(8,128)(2,1)}, bf16[2,200,400]{2,1,0:T(8,128)(2,1)}, u32[]{:S(2)}, u32[]{:S(2)}) %collective-permute-start.3) | collective-permute-done | bytes 320032 | tf_op jit(solution)/shard_map/ppermute | solution.py:714
  70.6 5.4 cut_mix.1
  83.5 10.6 %collective-permute-done.11.refs_3_.refs_2_ = bf16[192,1600]{1,0:T(8,128)(2,1)S(1)} collective-permute-done((bf16[192,1600]{1,0:T(8,128)(2,1)S(1)}, bf16[192,1600]{1,0:T(8,128)(2,1)S(1)}, u32[]{:S(2)}, u32[]{:S(2)}) %collective-permute-start.11) | collective-permute-done | bytes 614432 | tf_op jit(solution)/shard_map/ppermute | solution.py:714
  103.6 9.6 %norm.1 = (bf16[1536,1600]{1,0:T(8,128)(2,1)}, bf16[1600,1536]{1,0:T(8,128)(2,1)}) custom-call(s32[5]{0:T(128)} %pad_add_fusion.at_ref, bf16[384,1600]{1,0:T(8,128)(2,1)} %copy-done.2, bf16[384,1600]{1,0:T(8,128)(2,1)} %bitcast.75, bf16[384,1600]{1,0:T(8,128)(2,1)} %bitcast.7.refs_2_.refs_3_, bf16[192,1600]{1,0:T(8,128)(2,1)} %copy-done.17, ...), custom_call_target="tpu_custom_call" | custom-call | flops 2949120 | bytes 1179648 | tf_op jit(solution)/shard_map/norm/pallas_call | solution.py:70
  113.7 11.7 %collective-permute-done.15.refs_4_ = bf16[200,1536]{1,0:T(8,128)(2,1)} collective-permute-done((bf16[200,1536]{1,0:T(8,128)(2,1)}, bf16[200,1536]{1,0:T(8,128)(2,1)}, u32[]{:S(2)}, u32[]{:S(2)}) %collective-permute-start.15) | collective-permute-done | bytes 614432 | tf_op jit(solution)/shard_map/ppermute | solution.py:714
  131.7 16.3 %mix.1 = (bf16[1536,1536]{1,0:T(8,128)(2,1)}, bf16[1600,1536]{1,0:T(8,128)(2,1)}) custom-call(s32[5]{0:T(128)} %pad_add_fusion.at_ref, bf16[200,1536]{1,0:T(8,128)(2,1)} %get-tuple-element.292.refs_6_.refs_0_.refs_4_, bf16[200,1536]{1,0:T(8,128)(2,1)} %collective-permute-done.13.refs_1_, bf16[200,1536]{1,0:T(8,128)(2,1)} %collective-permute-done.14.refs_2_, ...), custom_call_target="tpu_custom_call" | custom-call | flops 905969664 | bytes 2359296 | tf_op jit(solution)/shard_map/mix/pallas_call | solution.py:70
  152.3 19.7 %attend_forward.2 = (bf16[384,256]{1,0:T(8,128)(2,1)}, bf16[384,256]{1,0:T(8,128)(2,1)}, bf16[384,256]{1,0:T(8,128)(2,1)}, bf16[384,256]{1,0:T(8,128)(2,1)}, f32[1536,256]{1,0:T(8,128)}) custom-call(s32[5]{0:T(128)} %pad_add_fusion.at_ref, bf16[1536,1536]{1,0:T(8,128)(2,1)} %get-tuple-element.309.refs_0_.refs_1_.refs_2_.refs_11_, ...), custom_call_target="tpu_custom_call" | custom-call | flops 253671504 | bytes 377487 | tf_op jit(solution)/shard_map/attend_forward/pallas_call | solution.py:70
  172.0 6.2 collective-permute-done.26
  183.5 15.6 %attend_forward.3 = (bf16[384,256]{1,0:T(8,128)(2,1)}, bf16[384,256]{1,0:T(8,128)(2,1)}, bf16[384,256]{1,0:T(8,128)(2,1)}, bf16[384,256]{1,0:T(8,128)(2,1)}, f32[1536,256]{1,0:T(8,128)}) custom-call(s32[5]{0:T(128)} %pad_add_fusion.at_ref, bf16[1536,1536]{1,0:T(8,128)(2,1)} %get-tuple-element.309.refs_0_.refs_1_.refs_2_.refs_11_, ...), custom_call_target="tpu_custom_call" | custom-call | flops 253671504 | bytes 377487 | tf_op jit(solution)/shard_map/attend_forward/pallas_call | solution.py:70
  199.1 6.1 collective-permute-done.30.refs_2_
  218.3 13.3 %merge_norm.1 = (f32[384,1600]{1,0:T(8,128)}, bf16[192,1600]{1,0:T(8,128)(2,1)}, bf16[192,1600]{1,0:T(8,128)(2,1)}, bf16[1800,1600]{1,0:T(8,128)(2,1)}) custom-call(s32[5]{0:T(128)} %pad_add_fusion.at_ref, bf16[384,256]{1,0:T(8,128)(2,1)} %get-tuple-element.328.refs_5_.refs_0_, bf16[384,256]{1,0:T(8,128)(2,1)} %copy-done.26, bf16[384,256]{1,0:T(8,128)(2,1)} %copy-done.27, ...), custom_call_target="tpu_custom_call" | custom-call | flops 301989888 | bytes 2928967 | tf_op jit(solution)/shard_map/merge_norm/pallas_call | solution.py:70
  236.6 20.0 %feed.3 = (bf16[384,1792]{1,0:T(8,128)(2,1)}, bf16[384,1792]{1,0:T(8,128)(2,1)}, f32[8,1792]{1,0:T(8,128)}, bf16[384,1600]{1,0:T(8,128)(2,1)}, bf16[384,1600]{1,0:T(8,128)(2,1)}) custom-call(s32[5]{0:T(128)} %pad_add_fusion.at_ref, bf16[192,1600]{1,0:T(8,128)(2,1)} %get-tuple-element.342.refs_0_, bf16[192,1600]{1,0:T(8,128)(2,1)} %get-tuple-element.343.refs_1_, ...), custom_call_target="tpu_custom_call" | custom-call | flops 1056964608 | bytes 2260992 | tf_op jit(solution)/shard_map/feed/pallas_call | solution.py:70
  265.7 34.1 %feed.4 = (bf16[768,1792]{1,0:T(8,128)(2,1)}, bf16[768,1792]{1,0:T(8,128)(2,1)}, f32[8,1792]{1,0:T(8,128)}, bf16[192,1600]{1,0:T(8,128)(2,1)}, bf16[192,1600]{1,...) custom-call(s32[5]{0:T(128)} %pad_add_fusion.at_ref, ...), custom_call_target="tpu_custom_call" | custom-call | flops 2113929216 | bytes 3145728 | tf_op jit(solution)/shard_map/feed/pallas_call | solution.py:70
  302.1 20.2 %feed.5 = (bf16[384,1792]{1,0:T(8,128)(2,1)}, bf16[384,1792]{1,0:T(8,128)(2,1)}, f32[8,1792]{1,0:T(8,128)}, bf16[192,1600]{1,0:T(8,128)(2,1)}, bf16[192,1600]{1,...) custom-call(s32[5]{0:T(128)} %pad_add_fusion.at_ref, ...), custom_call_target="tpu_custom_call" | custom-call | flops 1056964608 | bytes 2260992 | tf_op jit(solution)/shard_map/feed/pallas_call | solution.py:70
  325.1 18.8 %shrink_grad.1 = (bf16[1600,896]{1,0:T(8,128)(2,1)}, bf16[1600,896]{1,0:T(8,128)(2,1)}) custom-call(s32[5]{0:T(128)} %pad_add_fusion.at_ref, bf16[384,1600]{1,0:T(8,128)(2,1)} %copy-done.4, bf16[384,1600]{1,0:T(8,128)(2,1)} %bitcast.73, bf16[384,1600]{1,0:T(8,128)(2,1)} %bitcast.15.refs_5_.refs_2_, ...), custom_call_target="tpu_custom_call" | custom-call | flops 1056964608 | bytes 1867776 | tf_op jit(solution)/shard_map/shrink_grad/pallas_call | solution.py:70
  350.7 18.8 %expand_grad.1 = (bf16[896,1600]{1,0:T(8,128)(2,1)}, bf16[896,1600]{1,0:T(8,128)(2,1)}) custom-call(s32[5]{0:T(128)} %pad_add_fusion.at_ref, bf16[192,1600]{1,0:T(8,128)(2,1)} %get-tuple-element.342.refs_0_, bf16[192,1600]{1,0:T(8,128)(2,1)} %get-tuple-element.343.refs_1_, bf16[192,1600]{1,0:T(8,128)(2,1)} %copy-done.11, bf16[192,1600]{1,0:T(8,128)(2,1)} %copy-done.13, ...), custom_call_target="tpu_custom_call" | custom-call | flops 1056964608 | bytes 1867776 | tf_op jit(solution)/shard_map/expand_grad/pallas_call | solution.py:70
  376.0 12.4 %second_back.1 = (f32[384,1600]{1,0:T(8,128)}, bf16[384,1600]{1,0:T(8,128)(2,1)}, f32[8,1600]{1,0:T(8,128)}, bf16[384,512]{1,0:T(8,128)(2,1)}, bf16[384,512]{1,0...) custom-call(s32[5]{0:T(128)} %pad_add_fusion.at_ref, bf16[384,1600]{1,0:T(8,128)(2,1)} %get-tuple-element.353.refs_0_, ...), custom_call_target="tpu_custom_call" | custom-call | flops 301989888 | bytes 2555535 | tf_op jit(solution)/shard_map/second_back/pallas_call | solution.py:70
  392.5 12.1 %merge_grad.1 = (bf16[4,200,1600]{2,1,0:T(8,128)(2,1)}, bf16[4,200,1600]{2,1,0:T(8,128)(2,1)}) custom-call(s32[5]{0:T(128)} %pad_add_fusion.at_ref, bf16[384,256]{1,0:T(8,128)(2,1)} %get-tuple-element.328.refs_5_.refs_0_, bf16[384,256]{1,0:T(8,128)(2,1)} %copy-done.26, bf16[384,256]{1,0:T(8,128)(2,1)} %copy-done.27, bf16[384,256]{1,0:T(8,128)(2,1)} %copy-done.28, ...), custom_call_target="tpu_custom_call" | custom-call | flops 301989888 | bytes 1564999 | tf_op jit(solution)/shard_map/merge_grad/pallas_call | solution.py:70
  404.6 4.6 collective-permute-done.56.refs_6_
  414.5 4.9 add_parts.2
  422.9 28.4 %attend_backward.2.refs_10_.refs_0_ = bf16[3,1536,256]{2,1,0:T(8,128)(2,1)} custom-call(s32[5]{0:T(128)} %pad_add_fusion.at_ref, bf16[1536,1536]{1,0:T(8,128)(2,1)} %get-tuple-element.309.refs_0_.refs_1_.refs_2_.refs_11_, bf16[1536,1536]{1,0:T(8,128)(2,1)} %get-tuple-element.309.refs_0_.refs_1_.refs_2_.refs_11_, ...), custom_call_target="tpu_custom_call" | custom-call | flops 634178752 | bytes 754974 | tf_op jit(solution)/shard_map/attend_backward/pallas_call | solution.py:70
  453.8 22.6 %attend_backward.3.refs_1_ = bf16[3,1536,256]{2,1,0:T(8,128)(2,1)} custom-call(s32[5]{0:T(128)} %pad_add_fusion.at_ref, bf16[1536,1536]{1,0:T(8,128)(2,1)} %get-tuple-element.309.refs_0_.refs_1_.refs_2_.refs_11_, bf16[1536,1536]{1,0:T(8,128)(2,1)} %get-tuple-element.309.refs_0_.refs_1_.refs_2_.refs_11_, ...), custom_call_target="tpu_custom_call" | custom-call | flops 634178752 | bytes 754974 | tf_op jit(solution)/shard_map/attend_backward/pallas_call | solution.py:70
  483.8 13.2 %mix_grad.1 = (bf16[4,200,1536]{2,1,0:T(8,128)(2,1)}, bf16[4,200,1536]{2,1,0:T(8,128)(2,1)}, f32[8,1536]{1,0:T(8,128)}) custom-call(s32[5]{0:T(128)} %pad_add_fusion.at_ref, bf16[3,1536,256]{2,1,0:T(8,128)(2,1)} %attend_backward.2.refs_10_.refs_0_, bf16[3,1536,256]{2,1,0:T(8,128)(2,1)} %attend_backward.3.refs_1_, ...), custom_call_target="tpu_custom_call" | custom-call | flops 905969664 | bytes 1769472 | tf_op jit(solution)/shard_map/mix_grad/pallas_call | solution.py:70
  503.0 5.0 block_out.1
  518.6 5.1 add_parts.3
  525.6 8.2 %first_back.3 = (f32[8,1600]{1,0:T(8,128)}, bf16[192,1600]{1,0:T(8,128)(2,1)}, bf16[192,1600]{1,0:T(8,128)(2,1)}) custom-call(s32[5]{0:T(128)} %pad_add_fusion.at_ref, bf16[3,1536,256]{2,1,0:T(8,128)(2,1)} %attend_backward.2.refs_10_.refs_0_, bf16[3,1536,256]{2,1,0:T(8,128)(2,1)} %attend_backward.3.refs_1_, bf16[192,1600]{1,0:T(8,128)(2,1)} %copy-done.17, ...), custom_call_target="tpu_custom_call" | custom-call | flops 226492416 | bytes 589824 | tf_op jit(solution)/shard_map/first_back/pallas_call | solution.py:70
  537.3 13.0 %first_back.4 = (f32[8,1600]{1,0:T(8,128)}, bf16[192,1600]{1,0:T(8,128)(2,1)}, bf16[192,1600]{1,0:T(8,128)(2,1)}, bf16[192,1600]{1,0:T(8,128)(2,1)}, bf16[192,1600]{1,0:T(8,128)(2,1)}) custom-call(s32[5]{0:T(128)} %pad_add_fusion.at_ref, bf16[3,1536,256]{2,1,0:T(8,128)(2,1)} %attend_backward.2.refs_10_.refs_0_, ...), custom_call_target="tpu_custom_call" | custom-call | flops 452984832 | bytes 1179648 | tf_op jit(solution)/shard_map/first_back/pallas_call | solution.py:70
  550.4 8.4 %first_back.5 = (f32[8,1600]{1,0:T(8,128)}, bf16[384,1600]{1,0:T(8,128)(2,1)}) custom-call(s32[5]{0:T(128)} %pad_add_fusion.at_ref, bf16[3,1536,256]{2,1,0:T(8,128)(2,1)} %attend_backward.2.refs_10_.refs_0_, bf16[3,1536,256]{2,1,0:T(8,128)(2,1)} %attend_backward.3.refs_1_, bf16[384,1600]{1,0:T(8,128)(2,1)} %copy-done.2, ...), custom_call_target="tpu_custom_call" | custom-call | flops 226492416 | bytes 589824 | tf_op jit(solution)/shard_map/first_back/pallas_call | solution.py:70
  594.8 5.2 collective-permute-done.81
  607.8 4.8 collective-permute-done.84.refs_2_
  614.1 7.4 %input_grad.1 = (f32[192,1600]{1,0:T(8,128)}, f32[192,1600]{1,0:T(8,128)}) custom-call(s32[5]{0:T(128)} %pad_add_fusion.at_ref, bf16[384,1600]{1,0:T(8,128)(2,1)} %get-tuple-element.485.refs_0_, bf16[192,1600]{1,0:T(8,128)(2,1)} %copy-done.40, bf16[192,1600]{1,0:T(8,128)(2,1)} %copy-done.42, bf16[192,1600]{1,0:T(8,128)(2,1)} %copy-done.43, ...), custom_call_target="tpu_custom_call" | custom-call | bytes 1185792 | tf_op jit(solution)/shard_map/input_grad/pallas_call | solution.py:70
  (438 shorter events, 220.2 us)
Async XLA Ops:
  7.2 63.4 %all-gather.7.cloned.1.call-start = ((), (), s32[]{:S(2)}) async-start(), calls=%async_computation.8 | async-start | bytes 3328000 | tf_op jit(solution)/shard_map/all_gather | solution.py:720
  9.5 169.1 %all-gather.9.cloned.1.call-start = ((), (), s32[]{:S(2)}) async-start(), calls=%async_computation.9 | async-start | bytes 3727360 | tf_op jit(solution)/shard_map/all_gather | solution.py:720
  23.3 47.3 %collective-permute-start.9 = (bf16[2,192,1600]{2,1,0:T(8,128)(2,1)S(1)}, bf16[2,192,1600]{2,1,0:T(8,128)(2,1)S(1)}, u32[]{:S(2)}, u32[]{:S(2)}) collective-permute-start(bf16[2,192,1600]{2,1,0:T(8,128)(2,1)S(1)} %bitcast.61), channel_id=1, source_target_pairs={{0,2},{1,3},{2,0},{3,1},{4,6},{5,7},{6,4},{7,5},{8,10},{9,11},{10,... | collective-permute-start | bytes 3686408 | tf_op jit(solution)/shard_map/ppermute | solution.py:714
  25.4 45.2 %collective-permute-start.10 = (bf16[2,192,1600]{2,1,0:T(8,128)(2,1)S(1)}, bf16[2,192,1600]{2,1,0:T(8,128)(2,1)}, u32[]{:S(2)}, u32[]{:S(2)}) collective-permute-start(bf16[2,192,1600]{2,1,0:T(8,128)(2,1)S(1)} %bitcast.62), channel_id=1, source_target_pairs={{0,4},{1,5},{2,6},{3,7},{4,0},{5,1},{6,2},{7,3},{8,12},{9,13},{10,... | collective-permute-start | bytes 3686408 | tf_op jit(solution)/shard_map/ppermute | solution.py:714
  41.5 29.1 %collective-permute-start.3 = (bf16[2,200,400]{2,1,0:T(8,128)(2,1)}, bf16[2,200,400]{2,1,0:T(8,128)(2,1)}, u32[]{:S(2)}, u32[]{:S(2)}) collective-permute-start(bf16[2,200,400]{2,1,0:T(8,128)(2,1)} %get-tuple-element.278), channel_id=1, source_target_pairs={{0,4},{1,5},{2,6},{3,7},{4,0},{5,1},{6,2},{7,3},{8,12},{9,13},{10,... | collective-permute-start | bytes 960008 | tf_op jit(solution)/shard_map/ppermute | solution.py:714
  41.6 29.0 %collective-permute-start.4 = (bf16[2,200,400]{2,1,0:T(8,128)(2,1)}, bf16[2,200,400]{2,1,0:T(8,128)(2,1)}, u32[]{:S(2)}, u32[]{:S(2)}) collective-permute-start(bf16[2,200,400]{2,1,0:T(8,128)(2,1)} %get-tuple-element.279), channel_id=1, source_target_pairs={{0,6},{1,7},{2,4},{3,5},{4,2},{5,3},{6,0},{7,1},{8,14},{9,15},{10,... | collective-permute-start | bytes 960008 | tf_op jit(solution)/shard_map/ppermute | solution.py:714
  80.1 125.9 %all-gather.11.cloned.1.call-start = ((), (), s32[]{:S(2)}) async-start(), calls=%async_computation.10 | async-start | bytes 3584000 | tf_op jit(solution)/shard_map/all_gather | solution.py:720
  98.0 27.4 %collective-permute-start.15 = (bf16[200,1536]{1,0:T(8,128)(2,1)}, bf16[200,1536]{1,0:T(8,128)(2,1)}, u32[]{:S(2)}, u32[]{:S(2)}) collective-permute-start(bf16[200,1536]{1,0:T(8,128)(2,1)} %get-tuple-element.299), channel_id=1, source_target_pairs={{0,4},{1,5},{2,6},{3,7},{4,0},{5,1},{6,2},{7,3},{8,12},{9,13},{10,... | collective-permute-start | bytes 1843208 | tf_op jit(solution)/shard_map/ppermute | solution.py:714
  100.1 27.5 %collective-permute-start.25 = (bf16[192,1600]{1,0:T(8,128)(2,1)}, bf16[192,1600]{1,0:T(8,128)(2,1)}, u32[]{:S(2)}, u32[]{:S(2)}) collective-permute-start(bf16[192,1600]{1,0:T(8,128)(2,1)} %get-tuple-element.568), channel_id=1, source_target_pairs={{0,1},{1,0},{2,3},{3,2},{4,5},{5,4},{6,7},{7,6},{8,9},{9,8},{10,11... | collective-permute-start | bytes 1843208 | tf_op jit(solution)/shard_map/ppermute | solution.py:714
  100.1 28.0 %collective-permute-start.13 = (bf16[200,1536]{1,0:T(8,128)(2,1)S(1)}, bf16[200,1536]{1,0:T(8,128)(2,1)}, u32[]{:S(2)}, u32[]{:S(2)}) collective-permute-start(bf16[200,1536]{1,0:T(8,128)(2,1)S(1)} %copy-done.8), channel_id=1, source_target_pairs={{0,1},{1,0},{2,3},{3,2},{4,5},{5,4},{6,7},{7,6},{8,9},{9,8},{10,11... | collective-permute-start | bytes 1843208 | tf_op jit(solution)/shard_map/ppermute | solution.py:714
  128.8 379.2 %reduce-scatter.7.cloned.1.call-start = ((), (), s32[]{:S(2)}) async-start(), calls=%async_computation.5 | async-start | bytes 3584000 | tf_op jit(solution)/shard_map/reduce_scatter | solution.py:723
  148.0 30.2 %collective-permute-start.26 = (bf16[2,192,1600]{2,1,0:T(8,128)(2,1)S(1)}, bf16[2,192,1600]{2,1,0:T(8,128)(2,1)S(1)}, u32[]{:S(2)}, u32[]{:S(2)}) collective-permute-start(bf16[2,192,1600]{2,1,0:T(8,128)(2,1)S(1)} %bitcast.69), channel_id=1, source_target_pairs={{0,2},{1,3},{2,0},{3,1},{4,6},{5,7},{6,4},{7,5},{8,10},{9,11},{10,... | collective-permute-start | bytes 3686408 | tf_op jit(solution)/shard_map/ppermute | solution.py:714
  148.7 29.9 %collective-permute-start.27 = (bf16[2,192,1600]{2,1,0:T(8,128)(2,1)S(1)}, bf16[2,192,1600]{2,1,0:T(8,128)(2,1)}, u32[]{:S(2)}, u32[]{:S(2)}) collective-permute-start(bf16[2,192,1600]{2,1,0:T(8,128)(2,1)S(1)} %bitcast.70), channel_id=1, source_target_pairs={{0,4},{1,5},{2,6},{3,7},{4,0},{5,1},{6,2},{7,3},{8,12},{9,13},{10,... | collective-permute-start | bytes 3686408 | tf_op jit(solution)/shard_map/ppermute | solution.py:714
  206.0 30.6 %collective-permute-start.37 = (bf16[1600,896]{1,0:T(8,128)(2,1)}, bf16[1600,896]{1,0:T(8,128)(2,1)}, u32[]{:S(2)}, u32[]{:S(2)}) collective-permute-start(bf16[1600,896]{1,0:T(8,128)(2,1)} %all-gather.11.cloned.1.call-done.refs_4_.refs_7_.refs_5_), channel_id=1, source_target_pairs={{0,1},{1,0},{2,3},{3,2},{4,5},{5,4},{6,7},{7,6},{8,9},{9,8},{10,11... | collective-permute-start | bytes 8601608 | tf_op jit(solution)/shard_map/ppermute | solution.py:714
  233.0 27.7 %collective-permute-start.40 = (bf16[192,1600]{1,0:T(8,128)(2,1)}, bf16[192,1600]{1,0:T(8,128)(2,1)S(1)}, u32[]{:S(2)}, u32[]{:S(2)}) collective-permute-start(bf16[192,1600]{1,0:T(8,128)(2,1)} %get-tuple-element.342.refs_0_), channel_id=1, source_target_pairs={{0,4},{1,5},{2,6},{3,7},{4,0},{5,1},{6,2},{7,3},{8,12},{9,13},{10,... | collective-permute-start | bytes 1843208 | tf_op jit(solution)/shard_map/ppermute | solution.py:714
  261.6 38.2 %collective-permute-start.45 = (bf16[192,1600]{1,0:T(8,128)(2,1)}, bf16[192,1600]{1,0:T(8,128)(2,1)}, u32[]{:S(2)}, u32[]{:S(2)}) collective-permute-start(bf16[192,1600]{1,0:T(8,128)(2,1)} %slice.143.refs_19_), channel_id=1, source_target_pairs={{0,2},{1,3},{2,0},{3,1},{4,6},{5,7},{6,4},{7,5},{8,10},{9,11},{10,... | collective-permute-start | bytes 1843208 | tf_op jit(solution)/shard_map/ppermute | solution.py:714
  262.4 37.4 %collective-permute-start.44 = (bf16[192,1600]{1,0:T(8,128)(2,1)S(1)}, bf16[192,1600]{1,0:T(8,128)(2,1)}, u32[]{:S(2)}, u32[]{:S(2)}) collective-permute-start(bf16[192,1600]{1,0:T(8,128)(2,1)S(1)} %copy-done.15), channel_id=1, source_target_pairs={{0,4},{1,5},{2,6},{3,7},{4,0},{5,1},{6,2},{7,3},{8,12},{9,13},{10,... | collective-permute-start | bytes 1843208 | tf_op jit(solution)/shard_map/ppermute | solution.py:714
  263.8 36.0 %collective-permute-start.42 = (bf16[192,1600]{1,0:T(8,128)(2,1)S(1)}, bf16[192,1600]{1,0:T(8,128)(2,1)}, u32[]{:S(2)}, u32[]{:S(2)}) collective-permute-start(bf16[192,1600]{1,0:T(8,128)(2,1)S(1)} %collective-permute-done.38.refs_0_.refs_2_), channel_id=1, source_target_pairs={{0,4},{1,5},{2,6},{3,7},{4,0},{5,1},{6,2},{7,3},{8,12},{9,13},{10,... | collective-permute-start | bytes 1843208 | tf_op jit(solution)/shard_map/ppermute | solution.py:714
  264.5 35.4 %collective-permute-start.43 = (bf16[192,1600]{1,0:T(8,128)(2,1)S(1)}, bf16[192,1600]{1,0:T(8,128)(2,1)}, u32[]{:S(2)}, u32[]{:S(2)}) collective-permute-start(bf16[192,1600]{1,0:T(8,128)(2,1)S(1)} %collective-permute-done.41.refs_3_.refs_5_), channel_id=1, source_target_pairs={{0,2},{1,3},{2,0},{3,1},{4,6},{5,7},{6,4},{7,5},{8,10},{9,11},{10,... | collective-permute-start | bytes 1843208 | tf_op jit(solution)/shard_map/ppermute | solution.py:714
  373.9 134.1 %reduce-scatter.5.cloned.1.call-start = ((), (), s32[]{:S(2)}) async-start(), calls=%async_computation.4 | async-start | bytes 3727360 | tf_op jit(solution)/shard_map/reduce_scatter | solution.py:723
  374.0 35.2 %collective-permute-start.53 = (bf16[2,448,1600]{2,1,0:T(8,128)(2,1)}, bf16[2,448,1600]{2,1,0:T(8,128)(2,1)}, u32[]{:S(2)}, u32[]{:S(2)}) collective-permute-start(bf16[2,448,1600]{2,1,0:T(8,128)(2,1)} %bitcast.91), channel_id=1, source_target_pairs={{0,1},{1,0},{2,3},{3,2},{4,5},{5,4},{6,7},{7,6},{8,9},{9,8},{10,11... | collective-permute-start | bytes 8601608 | tf_op jit(solution)/shard_map/ppermute | solution.py:714
  374.9 29.7 %collective-permute-start.57 = (bf16[192,1600]{1,0:T(8,128)(2,1)}, bf16[192,1600]{1,0:T(8,128)(2,1)}, u32[]{:S(2)}, u32[]{:S(2)}) collective-permute-start(bf16[192,1600]{1,0:T(8,128)(2,1)} %get-tuple-element.420), channel_id=1, source_target_pairs={{0,2},{1,3},{2,0},{3,1},{4,6},{5,7},{6,4},{7,5},{8,10},{9,11},{10,... | collective-permute-start | bytes 1843208 | tf_op jit(solution)/shard_map/ppermute | solution.py:714
  413.6 208.4 %reduce-scatter.11.cloned.1.call-start = ((), (), s32[]{:S(2)}) async-start(), calls=%async_computation.7 | async-start | bytes 1024000 | tf_op jit(solution)/shard_map/reduce_scatter | solution.py:723
  419.4 31.9 %collective-permute-start.62 = (bf16[200,1600]{1,0:T(8,128)(2,1)}, bf16[200,1600]{1,0:T(8,128)(2,1)S(1)}, u32[]{:S(2)}, u32[]{:S(2)}) collective-permute-start(bf16[200,1600]{1,0:T(8,128)(2,1)} %get-tuple-element.439), channel_id=1, source_target_pairs={{0,6},{1,7},{2,4},{3,5},{4,2},{5,3},{6,0},{7,1},{8,14},{9,15},{10,... | collective-permute-start | bytes 1920008 | tf_op jit(solution)/shard_map/ppermute | solution.py:714
  420.8 31.0 %collective-permute-start.61 = (bf16[200,1600]{1,0:T(8,128)(2,1)}, bf16[200,1600]{1,0:T(8,128)(2,1)S(1)}, u32[]{:S(2)}, u32[]{:S(2)}) collective-permute-start(bf16[200,1600]{1,0:T(8,128)(2,1)} %get-tuple-element.437), channel_id=1, source_target_pairs={{0,4},{1,5},{2,6},{3,7},{4,0},{5,1},{6,2},{7,3},{8,12},{9,13},{10,... | collective-permute-start | bytes 1920008 | tf_op jit(solution)/shard_map/ppermute | solution.py:714
  421.7 30.1 %collective-permute-start.60 = (bf16[200,1600]{1,0:T(8,128)(2,1)}, bf16[200,1600]{1,0:T(8,128)(2,1)S(1)}, u32[]{:S(2)}, u32[]{:S(2)}) collective-permute-start(bf16[200,1600]{1,0:T(8,128)(2,1)} %get-tuple-element.435), channel_id=1, source_target_pairs={{0,2},{1,3},{2,0},{3,1},{4,6},{5,7},{6,4},{7,5},{8,10},{9,11},{10,... | collective-permute-start | bytes 1920008 | tf_op jit(solution)/shard_map/ppermute | solution.py:714
  517.1 118.6 %reduce-scatter.9.cloned.1.call-start = ((), (), s32[]{:S(2)}) async-start(), calls=%async_computation.6 | async-start | bytes 2560000 | tf_op jit(solution)/shard_map/reduce_scatter | solution.py:723
  523.7 40.0 %collective-permute-start.74 = (bf16[200,1536]{1,0:T(8,128)(2,1)}, bf16[200,1536]{1,0:T(8,128)(2,1)S(1)}, u32[]{:S(2)}, u32[]{:S(2)}) collective-permute-start(bf16[200,1536]{1,0:T(8,128)(2,1)} %get-tuple-element.502), channel_id=1, source_target_pairs={{0,2},{1,3},{2,0},{3,1},{4,6},{5,7},{6,4},{7,5},{8,10},{9,11},{10,... | collective-permute-start | bytes 1843208 | tf_op jit(solution)/shard_map/ppermute | solution.py:714
  524.8 38.9 %collective-permute-start.75 = (bf16[200,1536]{1,0:T(8,128)(2,1)}, bf16[200,1536]{1,0:T(8,128)(2,1)S(1)}, u32[]{:S(2)}, u32[]{:S(2)}) collective-permute-start(bf16[200,1536]{1,0:T(8,128)(2,1)} %get-tuple-element.503), channel_id=1, source_target_pairs={{0,4},{1,5},{2,6},{3,7},{4,0},{5,1},{6,2},{7,3},{8,12},{9,13},{10,... | collective-permute-start | bytes 1843208 | tf_op jit(solution)/shard_map/ppermute | solution.py:714
  533.8 29.8 %collective-permute-start.76 = (bf16[200,1536]{1,0:T(8,128)(2,1)}, bf16[200,1536]{1,0:T(8,128)(2,1)S(1)}, u32[]{:S(2)}, u32[]{:S(2)}) collective-permute-start(bf16[200,1536]{1,0:T(8,128)(2,1)} %get-tuple-element.504), channel_id=1, source_target_pairs={{0,6},{1,7},{2,4},{3,5},{4,2},{5,3},{6,0},{7,1},{8,14},{9,15},{10,... | collective-permute-start | bytes 1843208 | tf_op jit(solution)/shard_map/ppermute | solution.py:714
  535.4 38.2 %collective-permute-start.72 = (bf16[192,1600]{1,0:T(8,128)(2,1)}, bf16[192,1600]{1,0:T(8,128)(2,1)S(1)}, u32[]{:S(2)}, u32[]{:S(2)}) collective-permute-start(bf16[192,1600]{1,0:T(8,128)(2,1)} %get-tuple-element.483), channel_id=1, source_target_pairs={{0,2},{1,3},{2,0},{3,1},{4,6},{5,7},{6,4},{7,5},{8,10},{9,11},{10,... | collective-permute-start | bytes 1843208 | tf_op jit(solution)/shard_map/ppermute | solution.py:714
  536.5 37.8 %collective-permute-start.73 = (bf16[192,1600]{1,0:T(8,128)(2,1)}, bf16[192,1600]{1,0:T(8,128)(2,1)S(1)}, u32[]{:S(2)}, u32[]{:S(2)}) collective-permute-start(bf16[192,1600]{1,0:T(8,128)(2,1)} %get-tuple-element.484), channel_id=1, source_target_pairs={{0,4},{1,5},{2,6},{3,7},{4,0},{5,1},{6,2},{7,3},{8,12},{9,13},{10,... | collective-permute-start | bytes 1843208 | tf_op jit(solution)/shard_map/ppermute | solution.py:714
  (137 other events, 1769.7 us)
Sparse Core Ops, SparseCore 0:
  10.2 58.1 all-gather.6
  80.2 61.1 all-gather.8
  143.5 57.5 all-gather.10
  374.1 55.8 reduce-scatter.6
  432.1 57.5 reduce-scatter.4
  517.2 23.3 reduce-scatter.10
  579.8 43.3 reduce-scatter.8
